TPU v7x, 32 devices: a whole 2x2x4 slice. The times are simulated.
32 devices in a mesh: dp: 8 (over z, y), tensor: 4 (over x, core).
Axes of the slice: x: 2, y: 2, z: 4, core: 2. Of those that a mesh axis runs over, the one named last changes fastest.
Arguments:
- queries: bfloat16 [3072, 1536], P('dp', 'tensor'), may hold values from -6 to 6
- key_rows: bfloat16 [3072, 1536], P('dp', 'tensor'), may hold values from -6 to 6
- value_rows: bfloat16 [3072, 1536], P('dp', 'tensor'), may hold values from -6 to 6
- out_weight: bfloat16 [1536, 6144], P('tensor'), may hold values from -0.15625 to 0.15625
- segment_ids: int32 [8, 384], P('dp'), may hold values from 0 to 5, as said below
- move_flags: int32 [8, 384], P('dp'), may hold values from 0 to 1, as said below
- out_cotangent: bfloat16 [3584, 6144], P('dp', 'tensor'), may hold values from -6 to 6
Outputs:
- projected: bfloat16 [3584, 6144], P('dp', 'tensor')
- grad_queries: bfloat16 [3072, 1536], P('dp', 'tensor')
- grad_keys: bfloat16 [3072, 1536], P('dp', 'tensor')
- grad_values: bfloat16 [3072, 1536], P('dp', 'tensor')
Inputs may be any that keep to these rules, and one draw needn't show every extreme that they name: `segment_ids`: in each data group the image numbers start at 0 and rise by 0 or 1 from row to row; a new image can begin only at a row that is a multiple of 64, and one always begins at row 320; in every draw some group reaches the largest number. `move_flags`: the images that one data group hands on hold at most 64 rows together; in every draw some group hands on exactly 64 rows and the group after it keeps all of its images.
All inputs are finite; a program needn't handle non-finite values.
Results may differ from a plain program's by a relative error of at most 0.015.
Values may be sent and summed in bfloat16 or wider, within the bound.
No kernel may reach another device: no remote copies, remote signals or barrier semaphores. Data moves between devices by JAX's collectives and lax.ppermute only.
A program may use at most 64 MiB of HBM per device.

v0:
```python
import jax
import jax.numpy as jnp
from jax import lax
from jax.sharding import PartitionSpec as P

HEAD = 128


def shifted(shard, axis, by):
    size = lax.axis_size(axis)
    return lax.ppermute(shard, axis, [(i, (i + by) % size) for i in range(size)])


def attend(query_wide, key_wide, value_wide, image_of):
    rows = query_wide.shape[0]
    heads = query_wide.shape[1] // HEAD
    qh = query_wide.reshape(rows, heads, HEAD)
    kh = key_wide.reshape(rows, heads, HEAD)
    vh = value_wide.reshape(rows, heads, HEAD)
    scores = jnp.einsum("qhd,khd->hqk", qh, kh) * HEAD ** (-0.5)
    same = image_of[:, None] == image_of[None, :]
    scores = jnp.where(same[None, :, :], scores, -1e30)
    peak = jnp.max(scores, axis=2, keepdims=True)
    weights = jnp.exp(scores - peak)
    weights = weights / jnp.sum(weights, axis=2, keepdims=True)
    return jnp.einsum("hqk,khd->qhd", weights, vh).reshape(rows, heads * HEAD)


def select_rows(mask, values):
    return jnp.dot(mask.astype(values.dtype), values, preferred_element_type=jnp.float32)


def project_rows(attended, out_weight):
    term = jnp.dot(attended, out_weight, preferred_element_type=jnp.float32)
    return lax.psum_scatter(term.astype(jnp.bfloat16), "tensor", scatter_dimension=1, tiled=True)


def back_project(cot_rows, out_weight):
    return lax.dot_general(
        lax.all_gather(cot_rows, "tensor", axis=1, tiled=True),
        out_weight,
        (((1,), (1,)), ((), ())),
        preferred_element_type=jnp.float32,
    ).astype(jnp.bfloat16)


def attention_grads(query_wide, key_wide, value_wide, image_of, attended_cot):
    _, pull = jax.vjp(lambda a, b, c: attend(a, b, c, image_of), query_wide, key_wide, value_wide)
    grads = pull(attended_cot.astype(jnp.float32))
    return tuple((g.astype(jnp.bfloat16) for g in grads))


def shards(queries, key_rows, value_rows, out_weight, segment_ids, move_flags, out_cotangent):
    image_of = segment_ids[0]
    flag_list = move_flags[0]
    home_rows = image_of.shape[0]
    dest_rows = out_cotangent.shape[0]
    send_rows = dest_rows - home_rows
    image_index = jnp.arange(home_rows, dtype=jnp.int32)
    row_move = jnp.sum(
        jnp.where(image_of[:, None] == image_index[None, :], flag_list[None, :], 0), axis=1
    )
    kept = 1 - row_move
    kept_slot = jnp.cumsum(kept) - 1
    move_slot = jnp.cumsum(row_move) - 1
    kept_count = jnp.sum(kept)
    dest_index = jnp.arange(dest_rows, dtype=jnp.int32)
    send_index = jnp.arange(send_rows, dtype=jnp.int32)
    put_kept = (dest_index[:, None] == kept_slot[None, :]) & (kept[None, :] == 1)
    take_moved = (send_index[:, None] == move_slot[None, :]) & (row_move[None, :] == 1)
    put_recv = dest_index[:, None] == kept_count + send_index[None, :]
    out_q = select_rows(take_moved, queries).astype(jnp.bfloat16)
    out_k = select_rows(take_moved, key_rows).astype(jnp.bfloat16)
    out_v = select_rows(take_moved, value_rows).astype(jnp.bfloat16)
    out_image = jnp.max(jnp.where(take_moved, image_of[None, :], -1), axis=1)
    in_q, in_k, in_v, in_image = shifted((out_q, out_k, out_v, out_image), "dp", 1)
    in_image = jnp.where(in_image >= 0, in_image + home_rows, -1)
    dest_q = select_rows(put_kept, queries) + select_rows(put_recv, in_q)
    dest_k = select_rows(put_kept, key_rows) + select_rows(put_recv, in_k)
    dest_v = select_rows(put_kept, value_rows) + select_rows(put_recv, in_v)
    kept_image = jnp.max(jnp.where(put_kept, image_of[None, :], -1), axis=1)
    recv_image = jnp.max(jnp.where(put_recv, in_image[None, :], -1), axis=1)
    dest_image = jnp.maximum(kept_image, recv_image).astype(jnp.int32)
    attended = attend(dest_q, dest_k, dest_v, dest_image).astype(jnp.bfloat16)
    projected = project_rows(attended, out_weight)
    attended_cot = back_project(out_cotangent, out_weight)
    dest_gq, dest_gk, dest_gv = attention_grads(dest_q, dest_k, dest_v, dest_image, attended_cot)
    back_q = select_rows(put_recv.T, dest_gq).astype(jnp.bfloat16)
    back_k = select_rows(put_recv.T, dest_gk).astype(jnp.bfloat16)
    back_v = select_rows(put_recv.T, dest_gv).astype(jnp.bfloat16)
    ret_q, ret_k, ret_v = shifted((back_q, back_k, back_v), "dp", -1)
    grad_q = (select_rows(put_kept.T, dest_gq) + select_rows(take_moved.T, ret_q)).astype(
        jnp.bfloat16
    )
    grad_k = (select_rows(put_kept.T, dest_gk) + select_rows(take_moved.T, ret_k)).astype(
        jnp.bfloat16
    )
    grad_v = (select_rows(put_kept.T, dest_gv) + select_rows(take_moved.T, ret_v)).astype(
        jnp.bfloat16
    )
    return (projected, grad_q, grad_k, grad_v)


def solution(mesh):
    in_specs = (
        P("dp", "tensor"),
        P("dp", "tensor"),
        P("dp", "tensor"),
        P("tensor", None),
        P("dp", None),
        P("dp", None),
        P("dp", "tensor"),
    )
    out_specs = (P("dp", "tensor"), P("dp", "tensor"), P("dp", "tensor"), P("dp", "tensor"))
    return jax.shard_map(shards, mesh=mesh, in_specs=in_specs, out_specs=out_specs, check_vma=False)
```

profile of v0, /device:TPU:0, one launch (start us, length us, event | category | flops | bytes accessed | tf_op | source)
XLA Modules:
  0.0 117.4 jit_solution(2703833246554805052)
XLA Ops:
  7.2 0.7 all-gather.2.cloned.1.call-update
  8.0 0.7 reduce
  8.7 0.7 reduce.1
  9.4 0.2 select_reduce_fusion.1
  9.6 0.3 reduce-window.24
  10.0 0.1 slice_reduce_fusion
  10.2 0.1 select_reduce_fusion.3
  10.4 3.0 %collective-permute-start.1 = (s32[64]{0:T(128)S(1)}, s32[64]{0:T(128)S(1)}, u32[]{:S(2)}, u32[]{:S(2)}) collective-permute-start(s32[64]{0:T(128)S(1)} %select_reduce_fusion.3), channel_id=1, source_target_pairs={{0,4},{4,8},{8,12},{12,16},{16,20},{20,24},{24,28},{28,0},{1,5},{5... | collective-permute-start | bytes 776 | tf_op jit(solution)/shard_map/ppermute | solution.py:11
  13.4 1.1 convolution_convert_fusion.6
  14.5 1.6 %collective-permute-start = (bf16[64,384]{1,0:T(8,128)(2,1)S(1)}, bf16[64,384]{1,0:T(8,128)(2,1)S(1)}, u32[]{:S(2)}, u32[]{:S(2)}) collective-permute-start(bf16[64,384]{1,0:T(8,128)(2,1)S(1)} %convolution_convert_fusion.6), channel_id=1, source_target_pairs={{0,4},{4,8},{8,12},{12,16},{16,20},{20,24},{24,28},{28,0},{1,5},{5... | collective-permute-start | bytes 147464 | tf_op jit(solution)/shard_map/ppermute | solution.py:11
  16.1 1.1 convolution_convert_fusion.5
  17.2 1.6 %collective-permute-start.2 = (bf16[64,384]{1,0:T(8,128)(2,1)S(1)}, bf16[64,384]{1,0:T(8,128)(2,1)S(1)}, u32[]{:S(2)}, u32[]{:S(2)}) collective-permute-start(bf16[64,384]{1,0:T(8,128)(2,1)S(1)} %convolution_convert_fusion.5), channel_id=1, source_target_pairs={{0,4},{4,8},{8,12},{12,16},{16,20},{20,24},{24,28},{28,0},{1,5},{5... | collective-permute-start | bytes 147464 | tf_op jit(solution)/shard_map/ppermute | solution.py:11
  18.8 0.2 convolution_convert_fusion.4
  19.0 1.6 %collective-permute-start.3 = (bf16[64,384]{1,0:T(8,128)(2,1)S(1)}, bf16[64,384]{1,0:T(8,128)(2,1)S(1)}, u32[]{:S(2)}, u32[]{:S(2)}) collective-permute-start(bf16[64,384]{1,0:T(8,128)(2,1)S(1)} %convolution_convert_fusion.4), channel_id=1, source_target_pairs={{0,4},{4,8},{8,12},{12,16},{16,20},{20,24},{24,28},{28,0},{1,5},{5... | collective-permute-start | bytes 147464 | tf_op jit(solution)/shard_map/ppermute | solution.py:11
  20.6 0.3 reduce-window.16
  20.9 0.1 slice.14
  21.0 0.6 subtract_reduce_fusion
  21.6 0.1 slice_reduce_fusion.1
  21.7 0.1 add_bitcast_fusion.1
  21.8 0.2 select_reduce_fusion
  22.1 0.4 fusion.23
  22.4 0.3 fusion.25
  22.8 0.3 fusion.27
  23.2 0.7 iota_add_fusion
  23.8 0.1 select_reduce_fusion.2
  23.9 0.2 broadcast_compare_fusion
  24.1 1.7 %collective-permute-done.3 = bf16[64,384]{1,0:T(8,128)(2,1)S(1)} collective-permute-done((bf16[64,384]{1,0:T(8,128)(2,1)S(1)}, bf16[64,384]{1,0:T(8,128)(2,1)S(1)}, u32[]{:S(2)}, u32[]{:S(2)}) %collective-permute-start.3) | collective-permute-done | bytes 49184 | tf_op jit(solution)/shard_map/ppermute | solution.py:11
  25.8 0.4 convolution_add_fusion
  26.2 0.4 convolution_add_fusion.1
  26.6 0.9 copy.40
  27.5 0.9 copy.39
  28.5 0.4 convolution_add_fusion.2
  28.8 0.9 copy.38
  29.8 1.9 %fusion.1 = (f32[3,448]{1,0:T(4,128)S(1)}, f32[3,448,448]{1,2,0:T(8,128)S(1)}) fusion(pred[448,448]{0,1:T(8,128)(4,1)S(1)} %broadcast_compare_fusion, bf16[448,3,128]{0,2,1:T(8,128)(2,1)} %bitcast.55, bf16[448,3,128]{0,2,1:T(8,128)(2,1)} %bitcast.57), kind=kOutput, calls=%fused_computation.8 | convolution fusion | flops 155945664 | bytes 3302656 | tf_op jit(solution)/shard_map/qhd,khd->hqk/dot_general | solution.py:20
  31.7 0.6 fusion.76
  32.4 1.8 %fusion.20 = bf16[448,3,128]{2,0,1:T(8,128)(2,1)} fusion(bf16[448,3,128]{0,2,1:T(8,128)(2,1)S(1)} %bitcast.66, f32[3,448]{1,0:T(4,128)S(1)} %fusion.76, f32[3,448,448]{1,2,0:T(8,128)S(1)} %get-tuple-element.12, f32[3,448]{1,0:T(4,128)S(1)} %get-tuple-element.11, pred[448,448]{0,1:T(8,128)(4,1)S(1)} %broadcast_compare_fusion), kind=kOutput, calls=%fused_computation.37 | convolution fusion | flops 156549120 | bytes 3308032 | tf_op jit(solution)/shard_map/hqk,khd->qhd/dot_general | solution.py:26
  34.1 1.9 %copy.45 = bf16[448,3,128]{0,2,1:T(8,128)(2,1)} copy(bf16[448,3,128]{2,0,1:T(8,128)(2,1)} %fusion.20) | data formatting | bytes 688128 | tf_op jit(solution)/shard_map/convert_element_type | solution.py:84
  36.0 7.9 %convolution_convert_fusion = bf16[448,6144]{1,0:T(8,128)(2,1)} fusion(bf16[448,384]{0,1:T(8,128)(2,1)} %bitcast.54, bf16[384,6144]{1,0:T(8,128)(2,1)} %param.10), kind=kOutput, calls=%fused_computation | convolution fusion | flops 2116681728 | bytes 10567680 | tf_op jit(solution)/shard_map/dot_general | solution.py:34
  44.0 10.3 %all-gather.2.cloned.1.call-done = bf16[448,6144]{1,0:T(8,128)(2,1)} async-done(((bf16[448,1536]{1,0:T(8,128)(2,1)}), bf16[448,6144]{1,0:T(8,128)(2,1)}) %all-gather.2.cloned.1.call-update) | async-done | bytes 5505040 | tf_op jit(solution)/shard_map/all_gather | solution.py:40
  54.3 7.7 %convolution_convert_fusion.1 = bf16[448,384]{1,0:T(8,128)(2,1)} fusion(bf16[448,6144]{1,0:T(8,128)(2,1)} %all-gather.2.cloned.1.call-done, bf16[384,6144]{1,0:T(8,128)(2,1)} %param.10), kind=kOutput, calls=%fused_computation.26 | convolution fusion | flops 2114101248 | bytes 10567680 | tf_op jit(solution)/shard_map/dot_general | solution.py:39
  62.0 2.0 %copy.46 = bf16[448,384]{0,1:T(8,128)(2,1)} copy(bf16[448,384]{1,0:T(8,128)(2,1)} %convolution_convert_fusion.1) | data formatting | bytes 688128 | tf_op jit(solution)/shard_map/convert_element_type | solution.py:44
  64.0 2.6 %fusion.17 = bf16[448,3,128]{2,0,1:T(8,128)(2,1)} fusion(bf16[3,128,448]{2,1,0:T(8,128)(2,1)} %bitcast.67, f32[3,448]{1,0:T(4,128)S(1)} %fusion.76, f32[3,448,448]{1,2,0:T(8,128)S(1)} %get-tuple-element.12, f32[3,448]{1,0:T(4,128)S(1)} %get-tuple-element.11, pred[448,448]{0,1:T(8,128)(4,1)S(1)} %broadcast_compare_fusion), kind=kOutput, calls=%fused_computation.34 | convolution fusion | flops 156721152 | bytes 3308032 | tf_op jit(solution)/shard_map/transpose(jvp(hqk,khd->qhd))/dot_general | solution.py:26
  66.7 2.0 %copy.55 = bf16[448,3,128]{0,2,1:T(8,128)(2,1)} copy(bf16[448,3,128]{2,0,1:T(8,128)(2,1)} %fusion.17) | data formatting | bytes 688128 | tf_op jit(solution)/shard_map/convert_element_type | solution.py:50
  68.6 1.3 %convolution_convert_fusion.7 = bf16[64,384]{1,0:T(8,128)(2,1)S(1)} fusion(bf16[448,384]{0,1:T(8,128)(2,1)} %bitcast.59, s32[64]{0:T(128)S(1)} %iota_add_fusion), kind=kOutput, calls=%fused_computation.41 | convolution fusion | flops 22073344 | bytes 393472 | tf_op jit(solution)/shard_map/dot_general | solution.py:30
  69.9 4.5 %collective-permute-start.6 = (bf16[64,384]{1,0:T(8,128)(2,1)S(1)}, bf16[64,384]{1,0:T(8,128)(2,1)S(1)}, u32[]{:S(2)}, u32[]{:S(2)}) collective-permute-start(bf16[64,384]{1,0:T(8,128)(2,1)S(1)} %convolution_convert_fusion.7), channel_id=1, source_target_pairs={{0,28},{4,0},{8,4},{12,8},{16,12},{20,16},{24,20},{28,24},{1,29},{... | collective-permute-start | bytes 147464 | tf_op jit(solution)/shard_map/ppermute | solution.py:11
  74.4 2.8 %convert_reduce_fusion = (f32[3,448]{1,0:T(4,128)S(1)}, pred[3,448,448]{1,2,0:T(32,128)(4,1)S(1)}, f32[3,448]{1,0:T(4,128)S(1)}, f32[3,448,448]{1,2,0:T(8,128)S(1)}) fusion(f32[3,448]{1,0:T(4,128)S(1)} %get-tuple-element.11, f32[3,448,448]{1,2,0:T(8,128)S(1)} %get-tuple-element.12, pred[448,448]{0,1:T(8,128)(4,1)S(1)} %broadcast_compare_fusion, ...), kind=kOutput, calls=%fused_computation.2 | convolution fusion | flops 159556992 | bytes 6329344 | tf_op jit(solution)/shard_map/transpose(jvp(hqk,khd->qhd))/dot_general | solution.py:26
  77.2 0.9 fusion.77
  78.2 1.5 %copy-done.1 = f32[3,448,448]{1,2,0:T(8,128)} copy-done((f32[3,448,448]{1,2,0:T(8,128)}, f32[3,448,448]{1,2,0:T(8,128)S(1)}, u32[]{:S(2)}) %copy-start.1) | copy-done | bytes 2408472
  79.7 1.1 fusion.19
  80.8 0.2 copy.51
  81.0 2.8 %fusion.18 = bf16[448,3,128]{2,0,1:T(8,128)(2,1)S(1)} fusion(bf16[448,3,128]{0,2,1:T(8,128)(2,1)S(1)} %bitcast.56, f32[3,448,448]{1,2,0:T(8,128)} %copy-done.1, pred[3,448,448]{1,2,0:T(32,128)(4,1)} %copy-done.8, f32[3,448]{1,0:T(4,128)S(1)} %negate_divide_fusion, pred[448,448]{0,1:T(8,128)(4,1)S(1)} %broadcast_compare_fusion), kind=kOutput, calls=%fused_computation.35 | convolution fusion | flops 156549120 | bytes 3904768 | tf_op jit(solution)/shard_map/transpose(jvp(qhd,khd->hqk))/dot_general | solution.py:20
  83.8 0.2 copy.53
  84.0 0.3 convolution_convert_fusion.9
  84.3 0.4 fusion.29
  84.7 0.4 fusion.33
  85.1 0.4 fusion.31
  85.5 0.3 convolution_convert_fusion.8
  85.8 1.3 %collective-permute-start.5 = (bf16[64,384]{1,0:T(8,128)(2,1)S(1)}, bf16[64,384]{1,0:T(8,128)(2,1)S(1)}, u32[]{:S(2)}, u32[]{:S(2)}) collective-permute-start(bf16[64,384]{1,0:T(8,128)(2,1)S(1)} %convolution_convert_fusion.8), channel_id=1, source_target_pairs={{0,28},{4,0},{8,4},{12,8},{16,12},{20,16},{24,20},{28,24},{1,29},{... | collective-permute-start | bytes 147464 | tf_op jit(solution)/shard_map/ppermute | solution.py:11
  87.1 1.0 collective-permute-start.4
  88.1 1.0 fusion.16
  89.1 1.3 %collective-permute-done.5 = bf16[64,384]{1,0:T(8,128)(2,1)S(1)} collective-permute-done((bf16[64,384]{1,0:T(8,128)(2,1)S(1)}, bf16[64,384]{1,0:T(8,128)(2,1)S(1)}, u32[]{:S(2)}, u32[]{:S(2)}) %collective-permute-start.5) | collective-permute-done | bytes 49184 | tf_op jit(solution)/shard_map/ppermute | solution.py:11
  90.4 1.0 fusion.15
  91.5 1.0 fusion.14
  92.5 18.0 %reduce-scatter.2.cloned.1.call-done = bf16[448,1536]{1,0:T(8,128)(2,1)} async-done(((bf16[448,6144]{1,0:T(8,128)(2,1)}), bf16[448,1536]{1,0:T(8,128)(2,1)}) %reduce-scatter.2.cloned.1.call-update) | async-done | bytes 1376272 | tf_op jit(solution)/shard_map/reduce_scatter | solution.py:35
  (36 shorter events, 0.4 us)
Async XLA Ops:
  7.2 11.7 %copy-start = (bf16[384,384]{1,0:T(8,128)(2,1)S(1)}, bf16[384,384]{1,0:T(8,128)(2,1)}, u32[]{:S(2)}) copy-start(bf16[384,384]{1,0:T(8,128)(2,1)} %param.8) | copy-start | bytes 884740
  7.2 15.6 %copy-start.6 = (bf16[384,384]{1,0:T(8,128)(2,1)S(1)}, bf16[384,384]{1,0:T(8,128)(2,1)}, u32[]{:S(2)}) copy-start(bf16[384,384]{1,0:T(8,128)(2,1)} %param.9) | copy-start | bytes 884740
  7.2 15.2 %copy-start.5 = (bf16[384,384]{1,0:T(8,128)(2,1)S(1)}, bf16[384,384]{1,0:T(8,128)(2,1)}, u32[]{:S(2)}) copy-start(bf16[384,384]{1,0:T(8,128)(2,1)} %param.7) | copy-start | bytes 884740
  7.2 47.1 %all-gather.2.cloned.1.call-start = ((), (), s32[]{:S(2)}) async-start(), calls=%async_computation.2 | async-start | bytes 6881280 | tf_op jit(solution)/shard_map/all_gather | solution.py:40
  7.9 102.6 %reduce-scatter.2.cloned.1.call-start = ((), (), s32[]{:S(2)}) async-start(), calls=%async_computation.1 | async-start | bytes 6881280 | tf_op jit(solution)/shard_map/reduce_scatter | solution.py:35
  10.4 13.4 %collective-permute-start.1 = (s32[64]{0:T(128)S(1)}, s32[64]{0:T(128)S(1)}, u32[]{:S(2)}, u32[]{:S(2)}) collective-permute-start(s32[64]{0:T(128)S(1)} %select_reduce_fusion.3), channel_id=1, source_target_pairs={{0,4},{4,8},{8,12},{12,16},{16,20},{20,24},{24,28},{28,0},{1,5},{5... | collective-permute-start | bytes 776 | tf_op jit(solution)/shard_map/ppermute | solution.py:11
  14.5 13.9 %collective-permute-start = (bf16[64,384]{1,0:T(8,128)(2,1)S(1)}, bf16[64,384]{1,0:T(8,128)(2,1)S(1)}, u32[]{:S(2)}, u32[]{:S(2)}) collective-permute-start(bf16[64,384]{1,0:T(8,128)(2,1)S(1)} %convolution_convert_fusion.6), channel_id=1, source_target_pairs={{0,4},{4,8},{8,12},{12,16},{16,20},{20,24},{24,28},{28,0},{1,5},{5... | collective-permute-start | bytes 147464 | tf_op jit(solution)/shard_map/ppermute | solution.py:11
  17.2 9.0 %collective-permute-start.2 = (bf16[64,384]{1,0:T(8,128)(2,1)S(1)}, bf16[64,384]{1,0:T(8,128)(2,1)S(1)}, u32[]{:S(2)}, u32[]{:S(2)}) collective-permute-start(bf16[64,384]{1,0:T(8,128)(2,1)S(1)} %convolution_convert_fusion.5), channel_id=1, source_target_pairs={{0,4},{4,8},{8,12},{12,16},{16,20},{20,24},{24,28},{28,0},{1,5},{5... | collective-permute-start | bytes 147464 | tf_op jit(solution)/shard_map/ppermute | solution.py:11
  19.0 6.8 %collective-permute-start.3 = (bf16[64,384]{1,0:T(8,128)(2,1)S(1)}, bf16[64,384]{1,0:T(8,128)(2,1)S(1)}, u32[]{:S(2)}, u32[]{:S(2)}) collective-permute-start(bf16[64,384]{1,0:T(8,128)(2,1)S(1)} %convolution_convert_fusion.4), channel_id=1, source_target_pairs={{0,4},{4,8},{8,12},{12,16},{16,20},{20,24},{24,28},{28,0},{1,5},{5... | collective-permute-start | bytes 147464 | tf_op jit(solution)/shard_map/ppermute | solution.py:11
  29.8 2.6 %copy-start.7 = (bf16[448,384]{0,1:T(8,128)(2,1)S(1)}, bf16[448,384]{0,1:T(8,128)(2,1)}, u32[]{:S(2)}) copy-start(bf16[448,384]{0,1:T(8,128)(2,1)} %copy.38) | copy-start | bytes 1032196
  69.9 18.1 %collective-permute-start.6 = (bf16[64,384]{1,0:T(8,128)(2,1)S(1)}, bf16[64,384]{1,0:T(8,128)(2,1)S(1)}, u32[]{:S(2)}, u32[]{:S(2)}) collective-permute-start(bf16[64,384]{1,0:T(8,128)(2,1)S(1)} %convolution_convert_fusion.7), channel_id=1, source_target_pairs={{0,28},{4,0},{8,4},{12,8},{16,12},{20,16},{24,20},{28,24},{1,29},{... | collective-permute-start | bytes 147464 | tf_op jit(solution)/shard_map/ppermute | solution.py:11
  77.2 1.0 copy-start.8
  77.2 2.5 %copy-start.3 = (bf16[448,384]{0,1:T(8,128)(2,1)S(1)}, bf16[448,384]{0,1:T(8,128)(2,1)}, u32[]{:S(2)}) copy-start(bf16[448,384]{0,1:T(8,128)(2,1)} %copy.40) | copy-start | bytes 1032196
  78.2 1.5 %copy-start.1 = (f32[3,448,448]{1,2,0:T(8,128)}, f32[3,448,448]{1,2,0:T(8,128)S(1)}, u32[]{:S(2)}) copy-start(f32[3,448,448]{1,2,0:T(8,128)S(1)} %get-tuple-element.5) | copy-start | bytes 7225348
  79.7 1.3 %copy-start.2 = (bf16[448,384]{0,1:T(8,128)(2,1)S(1)}, bf16[448,384]{0,1:T(8,128)(2,1)}, u32[]{:S(2)}) copy-start(bf16[448,384]{0,1:T(8,128)(2,1)} %copy.39) | copy-start | bytes 1032196
  81.0 3.3 %copy-start.4 = (bf16[448,3,128]{0,2,1:T(8,128)(2,1)S(1)}, bf16[448,3,128]{0,2,1:T(8,128)(2,1)}, u32[]{:S(2)}) copy-start(bf16[448,3,128]{0,2,1:T(8,128)(2,1)} %copy.55) | copy-start | bytes 1032196
  85.8 4.6 %collective-permute-start.5 = (bf16[64,384]{1,0:T(8,128)(2,1)S(1)}, bf16[64,384]{1,0:T(8,128)(2,1)S(1)}, u32[]{:S(2)}, u32[]{:S(2)}) collective-permute-start(bf16[64,384]{1,0:T(8,128)(2,1)S(1)} %convolution_convert_fusion.8), channel_id=1, source_target_pairs={{0,28},{4,0},{8,4},{12,8},{16,12},{20,16},{24,20},{28,24},{1,29},{... | collective-permute-start | bytes 147464 | tf_op jit(solution)/shard_map/ppermute | solution.py:11
  87.1 4.4 %collective-permute-start.4 = (bf16[64,384]{1,0:T(8,128)(2,1)S(1)}, bf16[64,384]{1,0:T(8,128)(2,1)S(1)}, u32[]{:S(2)}, u32[]{:S(2)}) collective-permute-start(bf16[64,384]{1,0:T(8,128)(2,1)S(1)} %convolution_convert_fusion.9), channel_id=1, source_target_pairs={{0,28},{4,0},{8,4},{12,8},{16,12},{20,16},{24,20},{28,24},{1,29},{... | collective-permute-start | bytes 147464 | tf_op jit(solution)/shard_map/ppermute | solution.py:11
Sparse Core Ops, SparseCore 0:
  9.6 44.6 all-gather.1
  57.4 53.0 reduce-scatter.1
where the time goes:
time: 118 us; the launch traced here: 117 us
  matrix products  39.4 us (33%)
  waiting for transfers between devices  32.1 us (27%)
  starting transfers between devices  14.5 us (12%)
  between operations  14.4 us (12%)
  local copies, waits for them, and re-layouts  11 us (9%)
  other arithmetic  6.02 us (5%)
    reduce_scatter x1, waiting for transfers between devices, project_rows(): lax.psum_scatter(term.astype(jnp.bfloat16), 'tensor', scatter_dimension=1...  18 us
    ppermute x7, starting transfers between devices, shifted(): lax.ppermute(shard, axis, [(i, (i + by) % size) for i in range(size)])  14.5 us
    dot_general x18, matrix products, select_rows(): jnp.dot(mask.astype(values.dtype), values, preferred_element_type=jnp.flo...  10.7 us
    all_gather x1, waiting for transfers between devices, back_project(): lax.all_gather(cot_rows, 'tensor', axis=1, tiled=True)  10.3 us
    dot_general x1, matrix products, project_rows(): term = jnp.dot(attended, out_weight, preferred_element_type=jnp.float32)  7.91 us
    dot_general x1, matrix products, back_project(): lax.dot_general(lax.all_gather(cot_rows, 'tensor', axis=1, tiled=True), o...  7.73 us
    dot_general x3, matrix products, attend(): return jnp.einsum('hqk,khd->qhd', weights, vh).reshape(rows, heads * HEAD)  7.2 us
    dot_general x3, matrix products, attend(): scores = jnp.einsum('qhd,khd->hqk', qh, kh) * HEAD ** (-0.5)  5.81 us
  transfers between devices with their start and end apart: 9, of which 4 were waited for; matrix products, arithmetic and copies ran while one was open for 47% of the time, Pallas kernels for 0%

commit v1 on v0

v1 whole, which is shorter than its diff:
```python
import functools

import jax
import jax.numpy as jnp
from jax import lax
from jax.experimental import pallas as pl
from jax.experimental.pallas import tpu as pltpu
from jax.sharding import PartitionSpec as P

HEAD = 128
BF16 = jnp.bfloat16
F32 = jnp.float32
VMEM = pl.BlockSpec(memory_space=pltpu.VMEM)
SMEM = pl.BlockSpec(memory_space=pltpu.SMEM)
ANY = pl.BlockSpec(memory_space=pl.ANY)
LIMIT = 48 * 1024 * 1024


def nt(a, b):
    return lax.dot_general(a, b, (((1,), (1,)), ((), ())), preferred_element_type=F32)


def nn(a, b):
    return lax.dot_general(a, b, (((1,), (0,)), ((), ())), preferred_element_type=F32)


def tn(a, b):
    return lax.dot_general(a, b, (((0,), (0,)), ((), ())), preferred_element_type=F32)


def call(kernel, outs, ins, scratch=(), flops=0, moved=0, exps=0):
    return pl.pallas_call(
        kernel,
        out_shape=tuple(jax.ShapeDtypeStruct(s, t) for s, t in outs),
        in_specs=list(ins),
        out_specs=tuple(VMEM for _ in outs),
        scratch_shapes=list(scratch),
        compiler_params=pltpu.CompilerParams(vmem_limit_bytes=LIMIT),
        cost_estimate=pl.CostEstimate(flops=flops, bytes_accessed=moved, transcendentals=exps),
    )


def moved_block(seg, flags, blocks, cap):
    out = jnp.int32(blocks)
    for b in range(blocks):
        out = jnp.where(flags[0, seg[0, b * cap]] == 1, jnp.int32(b), out)
    return out


def forward_kernel(cap, seg, flags, q, k, v, att, sent, pt, rows_buf):
    rows, width = q.shape
    blocks = rows // cap
    gone = moved_block(seg, flags, blocks, cap)
    col_block = lax.broadcasted_iota(jnp.int32, (rows, 1), 0) // cap
    row_block = lax.broadcasted_iota(jnp.int32, (1, rows), 1) // cap
    key_id = jnp.zeros((rows, 1), jnp.int32)
    query_id = jnp.zeros((1, rows), jnp.int32)
    for b in range(blocks):
        image = seg[0, b * cap]
        key_id = jnp.where(col_block == b, image, key_id)
        query_id = jnp.where(row_block == b, image, query_id)
    same = key_id == query_id
    for h in range(width // HEAD):
        cols = slice(h * HEAD, (h + 1) * HEAD)
        scores = nt(k[:, cols], q[:, cols]) * HEAD ** (-0.5)
        scores = jnp.where(same, scores, -1e30)
        weights = jnp.exp(scores - jnp.max(scores, axis=0, keepdims=True))
        weights = weights * (1.0 / jnp.sum(weights, axis=0, keepdims=True))
        weights = weights.astype(BF16)
        pt[h] = weights
        out = tn(weights, v[:, cols]).astype(BF16)
        for b in range(blocks):
            slot = jnp.where(b < gone, b, jnp.where(b == gone, blocks, b - 1))
            rows_buf[slot, :, cols] = out[b * cap : (b + 1) * cap]
    empty = jnp.where(gone == blocks, blocks, blocks - 1)
    rows_buf[empty] = jnp.zeros((cap, width), BF16)
    for b in range(blocks):
        att[b * cap : (b + 1) * cap] = rows_buf[b]
    att[rows:] = jnp.zeros((cap, width), BF16)
    sent[...] = rows_buf[blocks]


def pick_kernel(cap, blocks, seg, flags, cot, out, sem):
    gone = moved_block(seg, flags, blocks, cap)
    start = pl.multiple_of(jnp.where(gone == blocks, blocks, blocks - 1) * cap, cap)
    copy = pltpu.make_async_copy(cot.at[pl.ds(start, cap), :], out, sem)
    copy.start()
    copy.wait()


def home_kernel(cap, blocks, seg, flags, cot, back, out, sems):
    gone = moved_block(seg, flags, blocks, cap)
    copies = []
    for b in range(blocks):
        start = pl.multiple_of((b - (b > gone).astype(jnp.int32)) * cap, cap)
        copies.append(
            pltpu.make_async_copy(
                cot.at[pl.ds(start, cap), :], out.at[pl.ds(b * cap, cap), :], sems.at[b]
            )
        )
    for c in copies:
        c.start()
    for c in copies:
        c.wait()

    @pl.when(gone < blocks)
    def _():
        start = pl.multiple_of(gone * cap, cap)
        copy = pltpu.make_async_copy(back, out.at[pl.ds(start, cap), :], sems.at[0])
        copy.start()
        copy.wait()


def own_kernel(ids, cot_own, cot_sib, weight, out, wbuf, sems):
    part = cot_own.shape[1]
    t = ids[0]
    copies = []
    for i in range(2):
        start = pl.multiple_of((t if i == 0 else t ^ 1) * part, part)
        copies.append(
            pltpu.make_async_copy(weight.at[:, pl.ds(start, part)], wbuf.at[i], sems.at[i])
        )
    for c in copies:
        c.start()
    copies[0].wait()
    out[...] = nt(cot_own[...], wbuf[0])
    copies[1].wait()
    out[...] += nt(cot_sib[...], wbuf[1])


def far_copies(ids, first, by_y, by_z, diag_a, diag_b, direct, wbuf, sems):
    place = ids[1]
    size, cols = first.shape
    half = size // 2
    top, low, whole = pl.ds(0, half), pl.ds(half, half), pl.ds(0, size)
    n = 0
    groups = []
    for share, pieces in (
        (place, ((first, whole),)),
        (place ^ 1, ((by_y, whole),)),
        (place ^ 2, ((by_z, whole),)),
        (place ^ 3, ((diag_a, top), (diag_b, low))),
    ):
        copies = []
        for src, where in pieces:
            copies.append(
                pltpu.make_async_copy(src, wbuf.at[share, where, :], sems.at[n])
            )
            n += 1
        start = pl.multiple_of(share * cols, cols)
        copies.append(
            pltpu.make_async_copy(
                direct.at[:, pl.ds(start, cols)],
                wbuf.at[share, pl.ds(size, direct.shape[0]), :],
                sems.at[n],
            )
        )
        n += 1
        groups.append((share, copies))
    return groups


def far_kernel(
    ids, cot_own, cot_sib, first, by_y, by_z, diag_a, diag_b, direct, out, wbuf, cbuf, sems, csems
):
    core = ids[0] & 1
    cols = wbuf.shape[2]
    loads = []
    for i, src in enumerate((cot_own, cot_sib)):
        for j in range(2):
            share = 2 * (core if i == 0 else 1 - core) + j
            loads.append(
                pltpu.make_async_copy(
                    src.at[:, pl.ds(j * cols, cols)], cbuf.at[share], csems.at[2 * i + j]
                )
            )
    groups = far_copies(ids, first, by_y, by_z, diag_a, diag_b, direct, wbuf, sems)
    for c in loads:
        c.start()
    for _, copies in groups:
        for c in copies:
            c.start()
    for c in loads:
        c.wait()
    total = None
    for share, copies in groups:
        for c in copies:
            c.wait()
        term = nt(cbuf[share], wbuf[share])
        total = term if total is None else total + term
    out[...] = total.astype(BF16)


def project_kernel(
    cap, seg, flags, ids, att, far_att, weight, first, by_y, by_z, diag_a, diag_b, direct,
    sib_out, own_out, left, wbuf, vbuf, sems, vsems,
):
    rows, width = att.shape
    blocks = rows // cap - 1
    t = ids[0]
    core = t & 1
    cols = wbuf.shape[2]
    groups = far_copies(ids, first, by_y, by_z, diag_a, diag_b, direct, wbuf, sems)
    loads = []
    for j in range(4):
        start = pl.multiple_of(((t >> 1) * 4 + j) * cols, cols)
        loads.append(
            pltpu.make_async_copy(weight.at[:, pl.ds(start, cols)], vbuf.at[j], vsems.at[j])
        )
    for c in loads:
        c.start()
    for _, copies in groups:
        for c in copies:
            c.start()
    gone = moved_block(seg, flags, blocks, cap)
    swap = gone < blocks
    last = (blocks - 1) * cap
    for i, src in enumerate((att, far_att)):
        where = slice(i * width, (i + 1) * width)
        left[:last, where] = src[:last]
        home, came = src[last:rows - cap], src[rows - cap :]
        left[last : rows - cap, where] = jnp.where(swap, came, home)
        left[rows - cap :, where] = jnp.where(swap, home, came)
    for c in loads:
        c.wait()
    for _, copies in groups:
        for c in copies:
            c.wait()
    for out, side in ((sib_out, 1 - core), (own_out, core)):
        for j in range(2):
            share = 2 * side + j
            term = nn(left[:, :width], vbuf[share]) + nn(left[:, width:], wbuf[share])
            out[:, j * cols : (j + 1) * cols] = term.astype(BF16)


def backward_kernel(q, k, v, pt, near, far, gq, gk, gv):
    for h in range(q.shape[1] // HEAD):
        cols = slice(h * HEAD, (h + 1) * HEAD)
        cot = (near[:, cols] + far[:, cols].astype(F32)).astype(BF16)
        weights = pt[h]
        gv[:, cols] = nn(weights, cot).astype(BF16)
        rise = nt(v[:, cols], cot)
        wide = weights.astype(F32)
        mean = jnp.sum(wide * rise, axis=0, keepdims=True)
        slope = (wide * (rise - mean) * HEAD ** (-0.5)).astype(BF16)
        gk[:, cols] = nn(slope, q[:, cols]).astype(BF16)
        gq[:, cols] = tn(slope, k[:, cols]).astype(BF16)


def flip(values, axis, by):
    size = lax.axis_size(axis)
    return lax.ppermute(values, axis, [(i, i ^ by) for i in range(size)])


def shifted(values, axis, by):
    size = lax.axis_size(axis)
    return lax.ppermute(values, axis, [(i, (i + by) % size) for i in range(size)])


def shards(queries, key_rows, value_rows, out_weight, segment_ids, move_flags, out_cotangent):
    home, width = queries.shape
    dest, part = out_cotangent.shape
    depth = out_weight.shape[1]
    cap = dest - home
    blocks = home // cap
    heads = width // HEAD
    t = lax.axis_index("tensor")
    place = lax.axis_index("dp") % 4
    ids = jnp.stack([t, place]).astype(jnp.int32)

    side_cols = depth // 2
    cols = side_cols // 4
    shared = (width * 3 // 4) // 32 * 32
    rest = width - shared
    far_side = (1 - t // 2) * side_cols
    share = lax.dynamic_slice(out_weight, (0, far_side + place * cols), (shared, cols))
    first = flip(share, "tensor", 2)

    scope = functools.partial(call)
    picked = scope(
        functools.partial(pick_kernel, cap, blocks),
        [((cap, part), BF16)],
        [SMEM, SMEM, ANY],
        [pltpu.SemaphoreType.DMA(())],
        moved=cap * part * 4,
    )(segment_ids, move_flags, out_cotangent)[0]
    back = shifted(picked, "dp", -1)

    att, sent, pt = scope(
        functools.partial(forward_kernel, cap),
        [((dest, width), BF16), ((cap, width), BF16), ((heads, home, home), BF16)],
        [SMEM, SMEM, VMEM, VMEM, VMEM],
        [pltpu.VMEM((blocks + 1, cap, width), BF16)],
        flops=4 * home * home * width,
        moved=5 * home * width * 2,
        exps=heads * home * home,
    )(segment_ids, move_flags, queries, key_rows, value_rows)
    came = shifted(sent, "dp", 1)

    by_y = flip(first, "dp", 1)
    by_z = flip(first, "dp", 2)
    direct = flip(
        lax.dynamic_slice(out_weight, (shared, far_side), (rest, side_cols)), "tensor", 2
    )

    cot_own = scope(
        functools.partial(home_kernel, cap, blocks),
        [((home, part), BF16)],
        [SMEM, SMEM, ANY, ANY],
        [pltpu.SemaphoreType.DMA((blocks,))],
        moved=home * part * 4,
    )(segment_ids, move_flags, out_cotangent, back)[0]
    cot_sib = flip(cot_own, "tensor", 1)

    half = shared // 2
    diag_a = flip(by_y[:half], "dp", 2)
    diag_b = flip(by_z[half:], "dp", 1)

    att = lax.dynamic_update_slice(att, came, (home, 0))
    far_att = flip(att, "tensor", 2)

    near = scope(
        own_kernel,
        [((home, width), F32)],
        [SMEM, VMEM, VMEM, ANY],
        [pltpu.VMEM((2, width, part), BF16), pltpu.SemaphoreType.DMA((2,))],
        flops=2 * home * width * side_cols,
        moved=(home + width) * side_cols * 2,
    )(ids, cot_own, cot_sib, out_weight)[0]

    pieces = (first, by_y, by_z, diag_a, diag_b, direct)
    send = scope(
        far_kernel,
        [((home, width), BF16)],
        [SMEM] + [ANY] * 8,
        [
            pltpu.VMEM((4, width, cols), BF16),
            pltpu.VMEM((4, home, cols), BF16),
            pltpu.SemaphoreType.DMA((9,)),
            pltpu.SemaphoreType.DMA((4,)),
        ],
        flops=2 * home * width * side_cols,
        moved=(home + width) * side_cols * 2,
    )(ids, cot_own, cot_sib, *pieces)[0]
    far = flip(send, "tensor", 2)

    sib_part, own_part = scope(
        functools.partial(project_kernel, cap),
        [((dest, part), BF16), ((dest, part), BF16)],
        [SMEM, SMEM, SMEM, VMEM, VMEM] + [ANY] * 7,
        [
            pltpu.VMEM((dest, 2 * width), BF16),
            pltpu.VMEM((4, width, cols), BF16),
            pltpu.VMEM((4, width, cols), BF16),
            pltpu.SemaphoreType.DMA((9,)),
            pltpu.SemaphoreType.DMA((4,)),
        ],
        flops=4 * dest * width * side_cols,
        moved=2 * width * side_cols * 2 + dest * side_cols * 2,
    )(segment_ids, move_flags, ids, att, far_att, out_weight, *pieces)
    other = flip(sib_part, "tensor", 1)
    projected = (own_part.astype(F32) + other.astype(F32)).astype(BF16)

    grad_q, grad_k, grad_v = scope(
        backward_kernel,
        [((home, width), BF16)] * 3,
        [VMEM] * 6,
        flops=8 * home * home * width,
        moved=9 * home * width * 2,
    )(queries, key_rows, value_rows, pt, near, far)
    return (projected, grad_q, grad_k, grad_v)


def wide_shards(queries, key_rows, value_rows, out_weight, segment_ids, move_flags, out_cotangent):
    home, width = queries.shape
    dest, part = out_cotangent.shape
    cap = dest - home
    blocks = home // cap
    heads = width // HEAD
    att, sent, pt = call(
        functools.partial(forward_kernel, cap),
        [((dest, width), BF16), ((cap, width), BF16), ((heads, home, home), BF16)],
        [SMEM, SMEM, VMEM, VMEM, VMEM],
        [pltpu.VMEM((blocks + 1, cap, width), BF16)],
    )(segment_ids, move_flags, queries, key_rows, value_rows)
    came = shifted(sent, "dp", 1)
    image_of = segment_ids[0, ::cap]
    gone = jnp.sum(jnp.take(move_flags[0], image_of))
    kept = home - gone * cap
    att = lax.dynamic_update_slice(att, came, (kept, 0))
    term = jnp.dot(att, out_weight, preferred_element_type=F32).astype(BF16)
    projected = lax.psum_scatter(term, "tensor", scatter_dimension=1, tiled=True)
    picked = lax.dynamic_slice(out_cotangent, (kept, 0), (cap, part))
    back = shifted(picked, "dp", -1)
    cot = call(
        functools.partial(home_kernel, cap, blocks),
        [((home, part), BF16)],
        [SMEM, SMEM, ANY, ANY],
        [pltpu.SemaphoreType.DMA((blocks,))],
    )(segment_ids, move_flags, out_cotangent, back)[0]
    whole = lax.all_gather(cot, "tensor", axis=1, tiled=True)
    near = nt(whole, out_weight)
    grad_q, grad_k, grad_v = call(
        backward_kernel, [((home, width), BF16)] * 3, [VMEM] * 6
    )(queries, key_rows, value_rows, pt, near, jnp.zeros((home, width), BF16))
    return (projected, grad_q, grad_k, grad_v)


def solution(mesh):
    square = mesh.shape["tensor"] == 4 and mesh.shape["dp"] % 4 == 0
    in_specs = (
        P("dp", "tensor"),
        P("dp", "tensor"),
        P("dp", "tensor"),
        P("tensor", None),
        P("dp", None),
        P("dp", None),
        P("dp", "tensor"),
    )
    out_specs = (P("dp", "tensor"), P("dp", "tensor"), P("dp", "tensor"), P("dp", "tensor"))
    return jax.shard_map(
        shards if square else wide_shards,
        mesh=mesh,
        in_specs=in_specs,
        out_specs=out_specs,
        check_vma=False,
    )
```

time: 118 us -> 64.9 us (0.55)
  matrix products: 39.4 us -> 0 us
  Pallas kernels: 0 us -> 20.3 us
  between operations: 14.4 us -> 0.81 us
  local copies, waits for them, and re-layouts: 11 us -> 2.36 us
  waiting for transfers between devices: 32.1 us -> 26.2 us
  other arithmetic: 6.02 us -> 1.49 us
    dot_general x26 -> x0, matrix products: 39.4 us -> none  [the longest x18 10.7 us: select_rows(): jnp.dot(mask.astype(values.dtype), values, preferred_element_type=jnp.flo...]
    ppermute x7 -> x12, waiting for transfers between devices: 3.05 us -> 26.2 us  [the longest x10 15.3 us: flip(): return lax.ppermute(values, axis, [(i, i ^ by) for i in range(size)])]
    pallas_call x0 -> x7, Pallas kernels: none -> 20.3 us  [the longest x1 5.37 us: shards(): scope(functools.partial(project_kernel, cap), [((dest, part), BF16), ((de...]
    reduce_scatter x1 -> x0, waiting for transfers between devices: 18 us -> none  [project_rows(): lax.psum_scatter(term.astype(jnp.bfloat16), 'tensor', scatter_dimension=1...]
    all_gather x1 -> x0, waiting for transfers between devices: 10.3 us -> none  [back_project(): lax.all_gather(cot_rows, 'tensor', axis=1, tiled=True)]
    convert_element_type x5 -> x0, local copies, waits for them, and re-layouts: 6.26 us -> none  [the longest x3 2.34 us: attention_grads(): return tuple((g.astype(jnp.bfloat16) for g in grads))]
    add x3 -> x0, local copies, waits for them, and re-layouts: 2.81 us -> none  [the longest x1 0.94 us: shards(): dest_q = select_rows(put_kept, queries) + select_rows(put_recv, in_q)]
    reduce_sum x4 -> x0, other arithmetic: 2.43 us -> none  [the longest x1 0.92 us: attend(): weights = jnp.exp(scores - peak)]
  transfers between devices with their start and end apart: 9 -> 12, of which waited for: 4 -> 4; matrix products, arithmetic and copies ran while one was open for 47% -> 2% of each run, Pallas kernels for 0% -> 31%
where the time goes in v1:
time: 64.9 us; the launch traced here: 64.7 us
  waiting for transfers between devices  26.2 us (40%)
  Pallas kernels  20.3 us (31%)
  starting transfers between devices  13.5 us (21%)
  local copies, waits for them, and re-layouts  2.36 us (4%)
  other arithmetic  1.49 us (2%)
  between operations  0.81 us (1%)
    ppermute x10, waiting for transfers between devices, flip(): return lax.ppermute(values, axis, [(i, i ^ by) for i in range(size)])  15.3 us
    ppermute x10, starting transfers between devices, flip(): return lax.ppermute(values, axis, [(i, i ^ by) for i in range(size)])  11.1 us
    ppermute x2, waiting for transfers between devices, shifted(): lax.ppermute(values, axis, [(i, (i + by) % size) for i in range(size)])  10.9 us
    pallas_call x1, Pallas kernels, shards(): scope(functools.partial(project_kernel, cap), [((dest, part), BF16), ((de...  5.37 us
    pallas_call x1, Pallas kernels, shards(): scope(far_kernel, [((home, width), BF16)], [SMEM] + [ANY] * 8, [pltpu.VME...  3.87 us
    pallas_call x1, Pallas kernels, shards(): scope(own_kernel, [((home, width), F32)], [SMEM, VMEM, VMEM, ANY], [pltpu...  3.31 us
    pallas_call x1, Pallas kernels, shards(): scope(backward_kernel, [((home, width), BF16)] * 3, [VMEM] * 6, flops=8 *...  2.51 us
    ppermute x2, starting transfers between devices, shifted(): lax.ppermute(values, axis, [(i, (i + by) % size) for i in range(size)])  2.37 us
  transfers between devices with their start and end apart: 12, of which 4 were waited for; matrix products, arithmetic and copies ran while one was open for 2% of the time, Pallas kernels for 31%

profile of v1, /device:TPU:0, one launch (start us, length us, event | category | flops | bytes accessed | tf_op | source)
XLA Modules:
  0.0 64.7 jit_solution(11775763426731514666)
XLA Ops:
  0.6 0.0 copy-start.5
  0.6 0.0 copy-start.4
  0.7 0.0 copy-start.3
  0.7 0.0 copy-start.2
  0.7 0.0 copy-start.1
  0.7 0.0 copy-start
  0.7 1.2 %constant_dynamic-slice_fusion.1 = bf16[288,768]{1,0:T(8,128)(2,1)S(1)} fusion(bf16[384,6144]{1,0:T(8,128)(2,1)} %weight.3, s32[]{:T(128)S(6)} %select_n.19), kind=kLoop, calls=%fused_computation.4 | loop fusion | bytes 884740 | tf_op jit(solution)/shard_map/dynamic_slice | solution.py:276
  1.9 3.0 %collective-permute-start.2 = (bf16[288,768]{1,0:T(8,128)(2,1)S(1)}, bf16[288,768]{1,0:T(8,128)(2,1)S(1)}, u32[]{:S(2)}, u32[]{:S(2)}) collective-permute-start(bf16[288,768]{1,0:T(8,128)(2,1)S(1)} %constant_dynamic-slice_fusion.1), channel_id=1, source_target_pairs={{0,2},{1,3},{2,0},{3,1},{4,6},{5,7},{6,4},{7,5},{8,10},{9,11},{10,... | collective-permute-start | bytes 1327112 | tf_op jit(solution)/shard_map/ppermute | solution.py:252
  4.9 10.2 %collective-permute-done.2.first = bf16[288,768]{1,0:T(8,128)(2,1)S(1)} collective-permute-done((bf16[288,768]{1,0:T(8,128)(2,1)S(1)}, bf16[288,768]{1,0:T(8,128)(2,1)S(1)}, u32[]{:S(2)}, u32[]{:S(2)}) %collective-permute-start.2) | collective-permute-done | bytes 442400 | tf_op jit(solution)/shard_map/ppermute | solution.py:252
  15.1 1.8 %collective-permute-start.4 = (bf16[288,768]{1,0:T(8,128)(2,1)S(1)}, bf16[288,768]{1,0:T(8,128)(2,1)S(1)}, u32[]{:S(2)}, u32[]{:S(2)}) collective-permute-start(bf16[288,768]{1,0:T(8,128)(2,1)S(1)} %collective-permute-done.2.first), channel_id=1, source_target_pairs={{0,8},{4,12},{8,0},{12,4},{16,24},{20,28},{24,16},{28,20},{1,9},{5... | collective-permute-start | bytes 1327112 | tf_op jit(solution)/shard_map/ppermute | solution.py:252
  16.9 1.5 %collective-permute-start.3 = (bf16[288,768]{1,0:T(8,128)(2,1)S(1)}, bf16[288,768]{1,0:T(8,128)(2,1)S(1)}, u32[]{:S(2)}, u32[]{:S(2)}) collective-permute-start(bf16[288,768]{1,0:T(8,128)(2,1)S(1)} %collective-permute-done.2.first), channel_id=1, source_target_pairs={{0,4},{4,0},{8,12},{12,8},{16,20},{20,16},{24,28},{28,24},{1,5},{5... | collective-permute-start | bytes 1327112 | tf_op jit(solution)/shard_map/ppermute | solution.py:252
  18.4 1.1 %constant_dynamic-slice_fusion = bf16[96,3072]{1,0:T(8,128)(2,1)S(1)} fusion(bf16[384,6144]{1,0:T(8,128)(2,1)} %weight.3, s32[]{:T(128)S(6)} %select_n.20), kind=kLoop, calls=%fused_computation.2 | loop fusion | bytes 1179652 | tf_op jit(solution)/shard_map/dynamic_slice | solution.py:303
  19.5 1.6 %collective-permute-start.7 = (bf16[96,3072]{1,0:T(8,128)(2,1)S(1)}, bf16[96,3072]{1,0:T(8,128)(2,1)S(1)}, u32[]{:S(2)}, u32[]{:S(2)}) collective-permute-start(bf16[96,3072]{1,0:T(8,128)(2,1)S(1)} %constant_dynamic-slice_fusion), channel_id=1, source_target_pairs={{0,2},{1,3},{2,0},{3,1},{4,6},{5,7},{6,4},{7,5},{8,10},{9,11},{10,... | collective-permute-start | bytes 1769480 | tf_op jit(solution)/shard_map/ppermute | solution.py:252
  21.1 0.0 copy-done.5
  21.1 0.0 copy-done.4
  21.1 0.0 copy-done.3
  21.1 0.0 copy-done.2
  21.1 0.0 copy-done.1
  21.1 2.2 %shard_map.102 = (bf16[448,384]{1,0:T(8,128)(2,1)S(1)}, bf16[64,384]{1,0:T(8,128)(2,1)S(1)}, bf16[3,384,384]{2,1,0:T(8,128)(2,1)S(1)}) custom-call(s32[1,384]{1,0:T(1,128)S(1)} %copy-done.4, s32[1,384]{1,0:T(1,128)S(1)} %copy-done.5, bf16[384,384]{1,0:T(8,128)(2,1)S(1)} %copy-done.1, bf16[384,384]{1,0:T(8,128)(2,1)S(1)} %copy-done.2, ...), custom_call_target="tpu_custom_call" | custom-call | flops 226492416 | bytes 1474560 | tf_op jit(solution)/shard_map/pallas_call | solution.py:289
  23.4 0.6 collective-permute-start
  23.9 6.5 %collective-permute-done = bf16[64,384]{1,0:T(8,128)(2,1)S(1)} collective-permute-done((bf16[64,384]{1,0:T(8,128)(2,1)S(1)}, bf16[64,384]{1,0:T(8,128)(2,1)S(1)}, u32[]{:S(2)}, u32[]{:S(2)}) %collective-permute-start) | collective-permute-done | bytes 49184 | tf_op jit(solution)/shard_map/ppermute | solution.py:257
  30.4 1.6 %collective-permute-start.1 = (bf16[448,384]{1,0:T(8,128)(2,1)S(1)}, bf16[448,384]{1,0:T(8,128)(2,1)S(1)}, u32[]{:S(2)}, u32[]{:S(2)}) collective-permute-start(bf16[448,384]{1,0:T(8,128)(2,1)S(1)} %constant_dynamic-update-slice_fusion.att), channel_id=1, source_target_pairs={{0,2},{1,3},{2,0},{3,1},{4,6},{5,7},{6,4},{7,5},{8,10},{9,11},{10,... | collective-permute-start | bytes 1032200 | tf_op jit(solution)/shard_map/ppermute | solution.py:252
  32.0 0.0 copy-done
  32.0 0.9 %shard_map.104 = bf16[64,1536]{1,0:T(8,128)(2,1)S(1)} custom-call(s32[1,384]{1,0:T(1,128)S(1)} %copy-done.4, s32[1,384]{1,0:T(1,128)S(1)} %copy-done.5, bf16[448,1536]{1,0:T(8,128)(2,1)S(1)} %copy-done), custom_call_target="tpu_custom_call" | custom-call | bytes 393216 | tf_op jit(solution)/shard_map/pallas_call | solution.py:280
  32.8 1.8 %collective-permute-start.9 = (bf16[64,1536]{1,0:T(8,128)(2,1)S(1)}, bf16[64,1536]{1,0:T(8,128)(2,1)S(1)}, u32[]{:S(2)}, u32[]{:S(2)}) collective-permute-start(bf16[64,1536]{1,0:T(8,128)(2,1)S(1)} %shard_map.104), channel_id=1, source_target_pairs={{0,28},{4,0},{8,4},{12,8},{16,12},{20,16},{24,20},{28,24},{1,29},{... | collective-permute-start | bytes 589832 | tf_op jit(solution)/shard_map/ppermute | solution.py:257
  34.6 0.0 collective-permute-done.4.by_z
  34.7 0.3 collective-permute-start.6
  35.0 0.0 collective-permute-done.3.by_y
  35.0 0.1 collective-permute-start.5
  35.1 4.4 %collective-permute-done.9.back = bf16[64,1536]{1,0:T(8,128)(2,1)S(1)} collective-permute-done((bf16[64,1536]{1,0:T(8,128)(2,1)S(1)}, bf16[64,1536]{1,0:T(8,128)(2,1)S(1)}, u32[]{:S(2)}, u32[]{:S(2)}) %collective-permute-start.9) | collective-permute-done | bytes 196640 | tf_op jit(solution)/shard_map/ppermute | solution.py:257
  39.5 2.2 %shard_map.105.cot_own = bf16[384,1536]{1,0:T(8,128)(2,1)S(1)} custom-call(s32[1,384]{1,0:T(1,128)S(1)} %copy-done.4, s32[1,384]{1,0:T(1,128)S(1)} %copy-done.5, bf16[448,1536]{1,0:T(8,128)(2,1)S(1)} %copy-done, bf16[64,1536]{1,0:T(8,128)(2,1)S(1)} %collective-permute-done.9.back), custom_call_target="tpu_custom_call" | custom-call | bytes 2359296 | tf_op jit(solution)/shard_map/pallas_call | solution.py:306
  41.7 0.1 collective-permute-start.10
  41.8 0.1 pad_add_fusion.ids
  41.9 0.0 collective-permute-done.1.far_att
  41.9 0.0 collective-permute-done.7.direct
  41.9 0.0 collective-permute-done.6.diag_b
  41.9 0.0 collective-permute-done.5.diag_a
  41.9 5.4 %shard_map.103 = (bf16[448,1536]{1,0:T(8,128)(2,1)S(1)}, bf16[448,1536]{1,0:T(8,128)(2,1)S(1)}) custom-call(s32[1,384]{1,0:T(1,128)S(1)} %copy-done.4, s32[1,384]{1,0:T(1,128)S(1)} %copy-done.5, s32[2]{0:T(128)S(1)} %pad_add_fusion.ids, bf16[448,384]{1,0:T(8,128)(2,1)S(1)} %constant_dynamic-update-slice_fusion.att, ...), custom_call_target="tpu_custom_call" | custom-call | flops 2113929216 | bytes 7471104 | tf_op jit(solution)/shard_map/pallas_call | solution.py:347
  47.3 0.6 collective-permute-start.8
  47.9 0.0 collective-permute-done.10.cot_sib
  47.9 3.9 %shard_map.107 = bf16[384,384]{1,0:T(8,128)(2,1)S(1)} custom-call(s32[2]{0:T(128)S(1)} %pad_add_fusion.ids, bf16[384,1536]{1,0:T(8,128)(2,1)S(1)} %shard_map.105.cot_own, bf16[384,1536]{1,0:T(8,128)(2,1)S(1)} %collective-permute-done.10.cot_sib, bf16[288,768]{1,0:T(8,128)(2,1)S(1)} %collective-permute-done.2.first, ...), custom_call_target="tpu_custom_call" | custom-call | flops 905969664 | bytes 4718592 | tf_op jit(solution)/shard_map/pallas_call | solution.py:332
  51.7 0.6 collective-permute-start.11
  52.3 3.3 %shard_map.106.near = f32[384,384]{1,0:T(8,128)S(1)} custom-call(s32[2]{0:T(128)S(1)} %pad_add_fusion.ids, bf16[384,1536]{1,0:T(8,128)(2,1)S(1)} %shard_map.105.cot_own, bf16[384,1536]{1,0:T(8,128)(2,1)S(1)} %collective-permute-done.10.cot_sib, bf16[384,6144]{1,0:T(8,128)(2,1)} %weight.3), custom_call_target="tpu_custom_call" | custom-call | flops 905969664 | bytes 4718592 | tf_op jit(solution)/shard_map/pallas_call | solution.py:322
  55.7 5.1 %collective-permute-done.11.far = bf16[384,384]{1,0:T(8,128)(2,1)S(1)} collective-permute-done((bf16[384,384]{1,0:T(8,128)(2,1)S(1)}, bf16[384,384]{1,0:T(8,128)(2,1)S(1)}, u32[]{:S(2)}, u32[]{:S(2)}) %collective-permute-start.11) | collective-permute-done | bytes 294944 | tf_op jit(solution)/shard_map/ppermute | solution.py:252
  60.7 2.5 %shard_map.108 = (bf16[384,384]{1,0:T(8,128)(2,1)}, bf16[384,384]{1,0:T(8,128)(2,1)}, bf16[384,384]{1,0:T(8,128)(2,1)}) custom-call(bf16[384,384]{1,0:T(8,128)(2,1)S(1)} %copy-done.1, bf16[384,384]{1,0:T(8,128)(2,1)S(1)} %copy-done.2, bf16[384,384]{1,0:T(8,128)(2,1)S(1)} %copy-done.3, bf16[3,384,384]{2,1,0:T(8,128)(2,1)S(1)} %get-tuple-element.16.pt, ...), custom_call_target="tpu_custom_call" | custom-call | flops 452984832 | bytes 2654208 | tf_op jit(solution)/shard_map/pallas_call | solution.py:364
  63.3 0.0 collective-permute-done.8
  63.3 1.4 %add_convert_fusion = bf16[448,1536]{1,0:T(8,128)(2,1)} fusion(bf16[448,1536]{1,0:T(8,128)(2,1)S(1)} %collective-permute-done.8, bf16[448,1536]{1,0:T(8,128)(2,1)S(1)} %get-tuple-element.14), kind=kLoop, calls=%fused_computation | loop fusion | flops 2752512 | bytes 4128768 | tf_op jit(solution)/shard_map/convert_element_type | solution.py:362
  (3 shorter events, 0.0 us)
Async XLA Ops:
  0.6 20.5 %copy-start.5 = (s32[1,384]{1,0:T(1,128)S(1)}, s32[1,384]{1,0:T(1,128)}, u32[]{:S(2)}) copy-start(s32[1,384]{1,0:T(1,128)} %flags.7) | copy-start | bytes 4612
  0.6 20.5 %copy-start.4 = (s32[1,384]{1,0:T(1,128)S(1)}, s32[1,384]{1,0:T(1,128)}, u32[]{:S(2)}) copy-start(s32[1,384]{1,0:T(1,128)} %seg.7) | copy-start | bytes 4612
  0.7 20.5 %copy-start.3 = (bf16[384,384]{1,0:T(8,128)(2,1)S(1)}, bf16[384,384]{1,0:T(8,128)(2,1)}, u32[]{:S(2)}) copy-start(bf16[384,384]{1,0:T(8,128)(2,1)} %v.3) | copy-start | bytes 884740
  0.7 20.4 %copy-start.2 = (bf16[384,384]{1,0:T(8,128)(2,1)S(1)}, bf16[384,384]{1,0:T(8,128)(2,1)}, u32[]{:S(2)}) copy-start(bf16[384,384]{1,0:T(8,128)(2,1)} %k.3) | copy-start | bytes 884740
  0.7 20.4 %copy-start.1 = (bf16[384,384]{1,0:T(8,128)(2,1)S(1)}, bf16[384,384]{1,0:T(8,128)(2,1)}, u32[]{:S(2)}) copy-start(bf16[384,384]{1,0:T(8,128)(2,1)} %q.3) | copy-start | bytes 884740
  0.7 31.3 %copy-start = (bf16[448,1536]{1,0:T(8,128)(2,1)S(1)}, bf16[448,1536]{1,0:T(8,128)(2,1)}, u32[]{:S(2)}) copy-start(bf16[448,1536]{1,0:T(8,128)(2,1)} %cot.3) | copy-start | bytes 4128772
  1.9 13.2 %collective-permute-start.2 = (bf16[288,768]{1,0:T(8,128)(2,1)S(1)}, bf16[288,768]{1,0:T(8,128)(2,1)S(1)}, u32[]{:S(2)}, u32[]{:S(2)}) collective-permute-start(bf16[288,768]{1,0:T(8,128)(2,1)S(1)} %constant_dynamic-slice_fusion.1), channel_id=1, source_target_pairs={{0,2},{1,3},{2,0},{3,1},{4,6},{5,7},{6,4},{7,5},{8,10},{9,11},{10,... | collective-permute-start | bytes 1327112 | tf_op jit(solution)/shard_map/ppermute | solution.py:252
  15.1 19.6 %collective-permute-start.4 = (bf16[288,768]{1,0:T(8,128)(2,1)S(1)}, bf16[288,768]{1,0:T(8,128)(2,1)S(1)}, u32[]{:S(2)}, u32[]{:S(2)}) collective-permute-start(bf16[288,768]{1,0:T(8,128)(2,1)S(1)} %collective-permute-done.2.first), channel_id=1, source_target_pairs={{0,8},{4,12},{8,0},{12,4},{16,24},{20,28},{24,16},{28,20},{1,9},{5... | collective-permute-start | bytes 1327112 | tf_op jit(solution)/shard_map/ppermute | solution.py:252
  16.9 18.1 %collective-permute-start.3 = (bf16[288,768]{1,0:T(8,128)(2,1)S(1)}, bf16[288,768]{1,0:T(8,128)(2,1)S(1)}, u32[]{:S(2)}, u32[]{:S(2)}) collective-permute-start(bf16[288,768]{1,0:T(8,128)(2,1)S(1)} %collective-permute-done.2.first), channel_id=1, source_target_pairs={{0,4},{4,0},{8,12},{12,8},{16,20},{20,16},{24,28},{28,24},{1,5},{5... | collective-permute-start | bytes 1327112 | tf_op jit(solution)/shard_map/ppermute | solution.py:252
  19.5 22.4 %collective-permute-start.7 = (bf16[96,3072]{1,0:T(8,128)(2,1)S(1)}, bf16[96,3072]{1,0:T(8,128)(2,1)S(1)}, u32[]{:S(2)}, u32[]{:S(2)}) collective-permute-start(bf16[96,3072]{1,0:T(8,128)(2,1)S(1)} %constant_dynamic-slice_fusion), channel_id=1, source_target_pairs={{0,2},{1,3},{2,0},{3,1},{4,6},{5,7},{6,4},{7,5},{8,10},{9,11},{10,... | collective-permute-start | bytes 1769480 | tf_op jit(solution)/shard_map/ppermute | solution.py:252
  23.4 7.1 %collective-permute-start = (bf16[64,384]{1,0:T(8,128)(2,1)S(1)}, bf16[64,384]{1,0:T(8,128)(2,1)S(1)}, u32[]{:S(2)}, u32[]{:S(2)}) collective-permute-start(bf16[64,384]{1,0:T(8,128)(2,1)S(1)} %get-tuple-element.13), channel_id=1, source_target_pairs={{0,4},{4,8},{8,12},{12,16},{16,20},{20,24},{24,28},{28,0},{1,5},{5... | collective-permute-start | bytes 147464 | tf_op jit(solution)/shard_map/ppermute | solution.py:257
  30.4 11.5 %collective-permute-start.1 = (bf16[448,384]{1,0:T(8,128)(2,1)S(1)}, bf16[448,384]{1,0:T(8,128)(2,1)S(1)}, u32[]{:S(2)}, u32[]{:S(2)}) collective-permute-start(bf16[448,384]{1,0:T(8,128)(2,1)S(1)} %constant_dynamic-update-slice_fusion.att), channel_id=1, source_target_pairs={{0,2},{1,3},{2,0},{3,1},{4,6},{5,7},{6,4},{7,5},{8,10},{9,11},{10,... | collective-permute-start | bytes 1032200 | tf_op jit(solution)/shard_map/ppermute | solution.py:252
  32.8 6.7 %collective-permute-start.9 = (bf16[64,1536]{1,0:T(8,128)(2,1)S(1)}, bf16[64,1536]{1,0:T(8,128)(2,1)S(1)}, u32[]{:S(2)}, u32[]{:S(2)}) collective-permute-start(bf16[64,1536]{1,0:T(8,128)(2,1)S(1)} %shard_map.104), channel_id=1, source_target_pairs={{0,28},{4,0},{8,4},{12,8},{16,12},{20,16},{24,20},{28,24},{1,29},{... | collective-permute-start | bytes 589832 | tf_op jit(solution)/shard_map/ppermute | solution.py:257
  34.7 7.2 %collective-permute-start.6 = (bf16[144,768]{1,0:T(8,128)(2,1)S(1)}, bf16[144,768]{1,0:T(8,128)(2,1)S(1)}, u32[]{:S(2)}, u32[]{:S(2)}) collective-permute-start(bf16[144,768]{1,0:T(8,128)(2,1)S(1)} %slice.9), channel_id=1, source_target_pairs={{0,4},{4,0},{8,12},{12,8},{16,20},{20,16},{24,28},{28,24},{1,5},{5... | collective-permute-start | bytes 663560 | tf_op jit(solution)/shard_map/ppermute | solution.py:252
  35.0 6.9 %collective-permute-start.5 = (bf16[144,768]{1,0:T(8,128)(2,1)S(1)}, bf16[144,768]{1,0:T(8,128)(2,1)S(1)}, u32[]{:S(2)}, u32[]{:S(2)}) collective-permute-start(bf16[144,768]{1,0:T(8,128)(2,1)S(1)} %slice.8), channel_id=1, source_target_pairs={{0,8},{4,12},{8,0},{12,4},{16,24},{20,28},{24,16},{28,20},{1,9},{5... | collective-permute-start | bytes 663560 | tf_op jit(solution)/shard_map/ppermute | solution.py:252
  41.7 6.1 %collective-permute-start.10 = (bf16[384,1536]{1,0:T(8,128)(2,1)S(1)}, bf16[384,1536]{1,0:T(8,128)(2,1)S(1)}, u32[]{:S(2)}, u32[]{:S(2)}) collective-permute-start(bf16[384,1536]{1,0:T(8,128)(2,1)S(1)} %shard_map.105.cot_own), channel_id=1, source_target_pairs={{0,1},{1,0},{2,3},{3,2},{4,5},{5,4},{6,7},{7,6},{8,9},{9,8},{10,11... | collective-permute-start | bytes 3538952 | tf_op jit(solution)/shard_map/ppermute | solution.py:252
  47.3 16.0 %collective-permute-start.8 = (bf16[448,1536]{1,0:T(8,128)(2,1)S(1)}, bf16[448,1536]{1,0:T(8,128)(2,1)S(1)}, u32[]{:S(2)}, u32[]{:S(2)}) collective-permute-start(bf16[448,1536]{1,0:T(8,128)(2,1)S(1)} %get-tuple-element.15), channel_id=1, source_target_pairs={{0,1},{1,0},{2,3},{3,2},{4,5},{5,4},{6,7},{7,6},{8,9},{9,8},{10,11... | collective-permute-start | bytes 4128776 | tf_op jit(solution)/shard_map/ppermute | solution.py:252
  51.7 9.0 %collective-permute-start.11 = (bf16[384,384]{1,0:T(8,128)(2,1)S(1)}, bf16[384,384]{1,0:T(8,128)(2,1)S(1)}, u32[]{:S(2)}, u32[]{:S(2)}) collective-permute-start(bf16[384,384]{1,0:T(8,128)(2,1)S(1)} %shard_map.107), channel_id=1, source_target_pairs={{0,2},{1,3},{2,0},{3,1},{4,6},{5,7},{6,4},{7,5},{8,10},{9,11},{10,... | collective-permute-start | bytes 884744 | tf_op jit(solution)/shard_map/ppermute | solution.py:252

commit v2 on v1

v2 whole, which is shorter than its diff:
```python
import functools

import jax
import jax.numpy as jnp
from jax import lax
from jax.experimental import pallas as pl
from jax.experimental.pallas import tpu as pltpu
from jax.sharding import PartitionSpec as P

HEAD = 128
BF16 = jnp.bfloat16
F32 = jnp.float32
VMEM = pl.BlockSpec(memory_space=pltpu.VMEM)
SMEM = pl.BlockSpec(memory_space=pltpu.SMEM)
ANY = pl.BlockSpec(memory_space=pl.ANY)
LIMIT = 16 * 1024 * 1024
OPEN_LIMIT = 60 * 1024 * 1024


def nt(a, b):
    return lax.dot_general(a, b, (((1,), (1,)), ((), ())), preferred_element_type=F32)


def nn(a, b):
    return lax.dot_general(a, b, (((1,), (0,)), ((), ())), preferred_element_type=F32)


def tn(a, b):
    return lax.dot_general(a, b, (((0,), (0,)), ((), ())), preferred_element_type=F32)


def call(kernel, outs, ins, scratch=(), flops=0, moved=0, exps=0, limit=LIMIT):
    return pl.pallas_call(
        kernel,
        out_shape=tuple(jax.ShapeDtypeStruct(s, t) for s, t in outs),
        in_specs=list(ins),
        out_specs=tuple(SMEM if t == jnp.int32 else VMEM for _, t in outs),
        scratch_shapes=list(scratch),
        compiler_params=pltpu.CompilerParams(vmem_limit_bytes=limit),
        cost_estimate=pl.CostEstimate(flops=flops, bytes_accessed=moved, transcendentals=exps),
    )


def moved_block(seg, flags, blocks, cap):
    out = jnp.int32(blocks)
    for b in range(blocks):
        out = jnp.where(flags[0, seg[0, b * cap]] == 1, jnp.int32(b), out)
    return out


def forward_kernel(cap, seg, gone_ref, q, k, v, att, sent, pt, rows_buf):
    rows, width = q.shape
    blocks = rows // cap
    gone = gone_ref[0]
    col_block = lax.broadcasted_iota(jnp.int32, (rows, 1), 0) // cap
    row_block = lax.broadcasted_iota(jnp.int32, (1, rows), 1) // cap
    key_id = jnp.zeros((rows, 1), jnp.int32)
    query_id = jnp.zeros((1, rows), jnp.int32)
    for b in range(blocks):
        image = seg[0, b * cap]
        key_id = jnp.where(col_block == b, image, key_id)
        query_id = jnp.where(row_block == b, image, query_id)
    same = key_id == query_id
    for h in range(width // HEAD):
        cols = slice(h * HEAD, (h + 1) * HEAD)
        scores = nt(k[:, cols], q[:, cols]) * HEAD ** (-0.5)
        scores = jnp.where(same, scores, -1e30)
        weights = jnp.exp(scores - jnp.max(scores, axis=0, keepdims=True))
        weights = weights * (1.0 / jnp.sum(weights, axis=0, keepdims=True))
        weights = weights.astype(BF16)
        pt[h] = weights
        out = tn(weights, v[:, cols]).astype(BF16)
        for b in range(blocks):
            slot = jnp.where(b < gone, b, jnp.where(b == gone, blocks, b - 1))
            rows_buf[slot, :, cols] = out[b * cap : (b + 1) * cap]
    empty = jnp.where(gone == blocks, blocks, blocks - 1)
    rows_buf[empty] = jnp.zeros((cap, width), BF16)
    for b in range(blocks):
        att[b * cap : (b + 1) * cap] = rows_buf[b]
    att[rows:] = jnp.zeros((cap, width), BF16)
    sent[...] = rows_buf[blocks]


def open_kernel(
    cap, blocks, seg, flags, t, place, weight, cot, gone_out, share_out, direct_out, picked_out, sems
):
    cols = share_out.shape[1]
    rest = direct_out.shape[1] // 2
    part = cot.shape[1]
    far = (1 - (t[0] >> 1)) * 2 * part
    start = pl.multiple_of(far + (place[0] >> 1) * part + (place[0] & 1) * cols, HEAD)
    copies = [pltpu.make_async_copy(weight.at[:, pl.ds(start, cols)], share_out, sems.at[0])]
    for k in range(2):
        start = pl.multiple_of(far + k * part + 2 * cols, HEAD)
        copies.append(
            pltpu.make_async_copy(
                weight.at[:, pl.ds(start, rest)],
                direct_out.at[:, pl.ds(k * rest, rest)],
                sems.at[1 + k],
            )
        )
    for c in copies:
        c.start()
    gone = moved_block(seg, flags, blocks, cap)
    gone_out[0] = gone
    row = pl.multiple_of(jnp.where(gone == blocks, blocks, blocks - 1) * cap, cap)
    copies.append(pltpu.make_async_copy(cot.at[pl.ds(row, cap), :], picked_out, sems.at[3]))
    copies[-1].start()
    for c in copies:
        c.wait()


def pick_kernel(cap, blocks, seg, flags, cot, gone_out, picked_out):
    gone = moved_block(seg, flags, blocks, cap)
    gone_out[0] = gone
    row = jnp.where(gone == blocks, blocks, blocks - 1)
    picked_out[...] = cot[pl.ds(pl.multiple_of(row * cap, cap), cap), :]


def home_kernel(cap, blocks, gone_ref, *refs):
    gone = gone_ref[0]
    n = len(refs) // 3
    cots, backs, outs = refs[:n], refs[n : 2 * n], refs[2 * n :]
    for cot, out in zip(cots, outs):
        for b in range(blocks):
            start = pl.multiple_of((b - (b > gone).astype(jnp.int32)) * cap, cap)
            out[b * cap : (b + 1) * cap] = cot[pl.ds(start, cap), :]

    @pl.when(gone < blocks)
    def _():
        for back, out in zip(backs, outs):
            out[pl.ds(pl.multiple_of(gone * cap, cap), cap), :] = back[...]


def own_kernel(t_ref, cot_own, cot_sib, weight, out):
    part = cot_own.shape[1]
    t = t_ref[0]
    total = None
    for cot, i in ((cot_own, t), (cot_sib, t ^ 1)):
        start = pl.multiple_of(i * part, part)
        term = nt(cot[...], weight[:, pl.ds(start, part)])
        total = term if total is None else total + term
    out[...] = total


def by_place(t, place, own, sib, run):
    same = (t & 1) == (place >> 1)
    pl.when(same)(lambda: run(own, sib))
    pl.when(jnp.logical_not(same))(lambda: run(sib, own))


def far_kernel(t, place, cot_own, cot_sib, first, by_y, by_z, out):
    cols = first.shape[1]
    y = place[0] & 1
    near_at = pl.ds(pl.multiple_of(y * cols, HEAD), cols)
    next_at = pl.ds(pl.multiple_of((1 - y) * cols, HEAD), cols)

    def run(a, b):
        out[...] = (
            nt(a[:, near_at], first[...])
            + nt(a[:, next_at], by_y[...])
            + nt(b[:, near_at], by_z[...])
        )

    by_place(t[0], place[0], cot_own, cot_sib, run)


def last_kernel(t, place, cot_own, cot_sib, part_sum, diag_a, diag_b, direct, out):
    wide_a, wide_b = diag_a.shape[1], diag_b.shape[1]
    cols = wide_a + wide_b
    rest = direct.shape[1] // 2
    y = place[0] & 1
    core = t[0] & 1
    a_at = pl.ds(pl.multiple_of((1 - y) * cols, HEAD), wide_a)
    b_at = pl.ds(pl.multiple_of((1 - y) * cols + wide_a, HEAD), wide_b)
    own_at = pl.ds(pl.multiple_of(core * rest, HEAD), rest)
    sib_at = pl.ds(pl.multiple_of((1 - core) * rest, HEAD), rest)

    def run(a, b):
        total = part_sum[...] + nt(b[:, a_at], diag_a[...]) + nt(b[:, b_at], diag_b[...])
        total += nt(cot_own[:, 2 * cols :], direct[:, own_at])
        total += nt(cot_sib[:, 2 * cols :], direct[:, sib_at])
        out[...] = total.astype(BF16)

    by_place(t[0], place[0], cot_own, cot_sib, run)


def project_kernel(
    cap, gone_ref, t_ref, place_ref, att, far_att, weight, first, by_y, by_z, diag_a, diag_b, direct,
    sib_out, own_out, left,
):
    rows, width = att.shape
    blocks = rows // cap - 1
    t, place = t_ref[0], place_ref[0]
    core = t & 1
    y = place & 1
    z = place >> 1
    part = own_out.shape[1]
    cols = first.shape[1]
    wide_a = diag_a.shape[1]
    rest = direct.shape[1] // 2
    swap = gone_ref[0] < blocks
    last = (blocks - 1) * cap
    for i, src in enumerate((att, far_att)):
        where = slice(i * width, (i + 1) * width)
        left[:last, where] = src[:last]
        home, came = src[last : rows - cap, :], src[rows - cap :, :]
        left[last : rows - cap, where] = jnp.where(swap, came, home)
        left[rows - cap :, where] = jnp.where(swap, home, came)

    def put(out, k, at, size, far_weight):
        start = pl.multiple_of((t >> 1) * 2 * part + k * part + at, HEAD)
        both = jnp.concatenate([weight[:, pl.ds(start, size)], far_weight], axis=0)
        term = nn(left[...], both)
        out[:, pl.ds(pl.multiple_of(at, HEAD), size)] = term.astype(BF16)

    def run(a, b):
        put(a, z, y * cols, cols, first[...])
        put(a, z, (1 - y) * cols, cols, by_y[...])
        put(b, 1 - z, y * cols, cols, by_z[...])
        put(b, 1 - z, (1 - y) * cols, wide_a, diag_a[...])
        put(b, 1 - z, (1 - y) * cols + wide_a, cols - wide_a, diag_b[...])

    by_place(t, place, own_out, sib_out, run)
    for out, k in ((sib_out, 1 - core), (own_out, core)):
        at = pl.ds(pl.multiple_of(k * rest, HEAD), rest)
        put(out, k, 2 * cols, rest, direct[:, at])


def backward_kernel(q, k, v, pt, near, far, gq, gk, gv):
    for h in range(q.shape[1] // HEAD):
        cols = slice(h * HEAD, (h + 1) * HEAD)
        cot = (near[:, cols] + far[:, cols].astype(F32)).astype(BF16)
        weights = pt[h]
        gv[:, cols] = nn(weights, cot).astype(BF16)
        rise = nt(v[:, cols], cot)
        wide = weights.astype(F32)
        mean = jnp.sum(wide * rise, axis=0, keepdims=True)
        slope = (wide * (rise - mean) * HEAD ** (-0.5)).astype(BF16)
        gk[:, cols] = nn(slope, q[:, cols]).astype(BF16)
        gq[:, cols] = tn(slope, k[:, cols]).astype(BF16)


def flip(values, axis, by):
    size = lax.axis_size(axis)
    return lax.ppermute(values, axis, [(i, i ^ by) for i in range(size)])


def shifted(values, axis, by):
    size = lax.axis_size(axis)
    return lax.ppermute(values, axis, [(i, (i + by) % size) for i in range(size)])


def tie(value, *others):
    return lax.optimization_barrier((value, *others))[0]


def shards(queries, key_rows, value_rows, out_weight, segment_ids, move_flags, out_cotangent):
    home, width = queries.shape
    dest, part = out_cotangent.shape
    cap = dest - home
    blocks = home // cap
    heads = width // HEAD
    cols = part * 5 // 12 // HEAD * HEAD
    rest = part - 2 * cols
    wide_a = (cols + HEAD) // 2 // HEAD * HEAD
    t = lax.axis_index("tensor").astype(jnp.int32).reshape(1)
    place = (lax.axis_index("dp").astype(jnp.int32) & 3).reshape(1)

    gone, share, direct, picked = call(
        functools.partial(open_kernel, cap, blocks),
        [
            ((1,), jnp.int32),
            ((width, cols), BF16),
            ((width, 2 * rest), BF16),
            ((cap, part), BF16),
        ],
        [SMEM, SMEM, SMEM, SMEM, ANY, ANY],
        [pltpu.SemaphoreType.DMA((4,))],
        limit=OPEN_LIMIT,
    )(segment_ids, move_flags, t, place, out_weight, out_cotangent)
    first = flip(share, "tensor", 2)
    cot_raw = flip(out_cotangent, "tensor", 1)
    back = shifted(picked, "dp", -1)

    att, sent, pt = call(
        functools.partial(forward_kernel, cap),
        [((dest, width), BF16), ((cap, width), BF16), ((heads, home, home), BF16)],
        [SMEM, SMEM, VMEM, VMEM, VMEM],
        [pltpu.VMEM((blocks + 1, cap, width), BF16)],
    )(segment_ids, gone, queries, key_rows, value_rows)
    came = shifted(sent, "dp", 1)
    back_sib = flip(tie(back, sent), "tensor", 1)

    first, back_sib, cot_raw, sent = lax.optimization_barrier((first, back_sib, cot_raw, sent))
    by_y = flip(first, "dp", 1)
    by_z = flip(first, "dp", 2)
    direct = flip(tie(direct, first), "tensor", 2)

    cot_own, cot_sib = call(
        functools.partial(home_kernel, cap, blocks),
        [((home, part), BF16)] * 2,
        [SMEM] + [VMEM] * 4,
    )(gone, out_cotangent, cot_raw, back, back_sib)

    near = call(
        own_kernel,
        [((home, width), F32)],
        [SMEM, VMEM, VMEM, VMEM],
        flops=4 * home * width * part,
        moved=(home + width) * part * 4,
    )(t, cot_own, cot_sib, out_weight)[0]

    by_y, by_z, near = lax.optimization_barrier((by_y, by_z, near))
    cut_a, cut_b = lax.optimization_barrier((by_y[:, :wide_a], by_z[:, wide_a:]))
    diag_a = flip(cut_a, "dp", 2)
    diag_b = flip(cut_b, "dp", 1)

    att = lax.dynamic_update_slice(att, came, (home, 0))
    far_att = flip(att, "tensor", 2)

    half = call(
        far_kernel,
        [((home, width), F32)],
        [SMEM, SMEM] + [VMEM] * 5,
        flops=6 * home * width * cols,
        moved=(home + width) * cols * 6,
    )(t, place, cot_own, cot_sib, first, by_y, by_z)[0]
    send = call(
        last_kernel,
        [((home, width), BF16)],
        [SMEM, SMEM] + [VMEM] * 6,
        flops=2 * home * width * (cols + 2 * rest),
        moved=(home + width) * (cols + 2 * rest) * 2,
    )(t, place, cot_own, cot_sib, half, diag_a, diag_b, direct)[0]
    far = flip(send, "tensor", 2)

    sib_part, own_part = call(
        functools.partial(project_kernel, cap),
        [((dest, part), BF16), ((dest, part), BF16)],
        [SMEM] * 3 + [VMEM] * 9,
        [pltpu.VMEM((dest, 2 * width), BF16)],
        flops=8 * dest * width * part,
        moved=8 * width * part + dest * part * 4,
    )(gone, t, tie(place, send), att, far_att, out_weight, first, by_y, by_z, diag_a, diag_b, direct)
    other = flip(sib_part, "tensor", 1)
    projected = (own_part.astype(F32) + other.astype(F32)).astype(BF16)

    grad_q, grad_k, grad_v = call(
        backward_kernel,
        [((home, width), BF16)] * 3,
        [VMEM] * 6,
        flops=3200 * home * home * width,
        moved=9 * home * width * 2,
    )(queries, key_rows, value_rows, pt, near, far)
    return (projected, grad_q, grad_k, grad_v)


def wide_shards(queries, key_rows, value_rows, out_weight, segment_ids, move_flags, out_cotangent):
    home, width = queries.shape
    dest, part = out_cotangent.shape
    cap = dest - home
    blocks = home // cap
    heads = width // HEAD
    gone, picked = call(
        functools.partial(pick_kernel, cap, blocks),
        [((1,), jnp.int32), ((cap, part), BF16)],
        [SMEM, SMEM, VMEM],
    )(segment_ids, move_flags, out_cotangent)
    att, sent, pt = call(
        functools.partial(forward_kernel, cap),
        [((dest, width), BF16), ((cap, width), BF16), ((heads, home, home), BF16)],
        [SMEM, SMEM, VMEM, VMEM, VMEM],
        [pltpu.VMEM((blocks + 1, cap, width), BF16)],
    )(segment_ids, gone, queries, key_rows, value_rows)
    came = shifted(sent, "dp", 1)
    kept = jnp.where(gone[0] < blocks, home - cap, home)
    att = lax.dynamic_update_slice(att, came, (kept, 0))
    term = jnp.dot(att, out_weight, preferred_element_type=F32).astype(BF16)
    projected = lax.psum_scatter(term, "tensor", scatter_dimension=1, tiled=True)
    back = shifted(picked, "dp", -1)
    cot = call(
        functools.partial(home_kernel, cap, blocks),
        [((home, part), BF16)],
        [SMEM, VMEM, VMEM],
    )(gone, out_cotangent, back)[0]
    whole = lax.all_gather(cot, "tensor", axis=1, tiled=True)
    near = nt(whole, out_weight)
    grad_q, grad_k, grad_v = call(
        backward_kernel, [((home, width), BF16)] * 3, [VMEM] * 6
    )(queries, key_rows, value_rows, pt, near, jnp.zeros((home, width), BF16))
    return (projected, grad_q, grad_k, grad_v)


def solution(mesh):
    square = mesh.shape["tensor"] == 4 and mesh.shape["dp"] % 4 == 0
    in_specs = (
        P("dp", "tensor"),
        P("dp", "tensor"),
        P("dp", "tensor"),
        P("tensor", None),
        P("dp", None),
        P("dp", None),
        P("dp", "tensor"),
    )
    out_specs = (P("dp", "tensor"), P("dp", "tensor"), P("dp", "tensor"), P("dp", "tensor"))
    return jax.shard_map(
        shards if square else wide_shards,
        mesh=mesh,
        in_specs=in_specs,
        out_specs=out_specs,
        check_vma=False,
    )
```

time: 64.9 us -> 56.6 us (0.87)
  waiting for transfers between devices: 26.2 us -> 16.6 us
  Pallas kernels: 20.3 us -> 17 us
  starting transfers between devices: 13.5 us -> 16.8 us
  other arithmetic: 1.49 us -> 2.75 us
    ppermute x2, waiting for transfers between devices: 10.9 us -> 3.38 us  [shifted(): lax.ppermute(values, axis, [(i, (i + by) % size) for i in range(size)])]
    pallas_call x7 -> x8, Pallas kernels: 20.3 us -> 17 us  [the longest x1 4.64 us: shards(): call(functools.partial(project_kernel, cap), [((dest, part), BF16), ((des...]
    ppermute x2, starting transfers between devices: 2.37 us -> 5.06 us  [shifted(): lax.ppermute(values, axis, [(i, (i + by) % size) for i in range(size)])]
    unnamed x12 -> x16, local copies, waits for them, and re-layouts: 0.03 us -> 2.37 us
    dynamic_slice x2 -> x0, local copies, waits for them, and re-layouts: 2.3 us -> none  [the longest x1 1.19 us: shards(): lax.dynamic_slice(out_weight, (0, far_side + place * cols), (shared, cols))]
    ppermute x10 -> x11, waiting for transfers between devices: 15.3 us -> 13.2 us  [flip(): return lax.ppermute(values, axis, [(i, i ^ by) for i in range(size)])]
    convert_element_type x1, other arithmetic: 1.41 us -> 2.75 us  [shards(): projected = (own_part.astype(F32) + other.astype(F32)).astype(BF16)]
    ppermute x10 -> x11, starting transfers between devices: 11.1 us -> 11.8 us  [flip(): return lax.ppermute(values, axis, [(i, i ^ by) for i in range(size)])]
  transfers between devices with their start and end apart: 12 -> 13, of which waited for: 4 -> 9; matrix products, arithmetic and copies ran while one was open for 2% -> 0% of each run, Pallas kernels for 31% -> 30%
where the time goes in v2:
time: 56.6 us; the launch traced here: 56.4 us
  Pallas kernels  17 us (30%)
  starting transfers between devices  16.8 us (30%)
  waiting for transfers between devices  16.6 us (29%)
  other arithmetic  2.75 us (5%)
  local copies, waits for them, and re-layouts  2.42 us (4%)
  between operations  0.75 us (1%)
    ppermute x11, waiting for transfers between devices, flip(): return lax.ppermute(values, axis, [(i, i ^ by) for i in range(size)])  13.2 us
    ppermute x11, starting transfers between devices, flip(): return lax.ppermute(values, axis, [(i, i ^ by) for i in range(size)])  11.8 us
    ppermute x2, starting transfers between devices, shifted(): lax.ppermute(values, axis, [(i, (i + by) % size) for i in range(size)])  5.06 us
    pallas_call x1, Pallas kernels, shards(): call(functools.partial(project_kernel, cap), [((dest, part), BF16), ((des...  4.64 us
    ppermute x2, waiting for transfers between devices, shifted(): lax.ppermute(values, axis, [(i, (i + by) % size) for i in range(size)])  3.38 us
    pallas_call x1, Pallas kernels, shards(): call(functools.partial(open_kernel, cap, blocks), [((1,), jnp.int32), ((w...  3.1 us
    pallas_call x1, Pallas kernels, shards(): call(functools.partial(forward_kernel, cap), [((dest, width), BF16), ((ca...  2.85 us
    convert_element_type x1, other arithmetic, shards(): projected = (own_part.astype(F32) + other.astype(F32)).astype(BF16)  2.75 us
  transfers between devices with their start and end apart: 13, of which 9 were waited for; matrix products, arithmetic and copies ran while one was open for 0% of the time, Pallas kernels for 30%

profile of v2, /device:TPU:0, one launch (start us, length us, event | category | flops | bytes accessed | tf_op | source)
XLA Modules:
  0.0 56.4 jit_solution(15971540305546073766)
XLA Ops:
  0.6 0.5 collective-permute-start.3
  1.2 0.0 copy-start.2
  1.2 0.0 copy-start.3
  1.2 0.0 copy-start.4
  1.2 0.0 copy-start.5
  1.2 0.0 copy-start.1
  1.2 3.1 %shard_map.102 = (s32[1]{0:T(128)}, bf16[384,640]{1,0:T(8,128)(2,1)}, bf16[384,512]{1,0:T(8,128)(2,1)}, bf16[64,1536]{1,0:T(8,128)(2,1)}) custom-call(s32[1,384]{1,0:T(1,128)} %seg.3, s32[1,384]{1,0:T(1,128)} %flags.1, s32[1]{0:T(128)} %bitcast.t.t_ref, s32[1]{0:T(128)} %bitcast.1.place.place_ref, bf16[384,6144]{1,0:T(8,128)(2,1)} %weight.5, ...), custom_call_target="tpu_custom_call" | custom-call | tf_op jit(solution)/shard_map/pallas_call | solution.py:270
  4.3 2.6 %collective-permute-start = (bf16[384,640]{1,0:T(8,128)(2,1)}, bf16[384,640]{1,0:T(8,128)(2,1)S(1)}, u32[]{:S(2)}, u32[]{:S(2)}) collective-permute-start(bf16[384,640]{1,0:T(8,128)(2,1)} %get-tuple-element.30), channel_id=1, source_target_pairs={{0,2},{1,3},{2,0},{3,1},{4,6},{5,7},{6,4},{7,5},{8,10},{9,11},{10,... | collective-permute-start | bytes 1474568 | tf_op jit(solution)/shard_map/ppermute | solution.py:246
  6.9 4.6 %collective-permute-start.1 = (bf16[64,1536]{1,0:T(8,128)(2,1)}, bf16[64,1536]{1,0:T(8,128)(2,1)S(1)}, u32[]{:S(2)}, u32[]{:S(2)}) collective-permute-start(bf16[64,1536]{1,0:T(8,128)(2,1)} %get-tuple-element.31), channel_id=1, source_target_pairs={{0,28},{4,0},{8,4},{12,8},{16,12},{20,16},{24,20},{28,24},{1,29},{... | collective-permute-start | bytes 589832 | tf_op jit(solution)/shard_map/ppermute | solution.py:251
  11.4 0.0 copy-done.2
  11.4 0.0 copy-done.3
  11.4 0.0 copy-done.4
  11.4 0.0 copy-done.5
  11.4 2.8 %shard_map.103 = (bf16[448,384]{1,0:T(8,128)(2,1)S(1)}, bf16[64,384]{1,0:T(8,128)(2,1)S(1)}, bf16[3,384,384]{2,1,0:T(8,128)(2,1)S(1)}) custom-call(s32[1,384]{1,0:T(1,128)S(1)} %copy-done.5, s32[1]{0:T(128)} %get-tuple-element.29.gone_ref, bf16[384,384]{1,0:T(8,128)(2,1)S(1)} %copy-done.2, bf16[384,384]{1,0:T(8,128)(2,1)S(1)} %copy-done.3, ...), custom_call_target="tpu_custom_call" | custom-call | tf_op jit(solution)/shard_map/pallas_call | solution.py:286
  14.3 2.0 %collective-permute-done.1.refs_2_ = bf16[64,1536]{1,0:T(8,128)(2,1)S(1)} collective-permute-done((bf16[64,1536]{1,0:T(8,128)(2,1)}, bf16[64,1536]{1,0:T(8,128)(2,1)S(1)}, u32[]{:S(2)}, u32[]{:S(2)}) %collective-permute-start.1) | collective-permute-done | bytes 196640 | tf_op jit(solution)/shard_map/ppermute | solution.py:251
  16.3 0.0 collective-permute-start.2
  16.3 1.4 %collective-permute-done.2.refs_3_ = bf16[64,1536]{1,0:T(8,128)(2,1)S(1)} collective-permute-done((bf16[64,1536]{1,0:T(8,128)(2,1)S(1)}, bf16[64,1536]{1,0:T(8,128)(2,1)S(1)}, u32[]{:S(2)}, u32[]{:S(2)}) %collective-permute-start.2) | collective-permute-done | bytes 196640 | tf_op jit(solution)/shard_map/ppermute | solution.py:246
  17.7 1.2 %collective-permute-done.first = bf16[384,640]{1,0:T(8,128)(2,1)S(1)} collective-permute-done((bf16[384,640]{1,0:T(8,128)(2,1)}, bf16[384,640]{1,0:T(8,128)(2,1)S(1)}, u32[]{:S(2)}, u32[]{:S(2)}) %collective-permute-start) | collective-permute-done | bytes 491552 | tf_op jit(solution)/shard_map/ppermute | solution.py:246
  18.9 0.0 collective-permute-done.3.refs_1_
  18.9 1.8 %collective-permute-start.4 = (bf16[384,640]{1,0:T(8,128)(2,1)S(1)}, bf16[384,640]{1,0:T(8,128)(2,1)S(1)}, u32[]{:S(2)}, u32[]{:S(2)}) collective-permute-start(bf16[384,640]{1,0:T(8,128)(2,1)S(1)} %collective-permute-done.first), channel_id=1, source_target_pairs={{0,4},{4,0},{8,12},{12,8},{16,20},{20,16},{24,28},{28,24},{1,5},{5... | collective-permute-start | bytes 1474568 | tf_op jit(solution)/shard_map/ppermute | solution.py:246
  20.7 1.6 %collective-permute-start.5 = (bf16[384,640]{1,0:T(8,128)(2,1)S(1)}, bf16[384,640]{1,0:T(8,128)(2,1)S(1)}, u32[]{:S(2)}, u32[]{:S(2)}) collective-permute-start(bf16[384,640]{1,0:T(8,128)(2,1)S(1)} %collective-permute-done.first), channel_id=1, source_target_pairs={{0,8},{4,12},{8,0},{12,4},{16,24},{20,28},{24,16},{28,20},{1,9},{5... | collective-permute-start | bytes 1474568 | tf_op jit(solution)/shard_map/ppermute | solution.py:246
  22.3 0.5 collective-permute-start.9
  22.8 1.5 %collective-permute-start.8 = (bf16[384,512]{1,0:T(8,128)(2,1)}, bf16[384,512]{1,0:T(8,128)(2,1)S(1)}, u32[]{:S(2)}, u32[]{:S(2)}) collective-permute-start(bf16[384,512]{1,0:T(8,128)(2,1)} %get-tuple-element.44), channel_id=1, source_target_pairs={{0,2},{1,3},{2,0},{3,1},{4,6},{5,7},{6,4},{7,5},{8,10},{9,11},{10,... | collective-permute-start | bytes 1179656 | tf_op jit(solution)/shard_map/ppermute | solution.py:246
  24.3 0.0 copy-done.1
  24.3 0.8 %shard_map.104 = (bf16[384,1536]{1,0:T(8,128)(2,1)S(1)}, bf16[384,1536]{1,0:T(8,128)(2,1)S(1)}) custom-call(s32[1]{0:T(128)} %get-tuple-element.29.gone_ref, bf16[448,1536]{1,0:T(8,128)(2,1)S(1)} %copy-done.1, bf16[448,1536]{1,0:T(8,128)(2,1)S(1)} %collective-permute-done.3.refs_1_, bf16[64,1536]{1,0:T(8,128)(2,1)S(1)} %collective-permute-done.1.refs_2_, ...), custom_call_target="tpu_custom_call" | custom-call | tf_op jit(solution)/shard_map/pallas_call | solution.py:300
  25.1 0.0 copy-start
  25.1 2.3 %copy-done = bf16[384,6144]{1,0:T(8,128)(2,1)S(1)} copy-done((bf16[384,6144]{1,0:T(8,128)(2,1)S(1)}, bf16[384,6144]{1,0:T(8,128)(2,1)}, u32[]{:S(2)}) %copy-start) | copy-done | bytes 4718616
  27.5 1.4 %shard_map.105.near = f32[384,384]{1,0:T(8,128)S(1)} custom-call(s32[1]{0:T(128)} %bitcast.t.t_ref, bf16[384,1536]{1,0:T(8,128)(2,1)S(1)} %get-tuple-element.36.cot_own, bf16[384,1536]{1,0:T(8,128)(2,1)S(1)} %get-tuple-element.37.cot_sib, bf16[384,6144]{1,0:T(8,128)(2,1)S(1)} %copy-done), custom_call_target="tpu_custom_call" | custom-call | flops 905969664 | bytes 4718592 | tf_op jit(solution)/shard_map/pallas_call | solution.py:306
  28.9 3.1 %collective-permute-done.4.by_y = bf16[384,640]{1,0:T(8,128)(2,1)S(1)} collective-permute-done((bf16[384,640]{1,0:T(8,128)(2,1)S(1)}, bf16[384,640]{1,0:T(8,128)(2,1)S(1)}, u32[]{:S(2)}, u32[]{:S(2)}) %collective-permute-start.4) | collective-permute-done | bytes 491552 | tf_op jit(solution)/shard_map/ppermute | solution.py:246
  32.0 1.3 %collective-permute-done.5.by_z = bf16[384,640]{1,0:T(8,128)(2,1)S(1)} collective-permute-done((bf16[384,640]{1,0:T(8,128)(2,1)S(1)}, bf16[384,640]{1,0:T(8,128)(2,1)S(1)}, u32[]{:S(2)}, u32[]{:S(2)}) %collective-permute-start.5) | collective-permute-done | bytes 491552 | tf_op jit(solution)/shard_map/ppermute | solution.py:246
  33.3 0.0 slice-start
  33.3 1.6 %collective-permute-start.6 = (bf16[384,384]{1,0:T(8,128)(2,1)S(1)}, bf16[384,384]{1,0:T(8,128)(2,1)S(1)}, u32[]{:S(2)}, u32[]{:S(2)}) collective-permute-start(bf16[384,384]{1,0:T(8,128)(2,1)S(1)} %slice.6), channel_id=1, source_target_pairs={{0,8},{4,12},{8,0},{12,4},{16,24},{20,28},{24,16},{28,20},{1,9},{5... | collective-permute-start | bytes 884744 | tf_op jit(solution)/shard_map/ppermute | solution.py:246
  34.9 1.4 %collective-permute-done.9 = bf16[64,384]{1,0:T(8,128)(2,1)S(1)} collective-permute-done((bf16[64,384]{1,0:T(8,128)(2,1)S(1)}, bf16[64,384]{1,0:T(8,128)(2,1)S(1)}, u32[]{:S(2)}, u32[]{:S(2)}) %collective-permute-start.9) | collective-permute-done | bytes 49184 | tf_op jit(solution)/shard_map/ppermute | solution.py:251
  36.4 0.0 slice-start.1
  36.4 1.6 %collective-permute-start.10 = (bf16[448,384]{1,0:T(8,128)(2,1)S(1)}, bf16[448,384]{1,0:T(8,128)(2,1)S(1)}, u32[]{:S(2)}, u32[]{:S(2)}) collective-permute-start(bf16[448,384]{1,0:T(8,128)(2,1)S(1)} %constant_dynamic-update-slice_fusion.att), channel_id=1, source_target_pairs={{0,2},{1,3},{2,0},{3,1},{4,6},{5,7},{6,4},{7,5},{8,10},{9,11},{10,... | collective-permute-start | bytes 1032200 | tf_op jit(solution)/shard_map/ppermute | solution.py:246
  37.9 0.0 collective-permute-start.7
  38.0 1.0 %shard_map.106.part_sum = f32[384,384]{1,0:T(8,128)S(1)} custom-call(s32[1]{0:T(128)} %bitcast.t.t_ref, s32[1]{0:T(128)} %bitcast.1.place.place_ref, bf16[384,1536]{1,0:T(8,128)(2,1)S(1)} %get-tuple-element.36.cot_own, bf16[384,1536]{1,0:T(8,128)(2,1)S(1)} %get-tuple-element.37.cot_sib, bf16[384,640]{1,0:T(8,128)(2,1)S(1)} %collective-permute-done.first, ...), custom_call_target="tpu_custom_call" | custom-call | flops 566231040 | bytes 2949120 | tf_op jit(solution)/shard_map/pallas_call | solution.py:322
  39.0 0.0 collective-permute-done.8.direct
  39.0 4.6 %collective-permute-done.7.diag_b = bf16[384,256]{1,0:T(8,128)(2,1)S(1)} collective-permute-done((bf16[384,256]{1,0:T(8,128)(2,1)S(1)}, bf16[384,256]{1,0:T(8,128)(2,1)S(1)}, u32[]{:S(2)}, u32[]{:S(2)}) %collective-permute-start.7) | collective-permute-done | bytes 196640 | tf_op jit(solution)/shard_map/ppermute | solution.py:246
  43.6 0.0 collective-permute-done.6.diag_a
  43.6 0.7 %shard_map.107 = bf16[384,384]{1,0:T(8,128)(2,1)S(1)} custom-call(s32[1]{0:T(128)} %bitcast.t.t_ref, s32[1]{0:T(128)} %bitcast.1.place.place_ref, bf16[384,1536]{1,0:T(8,128)(2,1)S(1)} %get-tuple-element.36.cot_own, bf16[384,1536]{1,0:T(8,128)(2,1)S(1)} %get-tuple-element.37.cot_sib, f32[384,384]{1,0:T(8,128)S(1)} %shard_map.106.part_sum, ...), custom_call_target="tpu_custom_call" | custom-call | flops 339738624 | bytes 1769472 | tf_op jit(solution)/shard_map/pallas_call | solution.py:329
  44.3 0.6 %collective-permute-start.12 = (bf16[384,384]{1,0:T(8,128)(2,1)S(1)}, bf16[384,384]{1,0:T(8,128)(2,1)S(1)}, u32[]{:S(2)}, u32[]{:S(2)}) collective-permute-start(bf16[384,384]{1,0:T(8,128)(2,1)S(1)} %shard_map.107), channel_id=1, source_target_pairs={{0,2},{1,3},{2,0},{3,1},{4,6},{5,7},{6,4},{7,5},{8,10},{9,11},{10,... | collective-permute-start | bytes 884744 | tf_op jit(solution)/shard_map/ppermute | solution.py:246
  44.9 0.1 collective-permute-done.10.far_att
  45.0 0.0 slice-done
  45.0 0.0 slice-done.1
  45.0 4.6 %shard_map.108 = (bf16[448,1536]{1,0:T(8,128)(2,1)}, bf16[448,1536]{1,0:T(8,128)(2,1)S(1)}) custom-call(s32[1]{0:T(128)} %get-tuple-element.29.gone_ref, s32[1]{0:T(128)} %bitcast.t.t_ref, s32[1]{0:T(128)} %bitcast.1.place.place_ref, bf16[448,384]{1,0:T(8,128)(2,1)S(1)} %constant_dynamic-update-slice_fusion.att, ...), custom_call_target="tpu_custom_call" | custom-call | flops 2113929216 | bytes 7471104 | tf_op jit(solution)/shard_map/pallas_call | solution.py:338
  49.7 0.0 collective-permute-start.11
  49.7 1.4 %collective-permute-done.12.far = bf16[384,384]{1,0:T(8,128)(2,1)S(1)} collective-permute-done((bf16[384,384]{1,0:T(8,128)(2,1)S(1)}, bf16[384,384]{1,0:T(8,128)(2,1)S(1)}, u32[]{:S(2)}, u32[]{:S(2)}) %collective-permute-start.12) | collective-permute-done | bytes 294944 | tf_op jit(solution)/shard_map/ppermute | solution.py:246
  51.1 2.5 %shard_map.109 = (bf16[384,384]{1,0:T(8,128)(2,1)}, bf16[384,384]{1,0:T(8,128)(2,1)}, bf16[384,384]{1,0:T(8,128)(2,1)}) custom-call(bf16[384,384]{1,0:T(8,128)(2,1)S(1)} %copy-done.2, bf16[384,384]{1,0:T(8,128)(2,1)S(1)} %copy-done.3, bf16[384,384]{1,0:T(8,128)(2,1)S(1)} %copy-done.4, bf16[3,384,384]{2,1,0:T(8,128)(2,1)S(1)} %get-tuple-element.49.pt, ...), custom_call_target="tpu_custom_call" | custom-call | flops 181193932800 | bytes 2654208 | tf_op jit(solution)/shard_map/pallas_call | solution.py:349
  53.6 0.0 collective-permute-done.11
  53.6 2.7 %add_convert_fusion = bf16[448,1536]{1,0:T(8,128)(2,1)} fusion(bf16[448,1536]{1,0:T(8,128)(2,1)} %collective-permute-done.11, bf16[448,1536]{1,0:T(8,128)(2,1)S(1)} %get-tuple-element.47), kind=kLoop, calls=%fused_computation | loop fusion | flops 2752512 | bytes 4128768 | tf_op jit(solution)/shard_map/convert_element_type | solution.py:347
  (4 shorter events, 0.1 us)
Async XLA Ops:
  0.6 18.3 %collective-permute-start.3 = (bf16[448,1536]{1,0:T(8,128)(2,1)}, bf16[448,1536]{1,0:T(8,128)(2,1)S(1)}, u32[]{:S(2)}, u32[]{:S(2)}) collective-permute-start(bf16[448,1536]{1,0:T(8,128)(2,1)} %refs_0_.1), channel_id=1, source_target_pairs={{0,1},{1,0},{2,3},{3,2},{4,5},{5,4},{6,7},{7,6},{8,9},{9,8},{10,11... | collective-permute-start | bytes 4128776 | tf_op jit(solution)/shard_map/ppermute | solution.py:246
  1.2 10.3 %copy-start.2 = (bf16[384,384]{1,0:T(8,128)(2,1)S(1)}, bf16[384,384]{1,0:T(8,128)(2,1)}, u32[]{:S(2)}) copy-start(bf16[384,384]{1,0:T(8,128)(2,1)} %q.3) | copy-start | bytes 884740
  1.2 10.3 %copy-start.3 = (bf16[384,384]{1,0:T(8,128)(2,1)S(1)}, bf16[384,384]{1,0:T(8,128)(2,1)}, u32[]{:S(2)}) copy-start(bf16[384,384]{1,0:T(8,128)(2,1)} %k.3) | copy-start | bytes 884740
  1.2 10.3 %copy-start.4 = (bf16[384,384]{1,0:T(8,128)(2,1)S(1)}, bf16[384,384]{1,0:T(8,128)(2,1)}, u32[]{:S(2)}) copy-start(bf16[384,384]{1,0:T(8,128)(2,1)} %v.3) | copy-start | bytes 884740
  1.2 10.3 %copy-start.5 = (s32[1,384]{1,0:T(1,128)S(1)}, s32[1,384]{1,0:T(1,128)}, u32[]{:S(2)}) copy-start(s32[1,384]{1,0:T(1,128)} %seg.3) | copy-start | bytes 4612
  1.2 23.1 %copy-start.1 = (bf16[448,1536]{1,0:T(8,128)(2,1)S(1)}, bf16[448,1536]{1,0:T(8,128)(2,1)}, u32[]{:S(2)}) copy-start(bf16[448,1536]{1,0:T(8,128)(2,1)} %refs_0_.1) | copy-start | bytes 4128772
  4.3 14.7 %collective-permute-start = (bf16[384,640]{1,0:T(8,128)(2,1)}, bf16[384,640]{1,0:T(8,128)(2,1)S(1)}, u32[]{:S(2)}, u32[]{:S(2)}) collective-permute-start(bf16[384,640]{1,0:T(8,128)(2,1)} %get-tuple-element.30), channel_id=1, source_target_pairs={{0,2},{1,3},{2,0},{3,1},{4,6},{5,7},{6,4},{7,5},{8,10},{9,11},{10,... | collective-permute-start | bytes 1474568 | tf_op jit(solution)/shard_map/ppermute | solution.py:246
  6.9 9.4 %collective-permute-start.1 = (bf16[64,1536]{1,0:T(8,128)(2,1)}, bf16[64,1536]{1,0:T(8,128)(2,1)S(1)}, u32[]{:S(2)}, u32[]{:S(2)}) collective-permute-start(bf16[64,1536]{1,0:T(8,128)(2,1)} %get-tuple-element.31), channel_id=1, source_target_pairs={{0,28},{4,0},{8,4},{12,8},{16,12},{20,16},{24,20},{28,24},{1,29},{... | collective-permute-start | bytes 589832 | tf_op jit(solution)/shard_map/ppermute | solution.py:251
  16.3 1.4 %collective-permute-start.2 = (bf16[64,1536]{1,0:T(8,128)(2,1)S(1)}, bf16[64,1536]{1,0:T(8,128)(2,1)S(1)}, u32[]{:S(2)}, u32[]{:S(2)}) collective-permute-start(bf16[64,1536]{1,0:T(8,128)(2,1)S(1)} %collective-permute-done.1.refs_2_), channel_id=1, source_target_pairs={{0,1},{1,0},{2,3},{3,2},{4,5},{5,4},{6,7},{7,6},{8,9},{9,8},{10,11... | collective-permute-start | bytes 589832 | tf_op jit(solution)/shard_map/ppermute | solution.py:246
  18.9 13.0 %collective-permute-start.4 = (bf16[384,640]{1,0:T(8,128)(2,1)S(1)}, bf16[384,640]{1,0:T(8,128)(2,1)S(1)}, u32[]{:S(2)}, u32[]{:S(2)}) collective-permute-start(bf16[384,640]{1,0:T(8,128)(2,1)S(1)} %collective-permute-done.first), channel_id=1, source_target_pairs={{0,4},{4,0},{8,12},{12,8},{16,20},{20,16},{24,28},{28,24},{1,5},{5... | collective-permute-start | bytes 1474568 | tf_op jit(solution)/shard_map/ppermute | solution.py:246
  20.7 12.5 %collective-permute-start.5 = (bf16[384,640]{1,0:T(8,128)(2,1)S(1)}, bf16[384,640]{1,0:T(8,128)(2,1)S(1)}, u32[]{:S(2)}, u32[]{:S(2)}) collective-permute-start(bf16[384,640]{1,0:T(8,128)(2,1)S(1)} %collective-permute-done.first), channel_id=1, source_target_pairs={{0,8},{4,12},{8,0},{12,4},{16,24},{20,28},{24,16},{28,20},{1,9},{5... | collective-permute-start | bytes 1474568 | tf_op jit(solution)/shard_map/ppermute | solution.py:246
  22.3 14.1 %collective-permute-start.9 = (bf16[64,384]{1,0:T(8,128)(2,1)S(1)}, bf16[64,384]{1,0:T(8,128)(2,1)S(1)}, u32[]{:S(2)}, u32[]{:S(2)}) collective-permute-start(bf16[64,384]{1,0:T(8,128)(2,1)S(1)} %get-tuple-element.32), channel_id=1, source_target_pairs={{0,4},{4,8},{8,12},{12,16},{16,20},{20,24},{24,28},{28,0},{1,5},{5... | collective-permute-start | bytes 147464 | tf_op jit(solution)/shard_map/ppermute | solution.py:251
  22.8 16.2 %collective-permute-start.8 = (bf16[384,512]{1,0:T(8,128)(2,1)}, bf16[384,512]{1,0:T(8,128)(2,1)S(1)}, u32[]{:S(2)}, u32[]{:S(2)}) collective-permute-start(bf16[384,512]{1,0:T(8,128)(2,1)} %get-tuple-element.44), channel_id=1, source_target_pairs={{0,2},{1,3},{2,0},{3,1},{4,6},{5,7},{6,4},{7,5},{8,10},{9,11},{10,... | collective-permute-start | bytes 1179656 | tf_op jit(solution)/shard_map/ppermute | solution.py:246
  25.1 2.3 %copy-start = (bf16[384,6144]{1,0:T(8,128)(2,1)S(1)}, bf16[384,6144]{1,0:T(8,128)(2,1)}, u32[]{:S(2)}) copy-start(bf16[384,6144]{1,0:T(8,128)(2,1)} %weight.5) | copy-start | bytes 14155780
  33.3 11.8 %slice-start = ((s8[4718592]{0:T(1024)(128)(4,1)}), s8[4194304]{0:T(1024)(128)(4,1)S(1)}, s32[]{:S(2)}) async-start(s8[4718592]{0:T(1024)(128)(4,1)} %bitcast.2), calls=%async_computation | async-start | bytes 8388608
  33.3 10.3 %collective-permute-start.6 = (bf16[384,384]{1,0:T(8,128)(2,1)S(1)}, bf16[384,384]{1,0:T(8,128)(2,1)S(1)}, u32[]{:S(2)}, u32[]{:S(2)}) collective-permute-start(bf16[384,384]{1,0:T(8,128)(2,1)S(1)} %slice.6), channel_id=1, source_target_pairs={{0,8},{4,12},{8,0},{12,4},{16,24},{20,28},{24,16},{28,20},{1,9},{5... | collective-permute-start | bytes 884744 | tf_op jit(solution)/shard_map/ppermute | solution.py:246
  36.4 8.7 %slice-start.1 = ((s8[4718592]{0:T(1024)(128)(4,1)}), s8[524288]{0:T(1024)(128)(4,1)S(1)}, s32[]{:S(2)}) async-start(s8[4718592]{0:T(1024)(128)(4,1)} %bitcast.2), calls=%async_computation.1 | async-start | bytes 1048576
  36.4 8.6 %collective-permute-start.10 = (bf16[448,384]{1,0:T(8,128)(2,1)S(1)}, bf16[448,384]{1,0:T(8,128)(2,1)S(1)}, u32[]{:S(2)}, u32[]{:S(2)}) collective-permute-start(bf16[448,384]{1,0:T(8,128)(2,1)S(1)} %constant_dynamic-update-slice_fusion.att), channel_id=1, source_target_pairs={{0,2},{1,3},{2,0},{3,1},{4,6},{5,7},{6,4},{7,5},{8,10},{9,11},{10,... | collective-permute-start | bytes 1032200 | tf_op jit(solution)/shard_map/ppermute | solution.py:246
  37.9 5.7 %collective-permute-start.7 = (bf16[384,256]{1,0:T(8,128)(2,1)S(1)}, bf16[384,256]{1,0:T(8,128)(2,1)S(1)}, u32[]{:S(2)}, u32[]{:S(2)}) collective-permute-start(bf16[384,256]{1,0:T(8,128)(2,1)S(1)} %slice.7), channel_id=1, source_target_pairs={{0,4},{4,0},{8,12},{12,8},{16,20},{20,16},{24,28},{28,24},{1,5},{5... | collective-permute-start | bytes 589832 | tf_op jit(solution)/shard_map/ppermute | solution.py:246
  44.3 6.8 %collective-permute-start.12 = (bf16[384,384]{1,0:T(8,128)(2,1)S(1)}, bf16[384,384]{1,0:T(8,128)(2,1)S(1)}, u32[]{:S(2)}, u32[]{:S(2)}) collective-permute-start(bf16[384,384]{1,0:T(8,128)(2,1)S(1)} %shard_map.107), channel_id=1, source_target_pairs={{0,2},{1,3},{2,0},{3,1},{4,6},{5,7},{6,4},{7,5},{8,10},{9,11},{10,... | collective-permute-start | bytes 884744 | tf_op jit(solution)/shard_map/ppermute | solution.py:246
  49.7 3.9 %collective-permute-start.11 = (bf16[448,1536]{1,0:T(8,128)(2,1)}, bf16[448,1536]{1,0:T(8,128)(2,1)}, u32[]{:S(2)}, u32[]{:S(2)}) collective-permute-start(bf16[448,1536]{1,0:T(8,128)(2,1)} %get-tuple-element.48), channel_id=1, source_target_pairs={{0,1},{1,0},{2,3},{3,2},{4,5},{5,4},{6,7},{7,6},{8,9},{9,8},{10,11... | collective-permute-start | bytes 4128776 | tf_op jit(solution)/shard_map/ppermute | solution.py:246

commit v3 on v2

--- a/solution.py
+++ b/solution.py
@@ -14,7 +14,7 @@
 SMEM = pl.BlockSpec(memory_space=pltpu.SMEM)
 ANY = pl.BlockSpec(memory_space=pl.ANY)
 LIMIT = 16 * 1024 * 1024
-OPEN_LIMIT = 60 * 1024 * 1024
+OPEN_LIMIT = 52 * 1024 * 1024
 
 
 def nt(a, b):
@@ -48,10 +48,31 @@
     return out
 
 
-def forward_kernel(cap, seg, gone_ref, q, k, v, att, sent, pt, rows_buf):
+def attend(segment_ids, move_flags, queries, key_rows, value_rows, out_cotangent):
+    home, width = queries.shape
+    dest, part = out_cotangent.shape
+    cap = dest - home
+    return call(
+        functools.partial(forward_kernel, cap),
+        [
+            ((1,), jnp.int32),
+            ((cap, part), BF16),
+            ((dest, width), BF16),
+            ((cap, width), BF16),
+            ((width // HEAD, home, home), BF16),
+        ],
+        [SMEM, SMEM] + [VMEM] * 4,
+        [pltpu.VMEM((home // cap + 1, cap, width), BF16)],
+    )(segment_ids, move_flags, queries, key_rows, value_rows, out_cotangent)
+
+
+def forward_kernel(cap, seg, flags, q, k, v, cot, gone_out, picked, att, sent, pt, rows_buf):
     rows, width = q.shape
     blocks = rows // cap
-    gone = gone_ref[0]
+    gone = moved_block(seg, flags, blocks, cap)
+    gone_out[0] = gone
+    row = jnp.where(gone == blocks, blocks, blocks - 1)
+    picked[...] = cot[pl.ds(pl.multiple_of(row * cap, cap), cap), :]
     col_block = lax.broadcasted_iota(jnp.int32, (rows, 1), 0) // cap
     row_block = lax.broadcasted_iota(jnp.int32, (1, rows), 1) // cap
     key_id = jnp.zeros((rows, 1), jnp.int32)
@@ -81,40 +102,25 @@
     sent[...] = rows_buf[blocks]
 
 
-def open_kernel(
-    cap, blocks, seg, flags, t, place, weight, cot, gone_out, share_out, direct_out, picked_out, sems
-):
-    cols = share_out.shape[1]
-    rest = direct_out.shape[1] // 2
-    part = cot.shape[1]
+def share_kernel(part, cols, t, place, weight, *refs):
+    outs, direct, sems = refs[:-2], refs[-2], refs[-1]
+    rest = direct.shape[1] // 2
     far = (1 - (t[0] >> 1)) * 2 * part
-    start = pl.multiple_of(far + (place[0] >> 1) * part + (place[0] & 1) * cols, HEAD)
-    copies = [pltpu.make_async_copy(weight.at[:, pl.ds(start, cols)], share_out, sems.at[0])]
+    at = far + (place[0] >> 1) * part + (place[0] & 1) * cols
+    moves = []
+    for out in outs:
+        moves.append((at, out))
+        at += out.shape[1]
     for k in range(2):
-        start = pl.multiple_of(far + k * part + 2 * cols, HEAD)
-        copies.append(
-            pltpu.make_async_copy(
-                weight.at[:, pl.ds(start, rest)],
-                direct_out.at[:, pl.ds(k * rest, rest)],
-                sems.at[1 + k],
-            )
-        )
+        moves.append((far + (k + 1) * part - rest, direct.at[:, pl.ds(k * rest, rest)]))
+    copies = []
+    for i, (start, out) in enumerate(moves):
+        where = pl.ds(pl.multiple_of(start, HEAD), out.shape[1])
+        copies.append(pltpu.make_async_copy(weight.at[:, where], out, sems.at[i]))
     for c in copies:
         c.start()
-    gone = moved_block(seg, flags, blocks, cap)
-    gone_out[0] = gone
-    row = pl.multiple_of(jnp.where(gone == blocks, blocks, blocks - 1) * cap, cap)
-    copies.append(pltpu.make_async_copy(cot.at[pl.ds(row, cap), :], picked_out, sems.at[3]))
-    copies[-1].start()
     for c in copies:
         c.wait()
-
-
-def pick_kernel(cap, blocks, seg, flags, cot, gone_out, picked_out):
-    gone = moved_block(seg, flags, blocks, cap)
-    gone_out[0] = gone
-    row = jnp.where(gone == blocks, blocks, blocks - 1)
-    picked_out[...] = cot[pl.ds(pl.multiple_of(row * cap, cap), cap), :]
 
 
 def home_kernel(cap, blocks, gone_ref, *refs):
@@ -149,18 +155,24 @@
     pl.when(jnp.logical_not(same))(lambda: run(sib, own))
 
 
-def far_kernel(t, place, cot_own, cot_sib, first, by_y, by_z, out):
-    cols = first.shape[1]
+def far_kernel(t, place, cot_own, cot_sib, *refs):
+    out, chunks = refs[-1], refs[:-1]
+    chunks = [chunks[i : i + 3] for i in range(0, len(chunks), 3)]
+    cols = sum(c[0].shape[1] for c in chunks)
     y = place[0] & 1
-    near_at = pl.ds(pl.multiple_of(y * cols, HEAD), cols)
-    next_at = pl.ds(pl.multiple_of((1 - y) * cols, HEAD), cols)
 
     def run(a, b):
-        out[...] = (
-            nt(a[:, near_at], first[...])
-            + nt(a[:, next_at], by_y[...])
-            + nt(b[:, near_at], by_z[...])
-        )
+        total = None
+        at = 0
+        for mine, by_y, by_z in chunks:
+            size = mine.shape[1]
+            near_at = pl.ds(pl.multiple_of(y * cols + at, HEAD), size)
+            next_at = pl.ds(pl.multiple_of((1 - y) * cols + at, HEAD), size)
+            term = nt(a[:, near_at], mine[...]) + nt(a[:, next_at], by_y[...])
+            term += nt(b[:, near_at], by_z[...])
+            total = term if total is None else total + term
+            at += size
+        out[...] = total
 
     by_place(t[0], place[0], cot_own, cot_sib, run)
 
@@ -185,22 +197,10 @@
     by_place(t[0], place[0], cot_own, cot_sib, run)
 
 
-def project_kernel(
-    cap, gone_ref, t_ref, place_ref, att, far_att, weight, first, by_y, by_z, diag_a, diag_b, direct,
-    sib_out, own_out, left,
-):
+def fill_left(cap, gone, att, far_att, left):
     rows, width = att.shape
-    blocks = rows // cap - 1
-    t, place = t_ref[0], place_ref[0]
-    core = t & 1
-    y = place & 1
-    z = place >> 1
-    part = own_out.shape[1]
-    cols = first.shape[1]
-    wide_a = diag_a.shape[1]
-    rest = direct.shape[1] // 2
-    swap = gone_ref[0] < blocks
-    last = (blocks - 1) * cap
+    last = rows - 2 * cap
+    swap = gone * cap < rows - cap
     for i, src in enumerate((att, far_att)):
         where = slice(i * width, (i + 1) * width)
         left[:last, where] = src[:last]
@@ -208,23 +208,77 @@
         left[last : rows - cap, where] = jnp.where(swap, came, home)
         left[rows - cap :, where] = jnp.where(swap, home, came)
 
-    def put(out, k, at, size, far_weight):
-        start = pl.multiple_of((t >> 1) * 2 * part + k * part + at, HEAD)
+
+def early_kernel(cap, part, gone, t_ref, place_ref, att, far_att, weight, *refs):
+    own_out, sib_out, left = refs[-3:]
+    chunks = [refs[i : i + 3] for i in range(0, len(refs) - 3, 3)]
+    t, place = t_ref[0], place_ref[0]
+    y, z = place & 1, place >> 1
+    cols = own_out.shape[1] // 2
+    fill_left(cap, gone[0], att, far_att, left)
+
+    def run(a, b):
+        at = 0
+        for mine, by_y, by_z in chunks:
+            size = mine.shape[1]
+            for out, k, j, far_weight in (
+                (a, z, y, mine),
+                (a, z, 1 - y, by_y),
+                (b, 1 - z, y, by_z),
+            ):
+                start = pl.multiple_of(((t >> 1) * 2 + k) * part + j * cols + at, HEAD)
+                both = jnp.concatenate([weight[:, pl.ds(start, size)], far_weight[...]], axis=0)
+                here = pl.ds(pl.multiple_of(j * cols + at, HEAD), size)
+                out[:, here] = nn(left[...], both).astype(BF16)
+            at += size
+
+    by_place(t, place, own_out, sib_out, run)
+
+
+def late_kernel(t_ref, place_ref, left, weight, diag_a, diag_b, direct, own_out, sib_out):
+    t, place = t_ref[0], place_ref[0]
+    core, y, z = t & 1, place & 1, place >> 1
+    part = weight.shape[1] // 4
+    cols = diag_a.shape[1] + diag_b.shape[1]
+    rest = direct.shape[1] // 2
+
+    def product(k, at, size, far_weight):
+        start = pl.multiple_of(((t >> 1) * 2 + k) * part + at, HEAD)
         both = jnp.concatenate([weight[:, pl.ds(start, size)], far_weight], axis=0)
-        term = nn(left[...], both)
-        out[:, pl.ds(pl.multiple_of(at, HEAD), size)] = term.astype(BF16)
-
-    def run(a, b):
-        put(a, z, y * cols, cols, first[...])
-        put(a, z, (1 - y) * cols, cols, by_y[...])
-        put(b, 1 - z, y * cols, cols, by_z[...])
-        put(b, 1 - z, (1 - y) * cols, wide_a, diag_a[...])
-        put(b, 1 - z, (1 - y) * cols + wide_a, cols - wide_a, diag_b[...])
-
-    by_place(t, place, own_out, sib_out, run)
-    for out, k in ((sib_out, 1 - core), (own_out, core)):
-        at = pl.ds(pl.multiple_of(k * rest, HEAD), rest)
-        put(out, k, 2 * cols, rest, direct[:, at])
+        return nn(left[...], both).astype(BF16)
+
+    at = 0
+    for piece in (diag_a, diag_b):
+        size = piece.shape[1]
+        value = product(1 - z, (1 - y) * cols + at, size, piece[...])
+        own_out[:, at : at + size] = value
+        sib_out[:, at : at + size] = value
+        at += size
+    for out, k in ((own_out, core), (sib_out, 1 - core)):
+        where = pl.ds(pl.multiple_of(k * rest, HEAD), rest)
+        out[:, cols:] = product(k, 2 * cols, rest, direct[:, where])
+
+
+def join_kernel(t_ref, place_ref, own, other, own_late, other_late, out):
+    t, place = t_ref[0], place_ref[0]
+    y, z = place & 1, place >> 1
+    cols = own.shape[1] // 2
+
+    def add(a, b):
+        return (a.astype(F32) + b.astype(F32)).astype(BF16)
+
+    @pl.when((t & 1) == z)
+    def _():
+        out[:, : 2 * cols] = add(own[...], other[...])
+
+    @pl.when((t & 1) != z)
+    def _():
+        here = pl.ds(pl.multiple_of(y * cols, HEAD), cols)
+        out[:, here] = add(own[:, here], other[:, here])
+        there = pl.ds(pl.multiple_of((1 - y) * cols, HEAD), cols)
+        out[:, there] = add(own_late[:, :cols], other_late[:, :cols])
+
+    out[:, 2 * cols :] = add(own_late[:, cols:], other_late[:, cols:])
 
 
 def backward_kernel(q, k, v, pt, near, far, gq, gk, gv):
@@ -267,35 +321,29 @@
     t = lax.axis_index("tensor").astype(jnp.int32).reshape(1)
     place = (lax.axis_index("dp").astype(jnp.int32) & 3).reshape(1)
 
-    gone, share, direct, picked = call(
-        functools.partial(open_kernel, cap, blocks),
-        [
-            ((1,), jnp.int32),
-            ((width, cols), BF16),
-            ((width, 2 * rest), BF16),
-            ((cap, part), BF16),
-        ],
-        [SMEM, SMEM, SMEM, SMEM, ANY, ANY],
-        [pltpu.SemaphoreType.DMA((4,))],
+    share, direct = call(
+        functools.partial(share_kernel, part, cols),
+        [((width, cols), BF16), ((width, 2 * rest), BF16)],
+        [SMEM, SMEM, ANY],
+        [pltpu.SemaphoreType.DMA((3,))],
         limit=OPEN_LIMIT,
-    )(segment_ids, move_flags, t, place, out_weight, out_cotangent)
+    )(t, place, out_weight)
     first = flip(share, "tensor", 2)
     cot_raw = flip(out_cotangent, "tensor", 1)
+
+    gone, picked, att, sent, pt = attend(
+        tie(segment_ids, share), move_flags, queries, key_rows, value_rows, out_cotangent
+    )
     back = shifted(picked, "dp", -1)
-
-    att, sent, pt = call(
-        functools.partial(forward_kernel, cap),
-        [((dest, width), BF16), ((cap, width), BF16), ((heads, home, home), BF16)],
-        [SMEM, SMEM, VMEM, VMEM, VMEM],
-        [pltpu.VMEM((blocks + 1, cap, width), BF16)],
-    )(segment_ids, gone, queries, key_rows, value_rows)
     came = shifted(sent, "dp", 1)
-    back_sib = flip(tie(back, sent), "tensor", 1)
-
-    first, back_sib, cot_raw, sent = lax.optimization_barrier((first, back_sib, cot_raw, sent))
+
+    first, back, came = lax.optimization_barrier((first, back, came))
     by_y = flip(first, "dp", 1)
     by_z = flip(first, "dp", 2)
-    direct = flip(tie(direct, first), "tensor", 2)
+    att = lax.dynamic_update_slice(att, came, (home, 0))
+    far_att = flip(att, "tensor", 2)
+    direct = flip(tie(direct, att), "tensor", 2)
+    back_sib = flip(back, "tensor", 1)
 
     cot_own, cot_sib = call(
         functools.partial(home_kernel, cap, blocks),
@@ -311,21 +359,27 @@
         moved=(home + width) * part * 4,
     )(t, cot_own, cot_sib, out_weight)[0]
 
-    by_y, by_z, near = lax.optimization_barrier((by_y, by_z, near))
-    cut_a, cut_b = lax.optimization_barrier((by_y[:, :wide_a], by_z[:, wide_a:]))
-    diag_a = flip(cut_a, "dp", 2)
-    diag_b = flip(cut_b, "dp", 1)
-
-    att = lax.dynamic_update_slice(att, came, (home, 0))
-    far_att = flip(att, "tensor", 2)
-
+    by_y, by_z, near, far_att = lax.optimization_barrier((by_y, by_z, near, far_att))
+    diag_a = flip(by_y[:, :wide_a], "dp", 2)
+    diag_b = flip(by_z[:, wide_a:], "dp", 1)
+
+    early = (first, by_y, by_z)
     half = call(
         far_kernel,
         [((home, width), F32)],
         [SMEM, SMEM] + [VMEM] * 5,
         flops=6 * home * width * cols,
         moved=(home + width) * cols * 6,
-    )(t, place, cot_own, cot_sib, first, by_y, by_z)[0]
+    )(t, place, cot_own, cot_sib, *early)[0]
+    own, sib, left = call(
+        functools.partial(early_kernel, cap, part),
+        [((dest, 2 * cols), BF16), ((dest, 2 * cols), BF16), ((dest, 2 * width), BF16)],
+        [SMEM] * 3 + [VMEM] * 6,
+        flops=12 * dest * width * cols,
+        moved=12 * width * cols + dest * part * 4,
+    )(gone, t, place, att, far_att, out_weight, *early)
+    other = flip(sib, "tensor", 1)
+    half, own, near = lax.optimization_barrier((half, own, near))
     send = call(
         last_kernel,
         [((home, width), BF16)],
@@ -334,23 +388,26 @@
         moved=(home + width) * (cols + 2 * rest) * 2,
     )(t, place, cot_own, cot_sib, half, diag_a, diag_b, direct)[0]
     far = flip(send, "tensor", 2)
-
-    sib_part, own_part = call(
-        functools.partial(project_kernel, cap),
-        [((dest, part), BF16), ((dest, part), BF16)],
-        [SMEM] * 3 + [VMEM] * 9,
-        [pltpu.VMEM((dest, 2 * width), BF16)],
-        flops=8 * dest * width * part,
-        moved=8 * width * part + dest * part * 4,
-    )(gone, t, tie(place, send), att, far_att, out_weight, first, by_y, by_z, diag_a, diag_b, direct)
-    other = flip(sib_part, "tensor", 1)
-    projected = (own_part.astype(F32) + other.astype(F32)).astype(BF16)
+    own_late, sib_late = call(
+        late_kernel,
+        [((dest, cols + rest), BF16)] * 2,
+        [SMEM] * 2 + [VMEM] * 5,
+        flops=4 * dest * width * (cols + 2 * rest),
+        moved=4 * width * (cols + 2 * rest) + dest * part * 2,
+    )(t, tie(place, send), left, out_weight, diag_a, diag_b, direct)
+    other_late = flip(sib_late, "tensor", 1)
+    projected = call(
+        join_kernel,
+        [((dest, part), BF16)],
+        [SMEM] * 2 + [VMEM] * 4,
+        moved=dest * part * 6,
+    )(t, place, own, other, own_late, other_late)[0]
 
     grad_q, grad_k, grad_v = call(
         backward_kernel,
         [((home, width), BF16)] * 3,
         [VMEM] * 6,
-        flops=3200 * home * home * width,
+        flops=800 * home * home * width,
         moved=9 * home * width * 2,
     )(queries, key_rows, value_rows, pt, near, far)
     return (projected, grad_q, grad_k, grad_v)
@@ -362,17 +419,9 @@
     cap = dest - home
     blocks = home // cap
     heads = width // HEAD
-    gone, picked = call(
-        functools.partial(pick_kernel, cap, blocks),
-        [((1,), jnp.int32), ((cap, part), BF16)],
-        [SMEM, SMEM, VMEM],
-    )(segment_ids, move_flags, out_cotangent)
-    att, sent, pt = call(
-        functools.partial(forward_kernel, cap),
-        [((dest, width), BF16), ((cap, width), BF16), ((heads, home, home), BF16)],
-        [SMEM, SMEM, VMEM, VMEM, VMEM],
-        [pltpu.VMEM((blocks + 1, cap, width), BF16)],
-    )(segment_ids, gone, queries, key_rows, value_rows)
+    gone, picked, att, sent, pt = attend(
+        segment_ids, move_flags, queries, key_rows, value_rows, out_cotangent
+    )
     came = shifted(sent, "dp", 1)
     kept = jnp.where(gone[0] < blocks, home - cap, home)
     att = lax.dynamic_update_slice(att, came, (kept, 0))

time: 56.6 us -> 50.5 us (0.89)
  other arithmetic: 2.75 us -> 0 us
  local copies, waits for them, and re-layouts: 2.42 us -> 0.09 us
  Pallas kernels: 17 us -> 15.5 us
  waiting for transfers between devices: 16.6 us -> 17.8 us
  starting transfers between devices: 16.8 us -> 16.2 us
    ppermute x2, waiting for transfers between devices: 3.38 us -> 6.79 us  [shifted(): lax.ppermute(values, axis, [(i, (i + by) % size) for i in range(size)])]
    convert_element_type x1 -> x0, other arithmetic: 2.75 us -> none  [shards(): projected = (own_part.astype(F32) + other.astype(F32)).astype(BF16)]
    unnamed x16 -> x14, local copies, waits for them, and re-layouts: 2.37 us -> 0.03 us
    ppermute x11 -> x12, waiting for transfers between devices: 13.2 us -> 11 us  [flip(): return lax.ppermute(values, axis, [(i, i ^ by) for i in range(size)])]
    pallas_call x4 -> x6, Pallas kernels: 13.1 us -> 11.4 us  [the longest x1 2.54 us: attend(): call(functools.partial(forward_kernel, cap), [((1,), jnp.int32), ((cap, p...]
    ppermute x11 -> x12, starting transfers between devices: 11.8 us -> 11.6 us  [flip(): return lax.ppermute(values, axis, [(i, i ^ by) for i in range(size)])]
  transfers between devices with their start and end apart: 13 -> 14, of which waited for: 9 -> 5; matrix products, arithmetic and copies ran while one was open for 0% -> 0% of each run, Pallas kernels for 30% -> 26%
where the time goes in v3:
time: 50.5 us; the launch traced here: 50.3 us
  waiting for transfers between devices  17.8 us (35%)
  starting transfers between devices  16.2 us (32%)
  Pallas kernels  15.5 us (31%)
  between operations  0.79 us (2%)
    ppermute x12, starting transfers between devices, flip(): return lax.ppermute(values, axis, [(i, i ^ by) for i in range(size)])  11.6 us
    ppermute x12, waiting for transfers between devices, flip(): return lax.ppermute(values, axis, [(i, i ^ by) for i in range(size)])  11 us
    ppermute x2, waiting for transfers between devices, shifted(): lax.ppermute(values, axis, [(i, (i + by) % size) for i in range(size)])  6.79 us
    ppermute x2, starting transfers between devices, shifted(): lax.ppermute(values, axis, [(i, (i + by) % size) for i in range(size)])  4.61 us
    pallas_call x1, Pallas kernels, attend(): call(functools.partial(forward_kernel, cap), [((1,), jnp.int32), ((cap, p...  2.54 us
    pallas_call x1, Pallas kernels, shards(): call(backward_kernel, [((home, width), BF16)] * 3, [VMEM] * 6, flops=800...  2.53 us
    pallas_call x1, Pallas kernels, shards(): call(functools.partial(early_kernel, cap, part), [((dest, 2 * cols), BF16...  2.5 us
    pallas_call x1, Pallas kernels, shards(): call(own_kernel, [((home, width), F32)], [SMEM, VMEM, VMEM, VMEM], flops=...  1.41 us
  transfers between devices with their start and end apart: 14, of which 5 were waited for; matrix products, arithmetic and copies ran while one was open for 0% of the time, Pallas kernels for 26%

profile of v3, /device:TPU:0, one launch (start us, length us, event | category | flops | bytes accessed | tf_op | source)
XLA Modules:
  0.0 50.3 jit_solution(12113668172468834121)
XLA Ops:
  0.6 0.5 %collective-permute-start = (bf16[448,1536]{1,0:T(8,128)(2,1)}, bf16[448,1536]{1,0:T(8,128)(2,1)S(1)}, u32[]{:S(2)}, u32[]{:S(2)}) collective-permute-start(bf16[448,1536]{1,0:T(8,128)(2,1)} %refs_0_.1), channel_id=1, source_target_pairs={{0,1},{1,0},{2,3},{3,2},{4,5},{5,4},{6,7},{7,6},{8,9},{9,8},{10,11... | collective-permute-start | bytes 4128776 | tf_op jit(solution)/shard_map/ppermute | solution.py:300
  1.2 0.0 copy-start.1
  1.2 0.0 copy-start.2
  1.2 0.0 copy-start.3
  1.2 0.0 copy-start.4
  1.2 0.0 copy-start.5
  1.2 0.0 copy-start.6
  1.2 1.4 %shard_map.102 = (bf16[384,640]{1,0:T(8,128)(2,1)S(1)}, bf16[384,512]{1,0:T(8,128)(2,1)S(1)}) custom-call(s32[1]{0:T(128)} %bitcast.t.t_ref, s32[1]{0:T(128)} %bitcast.1.place.place_ref, bf16[384,6144]{1,0:T(8,128)(2,1)} %weight.7), custom_call_target="tpu_custom_call" | custom-call | tf_op jit(solution)/shard_map/pallas_call | solution.py:324
  2.5 2.6 %collective-permute-start.1 = (bf16[384,640]{1,0:T(8,128)(2,1)S(1)}, bf16[384,640]{1,0:T(8,128)(2,1)S(1)}, u32[]{:S(2)}, u32[]{:S(2)}) collective-permute-start(bf16[384,640]{1,0:T(8,128)(2,1)S(1)} %get-tuple-element.34), channel_id=1, source_target_pairs={{0,2},{1,3},{2,0},{3,1},{4,6},{5,7},{6,4},{7,5},{8,10},{9,11},{10,... | collective-permute-start | bytes 1474568 | tf_op jit(solution)/shard_map/ppermute | solution.py:300
  5.1 0.0 copy-done.1
  5.1 0.0 copy-done.2
  5.1 0.0 copy-done.3
  5.2 0.0 copy-done.4
  5.2 0.0 copy-done.5
  5.2 0.0 copy-done.6
  5.2 0.0 copy-start
  5.2 2.5 %shard_map.103 = (s32[1]{0:T(128)}, bf16[64,1536]{1,0:T(8,128)(2,1)S(1)}, bf16[448,384]{1,0:T(8,128)(2,1)S(1)}, bf16[64,384]{1,0:T(8,128)(2,1)S(1)}, bf16[3,384,384]{2,1,0:T(8,128)(2,1)S(1)}) custom-call(s32[1,384]{1,0:T(1,128)S(1)} %copy-done.5, s32[1,384]{1,0:T(1,128)S(1)} %copy-done.6, bf16[384,384]{1,0:T(8,128)(2,1)S(1)} %copy-done.2, ...), custom_call_target="tpu_custom_call" | custom-call | tf_op jit(solution)/shard_map/pallas_call | solution.py:55
  7.7 4.6 %collective-permute-start.2 = (bf16[64,1536]{1,0:T(8,128)(2,1)S(1)}, bf16[64,1536]{1,0:T(8,128)(2,1)S(1)}, u32[]{:S(2)}, u32[]{:S(2)}) collective-permute-start(bf16[64,1536]{1,0:T(8,128)(2,1)S(1)} %get-tuple-element.37), channel_id=1, source_target_pairs={{0,28},{4,0},{8,4},{12,8},{16,12},{20,16},{24,20},{28,24},{1,29},{... | collective-permute-start | bytes 589832 | tf_op jit(solution)/shard_map/ppermute | solution.py:305
  12.3 0.0 collective-permute-start.3
  12.3 6.8 %collective-permute-done.3 = bf16[64,384]{1,0:T(8,128)(2,1)S(1)} collective-permute-done((bf16[64,384]{1,0:T(8,128)(2,1)S(1)}, bf16[64,384]{1,0:T(8,128)(2,1)S(1)}, u32[]{:S(2)}, u32[]{:S(2)}) %collective-permute-start.3) | collective-permute-done | bytes 49184 | tf_op jit(solution)/shard_map/ppermute | solution.py:305
  19.1 0.0 collective-permute-done.2.refs_2_
  19.1 0.0 collective-permute-done.1.refs_0_
  19.1 0.0 collective-permute-start.5
  19.1 1.2 %collective-permute-start.6 = (bf16[384,640]{1,0:T(8,128)(2,1)S(1)}, bf16[384,640]{1,0:T(8,128)(2,1)S(1)}, u32[]{:S(2)}, u32[]{:S(2)}) collective-permute-start(bf16[384,640]{1,0:T(8,128)(2,1)S(1)} %collective-permute-done.1.refs_0_), channel_id=1, source_target_pairs={{0,8},{4,12},{8,0},{12,4},{16,24},{20,28},{24,16},{28,20},{1,9},{5... | collective-permute-start | bytes 1474568 | tf_op jit(solution)/shard_map/ppermute | solution.py:300
  20.4 1.6 %collective-permute-start.7 = (bf16[448,384]{1,0:T(8,128)(2,1)S(1)}, bf16[448,384]{1,0:T(8,128)(2,1)S(1)}, u32[]{:S(2)}, u32[]{:S(2)}) collective-permute-start(bf16[448,384]{1,0:T(8,128)(2,1)S(1)} %constant_dynamic-update-slice_fusion.att), channel_id=1, source_target_pairs={{0,2},{1,3},{2,0},{3,1},{4,6},{5,7},{6,4},{7,5},{8,10},{9,11},{10,... | collective-permute-start | bytes 1032200 | tf_op jit(solution)/shard_map/ppermute | solution.py:300
  21.9 0.0 collective-permute-start.4
  21.9 1.4 %collective-permute-done.4.refs_3_ = bf16[64,1536]{1,0:T(8,128)(2,1)S(1)} collective-permute-done((bf16[64,1536]{1,0:T(8,128)(2,1)S(1)}, bf16[64,1536]{1,0:T(8,128)(2,1)S(1)}, u32[]{:S(2)}, u32[]{:S(2)}) %collective-permute-start.4) | collective-permute-done | bytes 196640 | tf_op jit(solution)/shard_map/ppermute | solution.py:300
  23.4 0.5 %collective-permute-start.11 = (bf16[384,512]{1,0:T(8,128)(2,1)S(1)}, bf16[384,512]{1,0:T(8,128)(2,1)S(1)}, u32[]{:S(2)}, u32[]{:S(2)}) collective-permute-start(bf16[384,512]{1,0:T(8,128)(2,1)S(1)} %get-tuple-element.54), channel_id=1, source_target_pairs={{0,2},{1,3},{2,0},{3,1},{4,6},{5,7},{6,4},{7,5},{8,10},{9,11},{10,... | collective-permute-start | bytes 1179656 | tf_op jit(solution)/shard_map/ppermute | solution.py:300
  23.9 0.0 collective-permute-done.refs_1_
  23.9 0.8 %shard_map.104 = (bf16[384,1536]{1,0:T(8,128)(2,1)S(1)}, bf16[384,1536]{1,0:T(8,128)(2,1)S(1)}) custom-call(s32[1]{0:T(128)} %get-tuple-element.36.gone_ref.gone, bf16[448,1536]{1,0:T(8,128)(2,1)S(1)} %copy-done.1, bf16[448,1536]{1,0:T(8,128)(2,1)S(1)} %collective-permute-done.refs_1_, bf16[64,1536]{1,0:T(8,128)(2,1)S(1)} %collective-permute-done.2.refs_2_, ...), custom_call_target="tpu_custom_call" | custom-call | tf_op jit(solution)/shard_map/pallas_call | solution.py:348
  24.7 0.0 copy-done
  24.7 1.4 %shard_map.105.near = f32[384,384]{1,0:T(8,128)S(1)} custom-call(s32[1]{0:T(128)} %bitcast.t.t_ref, bf16[384,1536]{1,0:T(8,128)(2,1)S(1)} %get-tuple-element.40.cot_own, bf16[384,1536]{1,0:T(8,128)(2,1)S(1)} %get-tuple-element.41.cot_sib, bf16[384,6144]{1,0:T(8,128)(2,1)S(1)} %copy-done), custom_call_target="tpu_custom_call" | custom-call | flops 905969664 | bytes 4718592 | tf_op jit(solution)/shard_map/pallas_call | solution.py:354
  26.1 5.3 %collective-permute-done.7.far_att = bf16[448,384]{1,0:T(8,128)(2,1)S(1)} collective-permute-done((bf16[448,384]{1,0:T(8,128)(2,1)S(1)}, bf16[448,384]{1,0:T(8,128)(2,1)S(1)}, u32[]{:S(2)}, u32[]{:S(2)}) %collective-permute-start.7) | collective-permute-done | bytes 344096 | tf_op jit(solution)/shard_map/ppermute | solution.py:300
  31.4 0.0 collective-permute-done.5.refs_1_
  31.4 0.0 collective-permute-done.6.refs_2_
  31.5 1.5 %collective-permute-start.9 = (bf16[384,384]{1,0:T(8,128)(2,1)S(1)}, bf16[384,384]{1,0:T(8,128)(2,1)S(1)}, u32[]{:S(2)}, u32[]{:S(2)}) collective-permute-start(bf16[384,384]{1,0:T(8,128)(2,1)S(1)} %slice.6), channel_id=1, source_target_pairs={{0,8},{4,12},{8,0},{12,4},{16,24},{20,28},{24,16},{28,20},{1,9},{5... | collective-permute-start | bytes 884744 | tf_op jit(solution)/shard_map/ppermute | solution.py:300
  33.0 1.5 %collective-permute-start.10 = (bf16[384,256]{1,0:T(8,128)(2,1)S(1)}, bf16[384,256]{1,0:T(8,128)(2,1)S(1)}, u32[]{:S(2)}, u32[]{:S(2)}) collective-permute-start(bf16[384,256]{1,0:T(8,128)(2,1)S(1)} %slice.7), channel_id=1, source_target_pairs={{0,4},{4,0},{8,12},{12,8},{16,20},{20,16},{24,28},{28,24},{1,5},{5... | collective-permute-start | bytes 589832 | tf_op jit(solution)/shard_map/ppermute | solution.py:300
  34.5 1.0 %shard_map.106.part_sum = f32[384,384]{1,0:T(8,128)S(1)} custom-call(s32[1]{0:T(128)} %bitcast.t.t_ref, s32[1]{0:T(128)} %bitcast.1.place.place_ref, bf16[384,1536]{1,0:T(8,128)(2,1)S(1)} %get-tuple-element.40.cot_own, bf16[384,1536]{1,0:T(8,128)(2,1)S(1)} %get-tuple-element.41.cot_sib, bf16[384,640]{1,0:T(8,128)(2,1)S(1)} %collective-permute-done.1.refs_0_, ...), custom_call_target="tpu_custom_call" | custom-call | flops 566231040 | bytes 2949120 | tf_op jit(solution)/shard_map/pallas_call | solution.py:367
  35.5 2.5 %shard_map.107 = (bf16[448,1280]{1,0:T(8,128)(2,1)S(1)}, bf16[448,1280]{1,0:T(8,128)(2,1)S(1)}, bf16[448,768]{1,0:T(8,128)(2,1)S(1)}) custom-call(s32[1]{0:T(128)} %get-tuple-element.36.gone_ref.gone, s32[1]{0:T(128)} %bitcast.t.t_ref, s32[1]{0:T(128)} %bitcast.1.place.place_ref, bf16[448,384]{1,0:T(8,128)(2,1)S(1)} %constant_dynamic-update-slice_fusion.att, ...), custom_call_target="tpu_custom_call" | custom-call | flops 1321205760 | bytes 5701632 | tf_op jit(solution)/shard_map/pallas_call | solution.py:374
  38.0 0.0 collective-permute-done.11.direct
  38.0 0.7 %collective-permute-done.10.diag_b = bf16[384,256]{1,0:T(8,128)(2,1)S(1)} collective-permute-done((bf16[384,256]{1,0:T(8,128)(2,1)S(1)}, bf16[384,256]{1,0:T(8,128)(2,1)S(1)}, u32[]{:S(2)}, u32[]{:S(2)}) %collective-permute-start.10) | collective-permute-done | bytes 196640 | tf_op jit(solution)/shard_map/ppermute | solution.py:300
  38.7 0.0 collective-permute-done.9.diag_a
  38.7 0.9 %shard_map.108 = bf16[384,384]{1,0:T(8,128)(2,1)S(1)} custom-call(s32[1]{0:T(128)} %bitcast.t.t_ref, s32[1]{0:T(128)} %bitcast.1.place.place_ref, bf16[384,1536]{1,0:T(8,128)(2,1)S(1)} %get-tuple-element.40.cot_own, bf16[384,1536]{1,0:T(8,128)(2,1)S(1)} %get-tuple-element.41.cot_sib, f32[384,384]{1,0:T(8,128)S(1)} %shard_map.106.part_sum, ...), custom_call_target="tpu_custom_call" | custom-call | flops 339738624 | bytes 1769472 | tf_op jit(solution)/shard_map/pallas_call | solution.py:383
  39.6 1.6 %collective-permute-start.13 = (bf16[384,384]{1,0:T(8,128)(2,1)S(1)}, bf16[384,384]{1,0:T(8,128)(2,1)S(1)}, u32[]{:S(2)}, u32[]{:S(2)}) collective-permute-start(bf16[384,384]{1,0:T(8,128)(2,1)S(1)} %shard_map.108), channel_id=1, source_target_pairs={{0,2},{1,3},{2,0},{3,1},{4,6},{5,7},{6,4},{7,5},{8,10},{9,11},{10,... | collective-permute-start | bytes 884744 | tf_op jit(solution)/shard_map/ppermute | solution.py:300
  41.2 0.0 collective-permute-start.8
  41.2 1.1 %shard_map.109 = (bf16[448,896]{1,0:T(8,128)(2,1)S(1)}, bf16[448,896]{1,0:T(8,128)(2,1)S(1)}) custom-call(s32[1]{0:T(128)} %bitcast.t.t_ref, s32[1]{0:T(128)} %bitcast.1.place.place_ref, bf16[448,768]{1,0:T(8,128)(2,1)S(1)} %get-tuple-element.56.left, bf16[384,6144]{1,0:T(8,128)(2,1)S(1)} %copy-done, bf16[384,384]{1,0:T(8,128)(2,1)S(1)} %collective-permute-done.9.diag_a, ...), custom_call_target="tpu_custom_call" | custom-call | flops 792723456 | bytes 3145728 | tf_op jit(solution)/shard_map/pallas_call | solution.py:391
  42.3 0.6 %collective-permute-start.12 = (bf16[448,896]{1,0:T(8,128)(2,1)S(1)}, bf16[448,896]{1,0:T(8,128)(2,1)S(1)}, u32[]{:S(2)}, u32[]{:S(2)}) collective-permute-start(bf16[448,896]{1,0:T(8,128)(2,1)S(1)} %get-tuple-element.58), channel_id=1, source_target_pairs={{0,1},{1,0},{2,3},{3,2},{4,5},{5,4},{6,7},{7,6},{8,9},{9,8},{10,11... | collective-permute-start | bytes 2408456 | tf_op jit(solution)/shard_map/ppermute | solution.py:300
  42.9 3.5 %collective-permute-done.13.far = bf16[384,384]{1,0:T(8,128)(2,1)S(1)} collective-permute-done((bf16[384,384]{1,0:T(8,128)(2,1)S(1)}, bf16[384,384]{1,0:T(8,128)(2,1)S(1)}, u32[]{:S(2)}, u32[]{:S(2)}) %collective-permute-start.13) | collective-permute-done | bytes 294944 | tf_op jit(solution)/shard_map/ppermute | solution.py:300
  46.4 2.5 %shard_map.111 = (bf16[384,384]{1,0:T(8,128)(2,1)}, bf16[384,384]{1,0:T(8,128)(2,1)}, bf16[384,384]{1,0:T(8,128)(2,1)}) custom-call(bf16[384,384]{1,0:T(8,128)(2,1)S(1)} %copy-done.2, bf16[384,384]{1,0:T(8,128)(2,1)S(1)} %copy-done.3, bf16[384,384]{1,0:T(8,128)(2,1)S(1)} %copy-done.4, bf16[3,384,384]{2,1,0:T(8,128)(2,1)S(1)} %get-tuple-element.59.pt, ...), custom_call_target="tpu_custom_call" | custom-call | flops 45298483200 | bytes 2654208 | tf_op jit(solution)/shard_map/pallas_call | solution.py:406
  48.9 0.0 collective-permute-done.12.other_late
  48.9 0.0 collective-permute-done.8.other
  48.9 1.4 %shard_map.110 = bf16[448,1536]{1,0:T(8,128)(2,1)} custom-call(s32[1]{0:T(128)} %bitcast.t.t_ref, s32[1]{0:T(128)} %bitcast.1.place.place_ref, bf16[448,1280]{1,0:T(8,128)(2,1)S(1)} %get-tuple-element.50.own, bf16[448,1280]{1,0:T(8,128)(2,1)S(1)} %collective-permute-done.8.other, bf16[448,896]{1,0:T(8,128)(2,1)S(1)} %get-tuple-element.57.own_late, ...), custom_call_target="tpu_custom_call" | custom-call | bytes 4128768 | tf_op jit(solution)/shard_map/pallas_call | solution.py:399
  (3 shorter events, 0.1 us)
Async XLA Ops:
  0.6 23.3 %collective-permute-start = (bf16[448,1536]{1,0:T(8,128)(2,1)}, bf16[448,1536]{1,0:T(8,128)(2,1)S(1)}, u32[]{:S(2)}, u32[]{:S(2)}) collective-permute-start(bf16[448,1536]{1,0:T(8,128)(2,1)} %refs_0_.1), channel_id=1, source_target_pairs={{0,1},{1,0},{2,3},{3,2},{4,5},{5,4},{6,7},{7,6},{8,9},{9,8},{10,11... | collective-permute-start | bytes 4128776 | tf_op jit(solution)/shard_map/ppermute | solution.py:300
  1.2 4.0 %copy-start.1 = (bf16[448,1536]{1,0:T(8,128)(2,1)S(1)}, bf16[448,1536]{1,0:T(8,128)(2,1)}, u32[]{:S(2)}) copy-start(bf16[448,1536]{1,0:T(8,128)(2,1)} %refs_0_.1) | copy-start | bytes 4128772
  1.2 4.0 %copy-start.2 = (bf16[384,384]{1,0:T(8,128)(2,1)S(1)}, bf16[384,384]{1,0:T(8,128)(2,1)}, u32[]{:S(2)}) copy-start(bf16[384,384]{1,0:T(8,128)(2,1)} %q.3) | copy-start | bytes 884740
  1.2 4.0 %copy-start.3 = (bf16[384,384]{1,0:T(8,128)(2,1)S(1)}, bf16[384,384]{1,0:T(8,128)(2,1)}, u32[]{:S(2)}) copy-start(bf16[384,384]{1,0:T(8,128)(2,1)} %k.3) | copy-start | bytes 884740
  1.2 4.0 %copy-start.4 = (bf16[384,384]{1,0:T(8,128)(2,1)S(1)}, bf16[384,384]{1,0:T(8,128)(2,1)}, u32[]{:S(2)}) copy-start(bf16[384,384]{1,0:T(8,128)(2,1)} %v.3) | copy-start | bytes 884740
  1.2 4.0 %copy-start.5 = (s32[1,384]{1,0:T(1,128)S(1)}, s32[1,384]{1,0:T(1,128)}, u32[]{:S(2)}) copy-start(s32[1,384]{1,0:T(1,128)} %seg) | copy-start | bytes 4612
  1.2 4.0 %copy-start.6 = (s32[1,384]{1,0:T(1,128)S(1)}, s32[1,384]{1,0:T(1,128)}, u32[]{:S(2)}) copy-start(s32[1,384]{1,0:T(1,128)} %flags.1) | copy-start | bytes 4612
  2.5 16.6 %collective-permute-start.1 = (bf16[384,640]{1,0:T(8,128)(2,1)S(1)}, bf16[384,640]{1,0:T(8,128)(2,1)S(1)}, u32[]{:S(2)}, u32[]{:S(2)}) collective-permute-start(bf16[384,640]{1,0:T(8,128)(2,1)S(1)} %get-tuple-element.34), channel_id=1, source_target_pairs={{0,2},{1,3},{2,0},{3,1},{4,6},{5,7},{6,4},{7,5},{8,10},{9,11},{10,... | collective-permute-start | bytes 1474568 | tf_op jit(solution)/shard_map/ppermute | solution.py:300
  5.2 19.5 %copy-start = (bf16[384,6144]{1,0:T(8,128)(2,1)S(1)}, bf16[384,6144]{1,0:T(8,128)(2,1)}, u32[]{:S(2)}) copy-start(bf16[384,6144]{1,0:T(8,128)(2,1)} %weight.7) | copy-start | bytes 14155780
  7.7 11.4 %collective-permute-start.2 = (bf16[64,1536]{1,0:T(8,128)(2,1)S(1)}, bf16[64,1536]{1,0:T(8,128)(2,1)S(1)}, u32[]{:S(2)}, u32[]{:S(2)}) collective-permute-start(bf16[64,1536]{1,0:T(8,128)(2,1)S(1)} %get-tuple-element.37), channel_id=1, source_target_pairs={{0,28},{4,0},{8,4},{12,8},{16,12},{20,16},{24,20},{28,24},{1,29},{... | collective-permute-start | bytes 589832 | tf_op jit(solution)/shard_map/ppermute | solution.py:305
  12.3 6.8 %collective-permute-start.3 = (bf16[64,384]{1,0:T(8,128)(2,1)S(1)}, bf16[64,384]{1,0:T(8,128)(2,1)S(1)}, u32[]{:S(2)}, u32[]{:S(2)}) collective-permute-start(bf16[64,384]{1,0:T(8,128)(2,1)S(1)} %get-tuple-element.38), channel_id=1, source_target_pairs={{0,4},{4,8},{8,12},{12,16},{16,20},{20,24},{24,28},{28,0},{1,5},{5... | collective-permute-start | bytes 147464 | tf_op jit(solution)/shard_map/ppermute | solution.py:305
  19.1 12.3 %collective-permute-start.5 = (bf16[384,640]{1,0:T(8,128)(2,1)S(1)}, bf16[384,640]{1,0:T(8,128)(2,1)S(1)}, u32[]{:S(2)}, u32[]{:S(2)}) collective-permute-start(bf16[384,640]{1,0:T(8,128)(2,1)S(1)} %collective-permute-done.1.refs_0_), channel_id=1, source_target_pairs={{0,4},{4,0},{8,12},{12,8},{16,20},{20,16},{24,28},{28,24},{1,5},{5... | collective-permute-start | bytes 1474568 | tf_op jit(solution)/shard_map/ppermute | solution.py:300
  19.1 12.3 %collective-permute-start.6 = (bf16[384,640]{1,0:T(8,128)(2,1)S(1)}, bf16[384,640]{1,0:T(8,128)(2,1)S(1)}, u32[]{:S(2)}, u32[]{:S(2)}) collective-permute-start(bf16[384,640]{1,0:T(8,128)(2,1)S(1)} %collective-permute-done.1.refs_0_), channel_id=1, source_target_pairs={{0,8},{4,12},{8,0},{12,4},{16,24},{20,28},{24,16},{28,20},{1,9},{5... | collective-permute-start | bytes 1474568 | tf_op jit(solution)/shard_map/ppermute | solution.py:300
  20.4 11.1 %collective-permute-start.7 = (bf16[448,384]{1,0:T(8,128)(2,1)S(1)}, bf16[448,384]{1,0:T(8,128)(2,1)S(1)}, u32[]{:S(2)}, u32[]{:S(2)}) collective-permute-start(bf16[448,384]{1,0:T(8,128)(2,1)S(1)} %constant_dynamic-update-slice_fusion.att), channel_id=1, source_target_pairs={{0,2},{1,3},{2,0},{3,1},{4,6},{5,7},{6,4},{7,5},{8,10},{9,11},{10,... | collective-permute-start | bytes 1032200 | tf_op jit(solution)/shard_map/ppermute | solution.py:300
  21.9 1.4 %collective-permute-start.4 = (bf16[64,1536]{1,0:T(8,128)(2,1)S(1)}, bf16[64,1536]{1,0:T(8,128)(2,1)S(1)}, u32[]{:S(2)}, u32[]{:S(2)}) collective-permute-start(bf16[64,1536]{1,0:T(8,128)(2,1)S(1)} %collective-permute-done.2.refs_2_), channel_id=1, source_target_pairs={{0,1},{1,0},{2,3},{3,2},{4,5},{5,4},{6,7},{7,6},{8,9},{9,8},{10,11... | collective-permute-start | bytes 589832 | tf_op jit(solution)/shard_map/ppermute | solution.py:300
  23.4 14.6 %collective-permute-start.11 = (bf16[384,512]{1,0:T(8,128)(2,1)S(1)}, bf16[384,512]{1,0:T(8,128)(2,1)S(1)}, u32[]{:S(2)}, u32[]{:S(2)}) collective-permute-start(bf16[384,512]{1,0:T(8,128)(2,1)S(1)} %get-tuple-element.54), channel_id=1, source_target_pairs={{0,2},{1,3},{2,0},{3,1},{4,6},{5,7},{6,4},{7,5},{8,10},{9,11},{10,... | collective-permute-start | bytes 1179656 | tf_op jit(solution)/shard_map/ppermute | solution.py:300
  31.5 7.3 %collective-permute-start.9 = (bf16[384,384]{1,0:T(8,128)(2,1)S(1)}, bf16[384,384]{1,0:T(8,128)(2,1)S(1)}, u32[]{:S(2)}, u32[]{:S(2)}) collective-permute-start(bf16[384,384]{1,0:T(8,128)(2,1)S(1)} %slice.6), channel_id=1, source_target_pairs={{0,8},{4,12},{8,0},{12,4},{16,24},{20,28},{24,16},{28,20},{1,9},{5... | collective-permute-start | bytes 884744 | tf_op jit(solution)/shard_map/ppermute | solution.py:300
  33.0 5.7 %collective-permute-start.10 = (bf16[384,256]{1,0:T(8,128)(2,1)S(1)}, bf16[384,256]{1,0:T(8,128)(2,1)S(1)}, u32[]{:S(2)}, u32[]{:S(2)}) collective-permute-start(bf16[384,256]{1,0:T(8,128)(2,1)S(1)} %slice.7), channel_id=1, source_target_pairs={{0,4},{4,0},{8,12},{12,8},{16,20},{20,16},{24,28},{28,24},{1,5},{5... | collective-permute-start | bytes 589832 | tf_op jit(solution)/shard_map/ppermute | solution.py:300
  39.6 6.8 %collective-permute-start.13 = (bf16[384,384]{1,0:T(8,128)(2,1)S(1)}, bf16[384,384]{1,0:T(8,128)(2,1)S(1)}, u32[]{:S(2)}, u32[]{:S(2)}) collective-permute-start(bf16[384,384]{1,0:T(8,128)(2,1)S(1)} %shard_map.108), channel_id=1, source_target_pairs={{0,2},{1,3},{2,0},{3,1},{4,6},{5,7},{6,4},{7,5},{8,10},{9,11},{10,... | collective-permute-start | bytes 884744 | tf_op jit(solution)/shard_map/ppermute | solution.py:300
  41.2 7.7 %collective-permute-start.8 = (bf16[448,1280]{1,0:T(8,128)(2,1)S(1)}, bf16[448,1280]{1,0:T(8,128)(2,1)S(1)}, u32[]{:S(2)}, u32[]{:S(2)}) collective-permute-start(bf16[448,1280]{1,0:T(8,128)(2,1)S(1)} %get-tuple-element.51), channel_id=1, source_target_pairs={{0,1},{1,0},{2,3},{3,2},{4,5},{5,4},{6,7},{7,6},{8,9},{9,8},{10,11... | collective-permute-start | bytes 3440648 | tf_op jit(solution)/shard_map/ppermute | solution.py:300
  42.3 6.6 %collective-permute-start.12 = (bf16[448,896]{1,0:T(8,128)(2,1)S(1)}, bf16[448,896]{1,0:T(8,128)(2,1)S(1)}, u32[]{:S(2)}, u32[]{:S(2)}) collective-permute-start(bf16[448,896]{1,0:T(8,128)(2,1)S(1)} %get-tuple-element.58), channel_id=1, source_target_pairs={{0,1},{1,0},{2,3},{3,2},{4,5},{5,4},{6,7},{7,6},{8,9},{9,8},{10,11... | collective-permute-start | bytes 2408456 | tf_op jit(solution)/shard_map/ppermute | solution.py:300

commit v4 on v3

--- a/solution.py
+++ b/solution.py
@@ -29,12 +29,12 @@
     return lax.dot_general(a, b, (((0,), (0,)), ((), ())), preferred_element_type=F32)
 
 
-def call(kernel, outs, ins, scratch=(), flops=0, moved=0, exps=0, limit=LIMIT):
+def call(kernel, outs, ins, scratch=(), flops=0, moved=0, exps=0, limit=LIMIT, out=None):
     return pl.pallas_call(
         kernel,
         out_shape=tuple(jax.ShapeDtypeStruct(s, t) for s, t in outs),
         in_specs=list(ins),
-        out_specs=tuple(SMEM if t == jnp.int32 else VMEM for _, t in outs),
+        out_specs=tuple(out or (SMEM if t == jnp.int32 else VMEM) for _, t in outs),
         scratch_shapes=list(scratch),
         compiler_params=pltpu.CompilerParams(vmem_limit_bytes=limit),
         cost_estimate=pl.CostEstimate(flops=flops, bytes_accessed=moved, transcendentals=exps),
@@ -178,18 +178,16 @@
 
 
 def last_kernel(t, place, cot_own, cot_sib, part_sum, diag_a, diag_b, direct, out):
-    wide_a, wide_b = diag_a.shape[1], diag_b.shape[1]
-    cols = wide_a + wide_b
+    cols = diag_a.shape[1]
     rest = direct.shape[1] // 2
-    y = place[0] & 1
     core = t[0] & 1
-    a_at = pl.ds(pl.multiple_of((1 - y) * cols, HEAD), wide_a)
-    b_at = pl.ds(pl.multiple_of((1 - y) * cols + wide_a, HEAD), wide_b)
+    at = pl.ds(pl.multiple_of((1 - (place[0] & 1)) * cols, HEAD), cols)
     own_at = pl.ds(pl.multiple_of(core * rest, HEAD), rest)
     sib_at = pl.ds(pl.multiple_of((1 - core) * rest, HEAD), rest)
 
     def run(a, b):
-        total = part_sum[...] + nt(b[:, a_at], diag_a[...]) + nt(b[:, b_at], diag_b[...])
+        diag = jnp.concatenate([diag_a[...], diag_b[...]], axis=0)
+        total = part_sum[...] + nt(b[:, at], diag)
         total += nt(cot_own[:, 2 * cols :], direct[:, own_at])
         total += nt(cot_sib[:, 2 * cols :], direct[:, sib_at])
         out[...] = total.astype(BF16)
@@ -239,60 +237,94 @@
     t, place = t_ref[0], place_ref[0]
     core, y, z = t & 1, place & 1, place >> 1
     part = weight.shape[1] // 4
-    cols = diag_a.shape[1] + diag_b.shape[1]
+    cols = diag_a.shape[1]
     rest = direct.shape[1] // 2
 
-    def product(k, at, size, far_weight):
+    def product(k, at, size, *far_weight):
         start = pl.multiple_of(((t >> 1) * 2 + k) * part + at, HEAD)
-        both = jnp.concatenate([weight[:, pl.ds(start, size)], far_weight], axis=0)
+        both = jnp.concatenate([weight[:, pl.ds(start, size)], *far_weight], axis=0)
         return nn(left[...], both).astype(BF16)
 
-    at = 0
-    for piece in (diag_a, diag_b):
-        size = piece.shape[1]
-        value = product(1 - z, (1 - y) * cols + at, size, piece[...])
-        own_out[:, at : at + size] = value
-        sib_out[:, at : at + size] = value
-        at += size
+    value = product(1 - z, (1 - y) * cols, cols, diag_a[...], diag_b[...])
+    own_out[:, :cols] = value
+    sib_out[:, :cols] = value
     for out, k in ((own_out, core), (sib_out, 1 - core)):
         where = pl.ds(pl.multiple_of(k * rest, HEAD), rest)
         out[:, cols:] = product(k, 2 * cols, rest, direct[:, where])
 
 
-def join_kernel(t_ref, place_ref, own, other, own_late, other_late, out):
+def join_kernel(cap, t_ref, place_ref, own, other, own_late, other_late, out, buf, sems):
     t, place = t_ref[0], place_ref[0]
     y, z = place & 1, place >> 1
     cols = own.shape[1] // 2
+    same = (t & 1) == z
 
     def add(a, b):
         return (a.astype(F32) + b.astype(F32)).astype(BF16)
 
-    @pl.when((t & 1) == z)
-    def _():
-        out[:, : 2 * cols] = add(own[...], other[...])
-
-    @pl.when((t & 1) != z)
-    def _():
-        here = pl.ds(pl.multiple_of(y * cols, HEAD), cols)
-        out[:, here] = add(own[:, here], other[:, here])
-        there = pl.ds(pl.multiple_of((1 - y) * cols, HEAD), cols)
-        out[:, there] = add(own_late[:, :cols], other_late[:, :cols])
-
-    out[:, 2 * cols :] = add(own_late[:, cols:], other_late[:, cols:])
-
-
-def backward_kernel(q, k, v, pt, near, far, gq, gk, gv):
+    copies = []
+    for i in range(own.shape[0] // cap):
+        rows = slice(i * cap, (i + 1) * cap)
+
+        @pl.when(same)
+        def _(rows=rows):
+            buf[rows, : 2 * cols] = add(own[rows], other[rows])
+
+        @pl.when(jnp.logical_not(same))
+        def _(rows=rows):
+            here = pl.ds(pl.multiple_of(y * cols, HEAD), cols)
+            buf[rows, here] = add(own[rows, here], other[rows, here])
+            there = pl.ds(pl.multiple_of((1 - y) * cols, HEAD), cols)
+            buf[rows, there] = add(own_late[rows, :cols], other_late[rows, :cols])
+
+        buf[rows, 2 * cols :] = add(own_late[rows, cols:], other_late[rows, cols:])
+        where = pl.ds(i * cap, cap)
+        copy = pltpu.make_async_copy(buf.at[where, :], out.at[where, :], sems.at[i])
+        copy.start()
+        copies.append(copy)
+    for copy in copies:
+        copy.wait()
+
+
+def backward_kernel(q, k, v, pt, near, far, gq, gk, gv, bq, bk, bv, sems):
+    copies = []
     for h in range(q.shape[1] // HEAD):
         cols = slice(h * HEAD, (h + 1) * HEAD)
+        where = pl.ds(h * HEAD, HEAD)
+
+        def send(buf, out, n, where=where, h=h):
+            copy = pltpu.make_async_copy(buf.at[:, where], out.at[:, where], sems.at[3 * h + n])
+            copy.start()
+            copies.append(copy)
+
         cot = (near[:, cols] + far[:, cols].astype(F32)).astype(BF16)
         weights = pt[h]
-        gv[:, cols] = nn(weights, cot).astype(BF16)
+        bv[:, cols] = nn(weights, cot).astype(BF16)
+        send(bv, gv, 0)
         rise = nt(v[:, cols], cot)
         wide = weights.astype(F32)
         mean = jnp.sum(wide * rise, axis=0, keepdims=True)
         slope = (wide * (rise - mean) * HEAD ** (-0.5)).astype(BF16)
-        gk[:, cols] = nn(slope, q[:, cols]).astype(BF16)
-        gq[:, cols] = tn(slope, k[:, cols]).astype(BF16)
+        bk[:, cols] = nn(slope, q[:, cols]).astype(BF16)
+        send(bk, gk, 1)
+        bq[:, cols] = tn(slope, k[:, cols]).astype(BF16)
+        send(bq, gq, 2)
+    for copy in copies:
+        copy.wait()
+
+
+def gradients(queries, key_rows, value_rows, pt, near, far, flops):
+    home, width = queries.shape
+    return call(
+        backward_kernel,
+        [((home, width), BF16)] * 3,
+        [VMEM] * 6,
+        [pltpu.VMEM((home, width), BF16)] * 3
+        + [pltpu.SemaphoreType.DMA((3 * (width // HEAD),))],
+        flops=flops,
+        moved=9 * home * width * 2,
+        out=ANY,
+    )(queries, key_rows, value_rows, pt, near, far)
 
 
 def flip(values, axis, by):
@@ -317,7 +349,6 @@
     heads = width // HEAD
     cols = part * 5 // 12 // HEAD * HEAD
     rest = part - 2 * cols
-    wide_a = (cols + HEAD) // 2 // HEAD * HEAD
     t = lax.axis_index("tensor").astype(jnp.int32).reshape(1)
     place = (lax.axis_index("dp").astype(jnp.int32) & 3).reshape(1)
 
@@ -360,8 +391,9 @@
     )(t, cot_own, cot_sib, out_weight)[0]
 
     by_y, by_z, near, far_att = lax.optimization_barrier((by_y, by_z, near, far_att))
-    diag_a = flip(by_y[:, :wide_a], "dp", 2)
-    diag_b = flip(by_z[:, wide_a:], "dp", 1)
+    rows_a = width * 7 // 12 // 32 * 32
+    diag_a = flip(by_y[:rows_a], "dp", 2)
+    diag_b = flip(by_z[rows_a:], "dp", 1)
 
     early = (first, by_y, by_z)
     half = call(
@@ -371,15 +403,6 @@
         flops=6 * home * width * cols,
         moved=(home + width) * cols * 6,
     )(t, place, cot_own, cot_sib, *early)[0]
-    own, sib, left = call(
-        functools.partial(early_kernel, cap, part),
-        [((dest, 2 * cols), BF16), ((dest, 2 * cols), BF16), ((dest, 2 * width), BF16)],
-        [SMEM] * 3 + [VMEM] * 6,
-        flops=12 * dest * width * cols,
-        moved=12 * width * cols + dest * part * 4,
-    )(gone, t, place, att, far_att, out_weight, *early)
-    other = flip(sib, "tensor", 1)
-    half, own, near = lax.optimization_barrier((half, own, near))
     send = call(
         last_kernel,
         [((home, width), BF16)],
@@ -388,6 +411,14 @@
         moved=(home + width) * (cols + 2 * rest) * 2,
     )(t, place, cot_own, cot_sib, half, diag_a, diag_b, direct)[0]
     far = flip(send, "tensor", 2)
+    own, sib, left = call(
+        functools.partial(early_kernel, cap, part),
+        [((dest, 2 * cols), BF16), ((dest, 2 * cols), BF16), ((dest, 2 * width), BF16)],
+        [SMEM] * 3 + [VMEM] * 6,
+        flops=12 * dest * width * cols,
+        moved=12 * width * cols + dest * part * 4,
+    )(gone, t, tie(place, send), att, far_att, out_weight, *early)
+    other = flip(sib, "tensor", 1)
     own_late, sib_late = call(
         late_kernel,
         [((dest, cols + rest), BF16)] * 2,
@@ -397,19 +428,17 @@
     )(t, tie(place, send), left, out_weight, diag_a, diag_b, direct)
     other_late = flip(sib_late, "tensor", 1)
     projected = call(
-        join_kernel,
+        functools.partial(join_kernel, cap),
         [((dest, part), BF16)],
         [SMEM] * 2 + [VMEM] * 4,
+        [pltpu.VMEM((dest, part), BF16), pltpu.SemaphoreType.DMA((blocks + 1,))],
         moved=dest * part * 6,
+        out=ANY,
     )(t, place, own, other, own_late, other_late)[0]
 
-    grad_q, grad_k, grad_v = call(
-        backward_kernel,
-        [((home, width), BF16)] * 3,
-        [VMEM] * 6,
-        flops=800 * home * home * width,
-        moved=9 * home * width * 2,
-    )(queries, key_rows, value_rows, pt, near, far)
+    grad_q, grad_k, grad_v = gradients(
+        queries, key_rows, value_rows, pt, near, far, 800 * home * home * width
+    )
     return (projected, grad_q, grad_k, grad_v)
 
 
@@ -435,9 +464,8 @@
     )(gone, out_cotangent, back)[0]
     whole = lax.all_gather(cot, "tensor", axis=1, tiled=True)
     near = nt(whole, out_weight)
-    grad_q, grad_k, grad_v = call(
-        backward_kernel, [((home, width), BF16)] * 3, [VMEM] * 6
-    )(queries, key_rows, value_rows, pt, near, jnp.zeros((home, width), BF16))
+    none = jnp.zeros((home, width), BF16)
+    grad_q, grad_k, grad_v = gradients(queries, key_rows, value_rows, pt, near, none, 0)
     return (projected, grad_q, grad_k, grad_v)
 
 

time: 50.5 us -> 50 us (0.990)
  transfers between devices with their start and end apart: 14 -> 14, of which waited for: 5 -> 6; matrix products, arithmetic and copies ran while one was open for 0% -> 0% of each run, Pallas kernels for 26% -> 26%
where the time goes in v4:
time: 50 us; the launch traced here: 49.8 us
  waiting for transfers between devices  17.8 us (36%)
  starting transfers between devices  16.1 us (32%)
  Pallas kernels  15 us (30%)
  between operations  0.81 us (2%)
    ppermute x12, starting transfers between devices, flip(): return lax.ppermute(values, axis, [(i, i ^ by) for i in range(size)])  11.5 us
    ppermute x12, waiting for transfers between devices, flip(): return lax.ppermute(values, axis, [(i, i ^ by) for i in range(size)])  11.1 us
    ppermute x2, waiting for transfers between devices, shifted(): lax.ppermute(values, axis, [(i, (i + by) % size) for i in range(size)])  6.79 us
    ppermute x2, starting transfers between devices, shifted(): lax.ppermute(values, axis, [(i, (i + by) % size) for i in range(size)])  4.62 us
    pallas_call x1, Pallas kernels, attend(): call(functools.partial(forward_kernel, cap), [((1,), jnp.int32), ((cap, p...  2.53 us
    pallas_call x1, Pallas kernels, shards(): call(functools.partial(early_kernel, cap, part), [((dest, 2 * cols), BF16...  2.5 us
    pallas_call x1, Pallas kernels, gradients(): call(backward_kernel, [((home, width), BF16)] * 3, [VMEM] * 6, [pltpu.VME...  2.4 us
    pallas_call x1, Pallas kernels, shards(): call(own_kernel, [((home, width), F32)], [SMEM, VMEM, VMEM, VMEM], flops=...  1.4 us
  transfers between devices with their start and end apart: 14, of which 6 were waited for; matrix products, arithmetic and copies ran while one was open for 0% of the time, Pallas kernels for 26%

profile of v4, /device:TPU:0, one launch (start us, length us, event | category | flops | bytes accessed | tf_op | source)
XLA Modules:
  0.0 49.8 jit_solution(4622582333438100415)
XLA Ops:
  0.6 0.5 %collective-permute-start = (bf16[448,1536]{1,0:T(8,128)(2,1)}, bf16[448,1536]{1,0:T(8,128)(2,1)S(1)}, u32[]{:S(2)}, u32[]{:S(2)}) collective-permute-start(bf16[448,1536]{1,0:T(8,128)(2,1)} %refs_0_.1), channel_id=1, source_target_pairs={{0,1},{1,0},{2,3},{3,2},{4,5},{5,4},{6,7},{7,6},{8,9},{9,8},{10,11... | collective-permute-start | bytes 4128776 | tf_op jit(solution)/shard_map/ppermute | solution.py:332
  1.2 0.0 copy-start.1
  1.2 0.0 copy-start.2
  1.2 0.0 copy-start.3
  1.2 0.0 copy-start.4
  1.2 0.0 copy-start.5
  1.2 0.0 copy-start.6
  1.2 1.4 %shard_map.102 = (bf16[384,640]{1,0:T(8,128)(2,1)S(1)}, bf16[384,512]{1,0:T(8,128)(2,1)S(1)}) custom-call(s32[1]{0:T(128)} %bitcast.t.t_ref, s32[1]{0:T(128)} %bitcast.1.place.place_ref, bf16[384,6144]{1,0:T(8,128)(2,1)} %weight.7), custom_call_target="tpu_custom_call" | custom-call | tf_op jit(solution)/shard_map/pallas_call | solution.py:355
  2.5 2.6 %collective-permute-start.1 = (bf16[384,640]{1,0:T(8,128)(2,1)S(1)}, bf16[384,640]{1,0:T(8,128)(2,1)S(1)}, u32[]{:S(2)}, u32[]{:S(2)}) collective-permute-start(bf16[384,640]{1,0:T(8,128)(2,1)S(1)} %get-tuple-element.31), channel_id=1, source_target_pairs={{0,2},{1,3},{2,0},{3,1},{4,6},{5,7},{6,4},{7,5},{8,10},{9,11},{10,... | collective-permute-start | bytes 1474568 | tf_op jit(solution)/shard_map/ppermute | solution.py:332
  5.1 0.0 copy-done.1
  5.1 0.0 copy-done.2
  5.1 0.0 copy-done.3
  5.2 0.0 copy-done.4
  5.2 0.0 copy-done.5
  5.2 0.0 copy-done.6
  5.2 0.0 copy-start
  5.2 2.5 %shard_map.103 = (s32[1]{0:T(128)}, bf16[64,1536]{1,0:T(8,128)(2,1)S(1)}, bf16[448,384]{1,0:T(8,128)(2,1)S(1)}, bf16[64,384]{1,0:T(8,128)(2,1)S(1)}, bf16[3,384,384]{2,1,0:T(8,128)(2,1)S(1)}) custom-call(s32[1,384]{1,0:T(1,128)S(1)} %copy-done.5, s32[1,384]{1,0:T(1,128)S(1)} %copy-done.6, bf16[384,384]{1,0:T(8,128)(2,1)S(1)} %copy-done.2, ...), custom_call_target="tpu_custom_call" | custom-call | tf_op jit(solution)/shard_map/pallas_call | solution.py:55
  7.7 4.6 %collective-permute-start.2 = (bf16[64,1536]{1,0:T(8,128)(2,1)S(1)}, bf16[64,1536]{1,0:T(8,128)(2,1)S(1)}, u32[]{:S(2)}, u32[]{:S(2)}) collective-permute-start(bf16[64,1536]{1,0:T(8,128)(2,1)S(1)} %get-tuple-element.34), channel_id=1, source_target_pairs={{0,28},{4,0},{8,4},{12,8},{16,12},{20,16},{24,20},{28,24},{1,29},{... | collective-permute-start | bytes 589832 | tf_op jit(solution)/shard_map/ppermute | solution.py:337
  12.3 0.0 collective-permute-start.3
  12.3 6.8 %collective-permute-done.3 = bf16[64,384]{1,0:T(8,128)(2,1)S(1)} collective-permute-done((bf16[64,384]{1,0:T(8,128)(2,1)S(1)}, bf16[64,384]{1,0:T(8,128)(2,1)S(1)}, u32[]{:S(2)}, u32[]{:S(2)}) %collective-permute-start.3) | collective-permute-done | bytes 49184 | tf_op jit(solution)/shard_map/ppermute | solution.py:337
  19.1 0.0 collective-permute-done.2.refs_2_
  19.1 0.0 collective-permute-done.1.refs_0_
  19.1 0.0 collective-permute-start.6
  19.1 1.2 %collective-permute-start.5 = (bf16[384,640]{1,0:T(8,128)(2,1)S(1)}, bf16[384,640]{1,0:T(8,128)(2,1)S(1)}, u32[]{:S(2)}, u32[]{:S(2)}) collective-permute-start(bf16[384,640]{1,0:T(8,128)(2,1)S(1)} %collective-permute-done.1.refs_0_), channel_id=1, source_target_pairs={{0,4},{4,0},{8,12},{12,8},{16,20},{20,16},{24,28},{28,24},{1,5},{5... | collective-permute-start | bytes 1474568 | tf_op jit(solution)/shard_map/ppermute | solution.py:332
  20.4 1.6 %collective-permute-start.7 = (bf16[448,384]{1,0:T(8,128)(2,1)S(1)}, bf16[448,384]{1,0:T(8,128)(2,1)S(1)}, u32[]{:S(2)}, u32[]{:S(2)}) collective-permute-start(bf16[448,384]{1,0:T(8,128)(2,1)S(1)} %constant_dynamic-update-slice_fusion.att), channel_id=1, source_target_pairs={{0,2},{1,3},{2,0},{3,1},{4,6},{5,7},{6,4},{7,5},{8,10},{9,11},{10,... | collective-permute-start | bytes 1032200 | tf_op jit(solution)/shard_map/ppermute | solution.py:332
  21.9 0.0 collective-permute-start.4
  21.9 1.4 %collective-permute-done.4.refs_3_ = bf16[64,1536]{1,0:T(8,128)(2,1)S(1)} collective-permute-done((bf16[64,1536]{1,0:T(8,128)(2,1)S(1)}, bf16[64,1536]{1,0:T(8,128)(2,1)S(1)}, u32[]{:S(2)}, u32[]{:S(2)}) %collective-permute-start.4) | collective-permute-done | bytes 196640 | tf_op jit(solution)/shard_map/ppermute | solution.py:332
  23.4 0.5 %collective-permute-start.10 = (bf16[384,512]{1,0:T(8,128)(2,1)S(1)}, bf16[384,512]{1,0:T(8,128)(2,1)S(1)}, u32[]{:S(2)}, u32[]{:S(2)}) collective-permute-start(bf16[384,512]{1,0:T(8,128)(2,1)S(1)} %get-tuple-element.45), channel_id=1, source_target_pairs={{0,2},{1,3},{2,0},{3,1},{4,6},{5,7},{6,4},{7,5},{8,10},{9,11},{10,... | collective-permute-start | bytes 1179656 | tf_op jit(solution)/shard_map/ppermute | solution.py:332
  23.9 0.0 collective-permute-done.refs_1_
  23.9 0.8 %shard_map.104 = (bf16[384,1536]{1,0:T(8,128)(2,1)S(1)}, bf16[384,1536]{1,0:T(8,128)(2,1)S(1)}) custom-call(s32[1]{0:T(128)} %get-tuple-element.33.gone_ref.gone, bf16[448,1536]{1,0:T(8,128)(2,1)S(1)} %copy-done.1, bf16[448,1536]{1,0:T(8,128)(2,1)S(1)} %collective-permute-done.refs_1_, bf16[64,1536]{1,0:T(8,128)(2,1)S(1)} %collective-permute-done.2.refs_2_, ...), custom_call_target="tpu_custom_call" | custom-call | tf_op jit(solution)/shard_map/pallas_call | solution.py:379
  24.7 0.0 copy-done
  24.7 1.4 %shard_map.105.near = f32[384,384]{1,0:T(8,128)S(1)} custom-call(s32[1]{0:T(128)} %bitcast.t.t_ref, bf16[384,1536]{1,0:T(8,128)(2,1)S(1)} %get-tuple-element.37.cot_own, bf16[384,1536]{1,0:T(8,128)(2,1)S(1)} %get-tuple-element.38.cot_sib, bf16[384,6144]{1,0:T(8,128)(2,1)S(1)} %copy-done), custom_call_target="tpu_custom_call" | custom-call | flops 905969664 | bytes 4718592 | tf_op jit(solution)/shard_map/pallas_call | solution.py:385
  26.1 5.3 %collective-permute-done.7.far_att = bf16[448,384]{1,0:T(8,128)(2,1)S(1)} collective-permute-done((bf16[448,384]{1,0:T(8,128)(2,1)S(1)}, bf16[448,384]{1,0:T(8,128)(2,1)S(1)}, u32[]{:S(2)}, u32[]{:S(2)}) %collective-permute-start.7) | collective-permute-done | bytes 344096 | tf_op jit(solution)/shard_map/ppermute | solution.py:332
  31.4 0.0 collective-permute-done.6.refs_2_
  31.4 0.0 collective-permute-done.5.refs_1_
  31.5 1.4 %collective-permute-start.8 = (bf16[224,640]{1,0:T(8,128)(2,1)S(1)}, bf16[224,640]{1,0:T(8,128)(2,1)S(1)}, u32[]{:S(2)}, u32[]{:S(2)}) collective-permute-start(bf16[224,640]{1,0:T(8,128)(2,1)S(1)} %slice.6), channel_id=1, source_target_pairs={{0,8},{4,12},{8,0},{12,4},{16,24},{20,28},{24,16},{28,20},{1,9},{5... | collective-permute-start | bytes 860168 | tf_op jit(solution)/shard_map/ppermute | solution.py:332
  32.9 1.6 %collective-permute-start.9 = (bf16[160,640]{1,0:T(8,128)(2,1)S(1)}, bf16[160,640]{1,0:T(8,128)(2,1)S(1)}, u32[]{:S(2)}, u32[]{:S(2)}) collective-permute-start(bf16[160,640]{1,0:T(8,128)(2,1)S(1)} %slice.7), channel_id=1, source_target_pairs={{0,4},{4,0},{8,12},{12,8},{16,20},{20,16},{24,28},{28,24},{1,5},{5... | collective-permute-start | bytes 614408 | tf_op jit(solution)/shard_map/ppermute | solution.py:332
  34.5 1.0 %shard_map.106.part_sum = f32[384,384]{1,0:T(8,128)S(1)} custom-call(s32[1]{0:T(128)} %bitcast.t.t_ref, s32[1]{0:T(128)} %bitcast.1.place.place_ref, bf16[384,1536]{1,0:T(8,128)(2,1)S(1)} %get-tuple-element.37.cot_own, bf16[384,1536]{1,0:T(8,128)(2,1)S(1)} %get-tuple-element.38.cot_sib, bf16[384,640]{1,0:T(8,128)(2,1)S(1)} %collective-permute-done.1.refs_0_, ...), custom_call_target="tpu_custom_call" | custom-call | flops 566231040 | bytes 2949120 | tf_op jit(solution)/shard_map/pallas_call | solution.py:399
  35.5 2.4 %collective-permute-done.10.direct = bf16[384,512]{1,0:T(8,128)(2,1)S(1)} collective-permute-done((bf16[384,512]{1,0:T(8,128)(2,1)S(1)}, bf16[384,512]{1,0:T(8,128)(2,1)S(1)}, u32[]{:S(2)}, u32[]{:S(2)}) %collective-permute-start.10) | collective-permute-done | bytes 393248 | tf_op jit(solution)/shard_map/ppermute | solution.py:332
  37.9 0.8 %collective-permute-done.9.diag_b = bf16[160,640]{1,0:T(8,128)(2,1)S(1)} collective-permute-done((bf16[160,640]{1,0:T(8,128)(2,1)S(1)}, bf16[160,640]{1,0:T(8,128)(2,1)S(1)}, u32[]{:S(2)}, u32[]{:S(2)}) %collective-permute-start.9) | collective-permute-done | bytes 204832 | tf_op jit(solution)/shard_map/ppermute | solution.py:332
  38.7 0.0 collective-permute-done.8.diag_a
  38.7 0.7 %shard_map.107 = bf16[384,384]{1,0:T(8,128)(2,1)S(1)} custom-call(s32[1]{0:T(128)} %bitcast.t.t_ref, s32[1]{0:T(128)} %bitcast.1.place.place_ref, bf16[384,1536]{1,0:T(8,128)(2,1)S(1)} %get-tuple-element.37.cot_own, bf16[384,1536]{1,0:T(8,128)(2,1)S(1)} %get-tuple-element.38.cot_sib, f32[384,384]{1,0:T(8,128)S(1)} %shard_map.106.part_sum, ...), custom_call_target="tpu_custom_call" | custom-call | flops 339738624 | bytes 1769472 | tf_op jit(solution)/shard_map/pallas_call | solution.py:406
  39.4 1.5 %collective-permute-start.13 = (bf16[384,384]{1,0:T(8,128)(2,1)S(1)}, bf16[384,384]{1,0:T(8,128)(2,1)S(1)}, u32[]{:S(2)}, u32[]{:S(2)}) collective-permute-start(bf16[384,384]{1,0:T(8,128)(2,1)S(1)} %shard_map.107), channel_id=1, source_target_pairs={{0,2},{1,3},{2,0},{3,1},{4,6},{5,7},{6,4},{7,5},{8,10},{9,11},{10,... | collective-permute-start | bytes 884744 | tf_op jit(solution)/shard_map/ppermute | solution.py:332
  40.9 2.5 %shard_map.108 = (bf16[448,1280]{1,0:T(8,128)(2,1)S(1)}, bf16[448,1280]{1,0:T(8,128)(2,1)S(1)}, bf16[448,768]{1,0:T(8,128)(2,1)S(1)}) custom-call(s32[1]{0:T(128)} %get-tuple-element.33.gone_ref.gone, s32[1]{0:T(128)} %bitcast.t.t_ref, s32[1]{0:T(128)} %bitcast.1.place.place_ref, bf16[448,384]{1,0:T(8,128)(2,1)S(1)} %constant_dynamic-update-slice_fusion.att, ...), custom_call_target="tpu_custom_call" | custom-call | flops 1321205760 | bytes 5701632 | tf_op jit(solution)/shard_map/pallas_call | solution.py:414
  43.4 1.1 %shard_map.109 = (bf16[448,896]{1,0:T(8,128)(2,1)S(1)}, bf16[448,896]{1,0:T(8,128)(2,1)S(1)}) custom-call(s32[1]{0:T(128)} %bitcast.t.t_ref, s32[1]{0:T(128)} %bitcast.1.place.place_ref, bf16[448,768]{1,0:T(8,128)(2,1)S(1)} %get-tuple-element.50.left, bf16[384,6144]{1,0:T(8,128)(2,1)S(1)} %copy-done, bf16[224,640]{1,0:T(8,128)(2,1)S(1)} %collective-permute-done.8.diag_a, ...), custom_call_target="tpu_custom_call" | custom-call | flops 792723456 | bytes 3145728 | tf_op jit(solution)/shard_map/pallas_call | solution.py:422
  44.5 0.1 collective-permute-start.12
  44.6 0.5 collective-permute-start.11
  45.1 1.1 %collective-permute-done.13.far = bf16[384,384]{1,0:T(8,128)(2,1)S(1)} collective-permute-done((bf16[384,384]{1,0:T(8,128)(2,1)S(1)}, bf16[384,384]{1,0:T(8,128)(2,1)S(1)}, u32[]{:S(2)}, u32[]{:S(2)}) %collective-permute-start.13) | collective-permute-done | bytes 294944 | tf_op jit(solution)/shard_map/ppermute | solution.py:332
  46.2 2.4 %shard_map.111 = (bf16[384,384]{1,0:T(8,128)(2,1)}, bf16[384,384]{1,0:T(8,128)(2,1)}, bf16[384,384]{1,0:T(8,128)(2,1)}) custom-call(bf16[384,384]{1,0:T(8,128)(2,1)S(1)} %copy-done.2, bf16[384,384]{1,0:T(8,128)(2,1)S(1)} %copy-done.3, bf16[384,384]{1,0:T(8,128)(2,1)S(1)} %copy-done.4, bf16[3,384,384]{2,1,0:T(8,128)(2,1)S(1)} %get-tuple-element.53.pt, ...), custom_call_target="tpu_custom_call" | custom-call | flops 45298483200 | bytes 2654208 | tf_op jit(solution)/shard_map/pallas_call | solution.py:318
  48.6 0.0 collective-permute-done.12.other_late
  48.6 0.0 collective-permute-done.11.other
  48.6 1.2 %shard_map.110 = bf16[448,1536]{1,0:T(8,128)(2,1)} custom-call(s32[1]{0:T(128)} %bitcast.t.t_ref, s32[1]{0:T(128)} %bitcast.1.place.place_ref, bf16[448,1280]{1,0:T(8,128)(2,1)S(1)} %get-tuple-element.48.own, bf16[448,1280]{1,0:T(8,128)(2,1)S(1)} %collective-permute-done.11.other, bf16[448,896]{1,0:T(8,128)(2,1)S(1)} %get-tuple-element.51.own_late, ...), custom_call_target="tpu_custom_call" | custom-call | bytes 4128768 | tf_op jit(solution)/shard_map/pallas_call | solution.py:430
  (3 shorter events, 0.1 us)
Async XLA Ops:
  0.6 23.3 %collective-permute-start = (bf16[448,1536]{1,0:T(8,128)(2,1)}, bf16[448,1536]{1,0:T(8,128)(2,1)S(1)}, u32[]{:S(2)}, u32[]{:S(2)}) collective-permute-start(bf16[448,1536]{1,0:T(8,128)(2,1)} %refs_0_.1), channel_id=1, source_target_pairs={{0,1},{1,0},{2,3},{3,2},{4,5},{5,4},{6,7},{7,6},{8,9},{9,8},{10,11... | collective-permute-start | bytes 4128776 | tf_op jit(solution)/shard_map/ppermute | solution.py:332
  1.2 4.0 %copy-start.1 = (bf16[448,1536]{1,0:T(8,128)(2,1)S(1)}, bf16[448,1536]{1,0:T(8,128)(2,1)}, u32[]{:S(2)}) copy-start(bf16[448,1536]{1,0:T(8,128)(2,1)} %refs_0_.1) | copy-start | bytes 4128772
  1.2 4.0 %copy-start.2 = (bf16[384,384]{1,0:T(8,128)(2,1)S(1)}, bf16[384,384]{1,0:T(8,128)(2,1)}, u32[]{:S(2)}) copy-start(bf16[384,384]{1,0:T(8,128)(2,1)} %q.3) | copy-start | bytes 884740
  1.2 4.0 %copy-start.3 = (bf16[384,384]{1,0:T(8,128)(2,1)S(1)}, bf16[384,384]{1,0:T(8,128)(2,1)}, u32[]{:S(2)}) copy-start(bf16[384,384]{1,0:T(8,128)(2,1)} %k.3) | copy-start | bytes 884740
  1.2 4.0 %copy-start.4 = (bf16[384,384]{1,0:T(8,128)(2,1)S(1)}, bf16[384,384]{1,0:T(8,128)(2,1)}, u32[]{:S(2)}) copy-start(bf16[384,384]{1,0:T(8,128)(2,1)} %v.3) | copy-start | bytes 884740
  1.2 4.0 %copy-start.5 = (s32[1,384]{1,0:T(1,128)S(1)}, s32[1,384]{1,0:T(1,128)}, u32[]{:S(2)}) copy-start(s32[1,384]{1,0:T(1,128)} %seg) | copy-start | bytes 4612
  1.2 4.0 %copy-start.6 = (s32[1,384]{1,0:T(1,128)S(1)}, s32[1,384]{1,0:T(1,128)}, u32[]{:S(2)}) copy-start(s32[1,384]{1,0:T(1,128)} %flags.1) | copy-start | bytes 4612
  2.5 16.6 %collective-permute-start.1 = (bf16[384,640]{1,0:T(8,128)(2,1)S(1)}, bf16[384,640]{1,0:T(8,128)(2,1)S(1)}, u32[]{:S(2)}, u32[]{:S(2)}) collective-permute-start(bf16[384,640]{1,0:T(8,128)(2,1)S(1)} %get-tuple-element.31), channel_id=1, source_target_pairs={{0,2},{1,3},{2,0},{3,1},{4,6},{5,7},{6,4},{7,5},{8,10},{9,11},{10,... | collective-permute-start | bytes 1474568 | tf_op jit(solution)/shard_map/ppermute | solution.py:332
  5.2 19.6 %copy-start = (bf16[384,6144]{1,0:T(8,128)(2,1)S(1)}, bf16[384,6144]{1,0:T(8,128)(2,1)}, u32[]{:S(2)}) copy-start(bf16[384,6144]{1,0:T(8,128)(2,1)} %weight.7) | copy-start | bytes 14155780
  7.7 11.4 %collective-permute-start.2 = (bf16[64,1536]{1,0:T(8,128)(2,1)S(1)}, bf16[64,1536]{1,0:T(8,128)(2,1)S(1)}, u32[]{:S(2)}, u32[]{:S(2)}) collective-permute-start(bf16[64,1536]{1,0:T(8,128)(2,1)S(1)} %get-tuple-element.34), channel_id=1, source_target_pairs={{0,28},{4,0},{8,4},{12,8},{16,12},{20,16},{24,20},{28,24},{1,29},{... | collective-permute-start | bytes 589832 | tf_op jit(solution)/shard_map/ppermute | solution.py:337
  12.3 6.8 %collective-permute-start.3 = (bf16[64,384]{1,0:T(8,128)(2,1)S(1)}, bf16[64,384]{1,0:T(8,128)(2,1)S(1)}, u32[]{:S(2)}, u32[]{:S(2)}) collective-permute-start(bf16[64,384]{1,0:T(8,128)(2,1)S(1)} %get-tuple-element.35), channel_id=1, source_target_pairs={{0,4},{4,8},{8,12},{12,16},{16,20},{20,24},{24,28},{28,0},{1,5},{5... | collective-permute-start | bytes 147464 | tf_op jit(solution)/shard_map/ppermute | solution.py:337
  19.1 12.3 %collective-permute-start.6 = (bf16[384,640]{1,0:T(8,128)(2,1)S(1)}, bf16[384,640]{1,0:T(8,128)(2,1)S(1)}, u32[]{:S(2)}, u32[]{:S(2)}) collective-permute-start(bf16[384,640]{1,0:T(8,128)(2,1)S(1)} %collective-permute-done.1.refs_0_), channel_id=1, source_target_pairs={{0,8},{4,12},{8,0},{12,4},{16,24},{20,28},{24,16},{28,20},{1,9},{5... | collective-permute-start | bytes 1474568 | tf_op jit(solution)/shard_map/ppermute | solution.py:332
  19.1 12.3 %collective-permute-start.5 = (bf16[384,640]{1,0:T(8,128)(2,1)S(1)}, bf16[384,640]{1,0:T(8,128)(2,1)S(1)}, u32[]{:S(2)}, u32[]{:S(2)}) collective-permute-start(bf16[384,640]{1,0:T(8,128)(2,1)S(1)} %collective-permute-done.1.refs_0_), channel_id=1, source_target_pairs={{0,4},{4,0},{8,12},{12,8},{16,20},{20,16},{24,28},{28,24},{1,5},{5... | collective-permute-start | bytes 1474568 | tf_op jit(solution)/shard_map/ppermute | solution.py:332
  20.4 11.1 %collective-permute-start.7 = (bf16[448,384]{1,0:T(8,128)(2,1)S(1)}, bf16[448,384]{1,0:T(8,128)(2,1)S(1)}, u32[]{:S(2)}, u32[]{:S(2)}) collective-permute-start(bf16[448,384]{1,0:T(8,128)(2,1)S(1)} %constant_dynamic-update-slice_fusion.att), channel_id=1, source_target_pairs={{0,2},{1,3},{2,0},{3,1},{4,6},{5,7},{6,4},{7,5},{8,10},{9,11},{10,... | collective-permute-start | bytes 1032200 | tf_op jit(solution)/shard_map/ppermute | solution.py:332
  21.9 1.4 %collective-permute-start.4 = (bf16[64,1536]{1,0:T(8,128)(2,1)S(1)}, bf16[64,1536]{1,0:T(8,128)(2,1)S(1)}, u32[]{:S(2)}, u32[]{:S(2)}) collective-permute-start(bf16[64,1536]{1,0:T(8,128)(2,1)S(1)} %collective-permute-done.2.refs_2_), channel_id=1, source_target_pairs={{0,1},{1,0},{2,3},{3,2},{4,5},{5,4},{6,7},{7,6},{8,9},{9,8},{10,11... | collective-permute-start | bytes 589832 | tf_op jit(solution)/shard_map/ppermute | solution.py:332
  23.4 14.6 %collective-permute-start.10 = (bf16[384,512]{1,0:T(8,128)(2,1)S(1)}, bf16[384,512]{1,0:T(8,128)(2,1)S(1)}, u32[]{:S(2)}, u32[]{:S(2)}) collective-permute-start(bf16[384,512]{1,0:T(8,128)(2,1)S(1)} %get-tuple-element.45), channel_id=1, source_target_pairs={{0,2},{1,3},{2,0},{3,1},{4,6},{5,7},{6,4},{7,5},{8,10},{9,11},{10,... | collective-permute-start | bytes 1179656 | tf_op jit(solution)/shard_map/ppermute | solution.py:332
  31.5 7.3 %collective-permute-start.8 = (bf16[224,640]{1,0:T(8,128)(2,1)S(1)}, bf16[224,640]{1,0:T(8,128)(2,1)S(1)}, u32[]{:S(2)}, u32[]{:S(2)}) collective-permute-start(bf16[224,640]{1,0:T(8,128)(2,1)S(1)} %slice.6), channel_id=1, source_target_pairs={{0,8},{4,12},{8,0},{12,4},{16,24},{20,28},{24,16},{28,20},{1,9},{5... | collective-permute-start | bytes 860168 | tf_op jit(solution)/shard_map/ppermute | solution.py:332
  32.9 5.8 %collective-permute-start.9 = (bf16[160,640]{1,0:T(8,128)(2,1)S(1)}, bf16[160,640]{1,0:T(8,128)(2,1)S(1)}, u32[]{:S(2)}, u32[]{:S(2)}) collective-permute-start(bf16[160,640]{1,0:T(8,128)(2,1)S(1)} %slice.7), channel_id=1, source_target_pairs={{0,4},{4,0},{8,12},{12,8},{16,20},{20,16},{24,28},{28,24},{1,5},{5... | collective-permute-start | bytes 614408 | tf_op jit(solution)/shard_map/ppermute | solution.py:332
  39.4 6.8 %collective-permute-start.13 = (bf16[384,384]{1,0:T(8,128)(2,1)S(1)}, bf16[384,384]{1,0:T(8,128)(2,1)S(1)}, u32[]{:S(2)}, u32[]{:S(2)}) collective-permute-start(bf16[384,384]{1,0:T(8,128)(2,1)S(1)} %shard_map.107), channel_id=1, source_target_pairs={{0,2},{1,3},{2,0},{3,1},{4,6},{5,7},{6,4},{7,5},{8,10},{9,11},{10,... | collective-permute-start | bytes 884744 | tf_op jit(solution)/shard_map/ppermute | solution.py:332
  44.5 4.1 %collective-permute-start.12 = (bf16[448,896]{1,0:T(8,128)(2,1)S(1)}, bf16[448,896]{1,0:T(8,128)(2,1)S(1)}, u32[]{:S(2)}, u32[]{:S(2)}) collective-permute-start(bf16[448,896]{1,0:T(8,128)(2,1)S(1)} %get-tuple-element.52), channel_id=1, source_target_pairs={{0,1},{1,0},{2,3},{3,2},{4,5},{5,4},{6,7},{7,6},{8,9},{9,8},{10,11... | collective-permute-start | bytes 2408456 | tf_op jit(solution)/shard_map/ppermute | solution.py:332
  44.6 4.0 %collective-permute-start.11 = (bf16[448,1280]{1,0:T(8,128)(2,1)S(1)}, bf16[448,1280]{1,0:T(8,128)(2,1)S(1)}, u32[]{:S(2)}, u32[]{:S(2)}) collective-permute-start(bf16[448,1280]{1,0:T(8,128)(2,1)S(1)} %get-tuple-element.49), channel_id=1, source_target_pairs={{0,1},{1,0},{2,3},{3,2},{4,5},{5,4},{6,7},{7,6},{8,9},{9,8},{10,11... | collective-permute-start | bytes 3440648 | tf_op jit(solution)/shard_map/ppermute | solution.py:332

commit v5 on v4

--- a/solution.py
+++ b/solution.py
@@ -390,7 +390,8 @@
         moved=(home + width) * part * 4,
     )(t, cot_own, cot_sib, out_weight)[0]
 
-    by_y, by_z, near, far_att = lax.optimization_barrier((by_y, by_z, near, far_att))
+    by_y, near, far_att = lax.optimization_barrier((by_y, near, far_att))
+    by_z = tie(by_z, near)
     rows_a = width * 7 // 12 // 32 * 32
     diag_a = flip(by_y[:rows_a], "dp", 2)
     diag_b = flip(by_z[rows_a:], "dp", 1)

time: 50 us -> 49.6 us (level)
  transfers between devices with their start and end apart: 14 -> 14, of which waited for: 6 -> 6; matrix products, arithmetic and copies ran while one was open for 0% -> 0% of each run, Pallas kernels for 26% -> 27%
where the time goes in v5:
time: 49.6 us; the launch traced here: 49.4 us
  waiting for transfers between devices  17.5 us (35%)
  starting transfers between devices  16 us (32%)
  Pallas kernels  15 us (30%)
  between operations  0.81 us (2%)
    ppermute x12, starting transfers between devices, flip(): return lax.ppermute(values, axis, [(i, i ^ by) for i in range(size)])  11.4 us
    ppermute x12, waiting for transfers between devices, flip(): return lax.ppermute(values, axis, [(i, i ^ by) for i in range(size)])  10.8 us
    ppermute x2, waiting for transfers between devices, shifted(): lax.ppermute(values, axis, [(i, (i + by) % size) for i in range(size)])  6.79 us
    ppermute x2, starting transfers between devices, shifted(): lax.ppermute(values, axis, [(i, (i + by) % size) for i in range(size)])  4.61 us
    pallas_call x1, Pallas kernels, attend(): call(functools.partial(forward_kernel, cap), [((1,), jnp.int32), ((cap, p...  2.53 us
    pallas_call x1, Pallas kernels, shards(): call(functools.partial(early_kernel, cap, part), [((dest, 2 * cols), BF16...  2.5 us
    pallas_call x1, Pallas kernels, gradients(): call(backward_kernel, [((home, width), BF16)] * 3, [VMEM] * 6, [pltpu.VME...  2.4 us
    pallas_call x1, Pallas kernels, shards(): call(own_kernel, [((home, width), F32)], [SMEM, VMEM, VMEM, VMEM], flops=...  1.41 us
  transfers between devices with their start and end apart: 14, of which 6 were waited for; matrix products, arithmetic and copies ran while one was open for 0% of the time, Pallas kernels for 27%

profile of v5, /device:TPU:0, one launch (start us, length us, event | category | flops | bytes accessed | tf_op | source)
XLA Modules:
  0.0 49.4 jit_solution(11810699537157301881)
XLA Ops:
  0.6 0.5 %collective-permute-start = (bf16[448,1536]{1,0:T(8,128)(2,1)}, bf16[448,1536]{1,0:T(8,128)(2,1)S(1)}, u32[]{:S(2)}, u32[]{:S(2)}) collective-permute-start(bf16[448,1536]{1,0:T(8,128)(2,1)} %refs_0_.1), channel_id=1, source_target_pairs={{0,1},{1,0},{2,3},{3,2},{4,5},{5,4},{6,7},{7,6},{8,9},{9,8},{10,11... | collective-permute-start | bytes 4128776 | tf_op jit(solution)/shard_map/ppermute | solution.py:332
  1.2 0.0 copy-start.1
  1.2 0.0 copy-start.2
  1.2 0.0 copy-start.3
  1.2 0.0 copy-start.4
  1.2 0.0 copy-start.5
  1.2 0.0 copy-start.6
  1.2 1.4 %shard_map.102 = (bf16[384,640]{1,0:T(8,128)(2,1)S(1)}, bf16[384,512]{1,0:T(8,128)(2,1)S(1)}) custom-call(s32[1]{0:T(128)} %bitcast.t.t_ref, s32[1]{0:T(128)} %bitcast.1.place.place_ref, bf16[384,6144]{1,0:T(8,128)(2,1)} %weight.7), custom_call_target="tpu_custom_call" | custom-call | tf_op jit(solution)/shard_map/pallas_call | solution.py:355
  2.5 2.6 %collective-permute-start.1 = (bf16[384,640]{1,0:T(8,128)(2,1)S(1)}, bf16[384,640]{1,0:T(8,128)(2,1)S(1)}, u32[]{:S(2)}, u32[]{:S(2)}) collective-permute-start(bf16[384,640]{1,0:T(8,128)(2,1)S(1)} %get-tuple-element.31), channel_id=1, source_target_pairs={{0,2},{1,3},{2,0},{3,1},{4,6},{5,7},{6,4},{7,5},{8,10},{9,11},{10,... | collective-permute-start | bytes 1474568 | tf_op jit(solution)/shard_map/ppermute | solution.py:332
  5.1 0.0 copy-done.1
  5.1 0.0 copy-done.2
  5.1 0.0 copy-done.3
  5.2 0.0 copy-done.4
  5.2 0.0 copy-done.5
  5.2 0.0 copy-done.6
  5.2 0.0 copy-start
  5.2 2.5 %shard_map.103 = (s32[1]{0:T(128)}, bf16[64,1536]{1,0:T(8,128)(2,1)S(1)}, bf16[448,384]{1,0:T(8,128)(2,1)S(1)}, bf16[64,384]{1,0:T(8,128)(2,1)S(1)}, bf16[3,384,384]{2,1,0:T(8,128)(2,1)S(1)}) custom-call(s32[1,384]{1,0:T(1,128)S(1)} %copy-done.5, s32[1,384]{1,0:T(1,128)S(1)} %copy-done.6, bf16[384,384]{1,0:T(8,128)(2,1)S(1)} %copy-done.2, ...), custom_call_target="tpu_custom_call" | custom-call | tf_op jit(solution)/shard_map/pallas_call | solution.py:55
  7.7 4.6 %collective-permute-start.2 = (bf16[64,1536]{1,0:T(8,128)(2,1)S(1)}, bf16[64,1536]{1,0:T(8,128)(2,1)S(1)}, u32[]{:S(2)}, u32[]{:S(2)}) collective-permute-start(bf16[64,1536]{1,0:T(8,128)(2,1)S(1)} %get-tuple-element.34), channel_id=1, source_target_pairs={{0,28},{4,0},{8,4},{12,8},{16,12},{20,16},{24,20},{28,24},{1,29},{... | collective-permute-start | bytes 589832 | tf_op jit(solution)/shard_map/ppermute | solution.py:337
  12.3 0.0 collective-permute-start.3
  12.3 6.8 %collective-permute-done.3 = bf16[64,384]{1,0:T(8,128)(2,1)S(1)} collective-permute-done((bf16[64,384]{1,0:T(8,128)(2,1)S(1)}, bf16[64,384]{1,0:T(8,128)(2,1)S(1)}, u32[]{:S(2)}, u32[]{:S(2)}) %collective-permute-start.3) | collective-permute-done | bytes 49184 | tf_op jit(solution)/shard_map/ppermute | solution.py:337
  19.1 0.0 collective-permute-done.2.refs_2_
  19.1 0.0 collective-permute-done.1.refs_0_
  19.1 0.0 collective-permute-start.5
  19.1 1.2 %collective-permute-start.7 = (bf16[384,640]{1,0:T(8,128)(2,1)S(1)}, bf16[384,640]{1,0:T(8,128)(2,1)S(1)}, u32[]{:S(2)}, u32[]{:S(2)}) collective-permute-start(bf16[384,640]{1,0:T(8,128)(2,1)S(1)} %collective-permute-done.1.refs_0_), channel_id=1, source_target_pairs={{0,8},{4,12},{8,0},{12,4},{16,24},{20,28},{24,16},{28,20},{1,9},{5... | collective-permute-start | bytes 1474568 | tf_op jit(solution)/shard_map/ppermute | solution.py:332
  20.4 1.6 %collective-permute-start.6 = (bf16[448,384]{1,0:T(8,128)(2,1)S(1)}, bf16[448,384]{1,0:T(8,128)(2,1)S(1)}, u32[]{:S(2)}, u32[]{:S(2)}) collective-permute-start(bf16[448,384]{1,0:T(8,128)(2,1)S(1)} %constant_dynamic-update-slice_fusion.att), channel_id=1, source_target_pairs={{0,2},{1,3},{2,0},{3,1},{4,6},{5,7},{6,4},{7,5},{8,10},{9,11},{10,... | collective-permute-start | bytes 1032200 | tf_op jit(solution)/shard_map/ppermute | solution.py:332
  21.9 0.0 collective-permute-start.4
  21.9 1.4 %collective-permute-done.4.refs_3_ = bf16[64,1536]{1,0:T(8,128)(2,1)S(1)} collective-permute-done((bf16[64,1536]{1,0:T(8,128)(2,1)S(1)}, bf16[64,1536]{1,0:T(8,128)(2,1)S(1)}, u32[]{:S(2)}, u32[]{:S(2)}) %collective-permute-start.4) | collective-permute-done | bytes 196640 | tf_op jit(solution)/shard_map/ppermute | solution.py:332
  23.4 0.5 %collective-permute-start.10 = (bf16[384,512]{1,0:T(8,128)(2,1)S(1)}, bf16[384,512]{1,0:T(8,128)(2,1)S(1)}, u32[]{:S(2)}, u32[]{:S(2)}) collective-permute-start(bf16[384,512]{1,0:T(8,128)(2,1)S(1)} %get-tuple-element.46), channel_id=1, source_target_pairs={{0,2},{1,3},{2,0},{3,1},{4,6},{5,7},{6,4},{7,5},{8,10},{9,11},{10,... | collective-permute-start | bytes 1179656 | tf_op jit(solution)/shard_map/ppermute | solution.py:332
  23.9 0.0 collective-permute-done.refs_1_
  23.9 0.8 %shard_map.104 = (bf16[384,1536]{1,0:T(8,128)(2,1)S(1)}, bf16[384,1536]{1,0:T(8,128)(2,1)S(1)}) custom-call(s32[1]{0:T(128)} %get-tuple-element.33.gone_ref.gone, bf16[448,1536]{1,0:T(8,128)(2,1)S(1)} %copy-done.1, bf16[448,1536]{1,0:T(8,128)(2,1)S(1)} %collective-permute-done.refs_1_, bf16[64,1536]{1,0:T(8,128)(2,1)S(1)} %collective-permute-done.2.refs_2_, ...), custom_call_target="tpu_custom_call" | custom-call | tf_op jit(solution)/shard_map/pallas_call | solution.py:379
  24.7 0.0 copy-done
  24.7 1.4 %shard_map.105.near = f32[384,384]{1,0:T(8,128)S(1)} custom-call(s32[1]{0:T(128)} %bitcast.t.t_ref, bf16[384,1536]{1,0:T(8,128)(2,1)S(1)} %get-tuple-element.37.cot_own, bf16[384,1536]{1,0:T(8,128)(2,1)S(1)} %get-tuple-element.38.cot_sib, bf16[384,6144]{1,0:T(8,128)(2,1)S(1)} %copy-done), custom_call_target="tpu_custom_call" | custom-call | flops 905969664 | bytes 4718592 | tf_op jit(solution)/shard_map/pallas_call | solution.py:385
  26.1 5.3 %collective-permute-done.6.far_att = bf16[448,384]{1,0:T(8,128)(2,1)S(1)} collective-permute-done((bf16[448,384]{1,0:T(8,128)(2,1)S(1)}, bf16[448,384]{1,0:T(8,128)(2,1)S(1)}, u32[]{:S(2)}, u32[]{:S(2)}) %collective-permute-start.6) | collective-permute-done | bytes 344096 | tf_op jit(solution)/shard_map/ppermute | solution.py:332
  31.4 0.0 collective-permute-done.5.refs_1_
  31.5 1.0 %collective-permute-start.8 = (bf16[224,640]{1,0:T(8,128)(2,1)S(1)}, bf16[224,640]{1,0:T(8,128)(2,1)S(1)}, u32[]{:S(2)}, u32[]{:S(2)}) collective-permute-start(bf16[224,640]{1,0:T(8,128)(2,1)S(1)} %slice.6), channel_id=1, source_target_pairs={{0,8},{4,12},{8,0},{12,4},{16,24},{20,28},{24,16},{28,20},{1,9},{5... | collective-permute-start | bytes 860168 | tf_op jit(solution)/shard_map/ppermute | solution.py:332
  32.4 0.0 collective-permute-done.7.refs_2_
  32.4 2.0 %collective-permute-start.9 = (bf16[160,640]{1,0:T(8,128)(2,1)S(1)}, bf16[160,640]{1,0:T(8,128)(2,1)S(1)}, u32[]{:S(2)}, u32[]{:S(2)}) collective-permute-start(bf16[160,640]{1,0:T(8,128)(2,1)S(1)} %slice.7), channel_id=1, source_target_pairs={{0,4},{4,0},{8,12},{12,8},{16,20},{20,16},{24,28},{28,24},{1,5},{5... | collective-permute-start | bytes 614408 | tf_op jit(solution)/shard_map/ppermute | solution.py:332
  34.5 1.0 %shard_map.106.part_sum = f32[384,384]{1,0:T(8,128)S(1)} custom-call(s32[1]{0:T(128)} %bitcast.t.t_ref, s32[1]{0:T(128)} %bitcast.1.place.place_ref, bf16[384,1536]{1,0:T(8,128)(2,1)S(1)} %get-tuple-element.37.cot_own, bf16[384,1536]{1,0:T(8,128)(2,1)S(1)} %get-tuple-element.38.cot_sib, bf16[384,640]{1,0:T(8,128)(2,1)S(1)} %collective-permute-done.1.refs_0_, ...), custom_call_target="tpu_custom_call" | custom-call | flops 566231040 | bytes 2949120 | tf_op jit(solution)/shard_map/pallas_call | solution.py:400
  35.5 2.5 %collective-permute-done.10.direct = bf16[384,512]{1,0:T(8,128)(2,1)S(1)} collective-permute-done((bf16[384,512]{1,0:T(8,128)(2,1)S(1)}, bf16[384,512]{1,0:T(8,128)(2,1)S(1)}, u32[]{:S(2)}, u32[]{:S(2)}) %collective-permute-start.10) | collective-permute-done | bytes 393248 | tf_op jit(solution)/shard_map/ppermute | solution.py:332
  37.9 0.3 collective-permute-done.9.diag_b
  38.3 0.0 collective-permute-done.8.diag_a
  38.3 0.7 %shard_map.107 = bf16[384,384]{1,0:T(8,128)(2,1)S(1)} custom-call(s32[1]{0:T(128)} %bitcast.t.t_ref, s32[1]{0:T(128)} %bitcast.1.place.place_ref, bf16[384,1536]{1,0:T(8,128)(2,1)S(1)} %get-tuple-element.37.cot_own, bf16[384,1536]{1,0:T(8,128)(2,1)S(1)} %get-tuple-element.38.cot_sib, f32[384,384]{1,0:T(8,128)S(1)} %shard_map.106.part_sum, ...), custom_call_target="tpu_custom_call" | custom-call | flops 339738624 | bytes 1769472 | tf_op jit(solution)/shard_map/pallas_call | solution.py:407
  38.9 1.4 %collective-permute-start.13 = (bf16[384,384]{1,0:T(8,128)(2,1)S(1)}, bf16[384,384]{1,0:T(8,128)(2,1)S(1)}, u32[]{:S(2)}, u32[]{:S(2)}) collective-permute-start(bf16[384,384]{1,0:T(8,128)(2,1)S(1)} %shard_map.107), channel_id=1, source_target_pairs={{0,2},{1,3},{2,0},{3,1},{4,6},{5,7},{6,4},{7,5},{8,10},{9,11},{10,... | collective-permute-start | bytes 884744 | tf_op jit(solution)/shard_map/ppermute | solution.py:332
  40.4 2.5 %shard_map.108 = (bf16[448,1280]{1,0:T(8,128)(2,1)S(1)}, bf16[448,1280]{1,0:T(8,128)(2,1)S(1)}, bf16[448,768]{1,0:T(8,128)(2,1)S(1)}) custom-call(s32[1]{0:T(128)} %get-tuple-element.33.gone_ref.gone, s32[1]{0:T(128)} %bitcast.t.t_ref, s32[1]{0:T(128)} %bitcast.1.place.place_ref, bf16[448,384]{1,0:T(8,128)(2,1)S(1)} %constant_dynamic-update-slice_fusion.att, ...), custom_call_target="tpu_custom_call" | custom-call | flops 1321205760 | bytes 5701632 | tf_op jit(solution)/shard_map/pallas_call | solution.py:415
  42.9 1.1 %shard_map.109 = (bf16[448,896]{1,0:T(8,128)(2,1)S(1)}, bf16[448,896]{1,0:T(8,128)(2,1)S(1)}) custom-call(s32[1]{0:T(128)} %bitcast.t.t_ref, s32[1]{0:T(128)} %bitcast.1.place.place_ref, bf16[448,768]{1,0:T(8,128)(2,1)S(1)} %get-tuple-element.51.left, bf16[384,6144]{1,0:T(8,128)(2,1)S(1)} %copy-done, bf16[224,640]{1,0:T(8,128)(2,1)S(1)} %collective-permute-done.8.diag_a, ...), custom_call_target="tpu_custom_call" | custom-call | flops 792723456 | bytes 3145728 | tf_op jit(solution)/shard_map/pallas_call | solution.py:423
  44.0 0.1 collective-permute-start.12
  44.1 0.5 %collective-permute-start.11 = (bf16[448,1280]{1,0:T(8,128)(2,1)S(1)}, bf16[448,1280]{1,0:T(8,128)(2,1)S(1)}, u32[]{:S(2)}, u32[]{:S(2)}) collective-permute-start(bf16[448,1280]{1,0:T(8,128)(2,1)S(1)} %get-tuple-element.50), channel_id=1, source_target_pairs={{0,1},{1,0},{2,3},{3,2},{4,5},{5,4},{6,7},{7,6},{8,9},{9,8},{10,11... | collective-permute-start | bytes 3440648 | tf_op jit(solution)/shard_map/ppermute | solution.py:332
  44.6 1.2 %collective-permute-done.13.far = bf16[384,384]{1,0:T(8,128)(2,1)S(1)} collective-permute-done((bf16[384,384]{1,0:T(8,128)(2,1)S(1)}, bf16[384,384]{1,0:T(8,128)(2,1)S(1)}, u32[]{:S(2)}, u32[]{:S(2)}) %collective-permute-start.13) | collective-permute-done | bytes 294944 | tf_op jit(solution)/shard_map/ppermute | solution.py:332
  45.8 2.4 %shard_map.111 = (bf16[384,384]{1,0:T(8,128)(2,1)}, bf16[384,384]{1,0:T(8,128)(2,1)}, bf16[384,384]{1,0:T(8,128)(2,1)}) custom-call(bf16[384,384]{1,0:T(8,128)(2,1)S(1)} %copy-done.2, bf16[384,384]{1,0:T(8,128)(2,1)S(1)} %copy-done.3, bf16[384,384]{1,0:T(8,128)(2,1)S(1)} %copy-done.4, bf16[3,384,384]{2,1,0:T(8,128)(2,1)S(1)} %get-tuple-element.54.pt, ...), custom_call_target="tpu_custom_call" | custom-call | flops 45298483200 | bytes 2654208 | tf_op jit(solution)/shard_map/pallas_call | solution.py:318
  48.2 0.0 collective-permute-done.12.other_late
  48.2 0.0 collective-permute-done.11.other
  48.2 1.2 %shard_map.110 = bf16[448,1536]{1,0:T(8,128)(2,1)} custom-call(s32[1]{0:T(128)} %bitcast.t.t_ref, s32[1]{0:T(128)} %bitcast.1.place.place_ref, bf16[448,1280]{1,0:T(8,128)(2,1)S(1)} %get-tuple-element.49.own, bf16[448,1280]{1,0:T(8,128)(2,1)S(1)} %collective-permute-done.11.other, bf16[448,896]{1,0:T(8,128)(2,1)S(1)} %get-tuple-element.52.own_late, ...), custom_call_target="tpu_custom_call" | custom-call | bytes 4128768 | tf_op jit(solution)/shard_map/pallas_call | solution.py:431
  (3 shorter events, 0.1 us)
Async XLA Ops:
  0.6 23.3 %collective-permute-start = (bf16[448,1536]{1,0:T(8,128)(2,1)}, bf16[448,1536]{1,0:T(8,128)(2,1)S(1)}, u32[]{:S(2)}, u32[]{:S(2)}) collective-permute-start(bf16[448,1536]{1,0:T(8,128)(2,1)} %refs_0_.1), channel_id=1, source_target_pairs={{0,1},{1,0},{2,3},{3,2},{4,5},{5,4},{6,7},{7,6},{8,9},{9,8},{10,11... | collective-permute-start | bytes 4128776 | tf_op jit(solution)/shard_map/ppermute | solution.py:332
  1.2 4.0 %copy-start.1 = (bf16[448,1536]{1,0:T(8,128)(2,1)S(1)}, bf16[448,1536]{1,0:T(8,128)(2,1)}, u32[]{:S(2)}) copy-start(bf16[448,1536]{1,0:T(8,128)(2,1)} %refs_0_.1) | copy-start | bytes 4128772
  1.2 4.0 %copy-start.2 = (bf16[384,384]{1,0:T(8,128)(2,1)S(1)}, bf16[384,384]{1,0:T(8,128)(2,1)}, u32[]{:S(2)}) copy-start(bf16[384,384]{1,0:T(8,128)(2,1)} %q.3) | copy-start | bytes 884740
  1.2 4.0 %copy-start.3 = (bf16[384,384]{1,0:T(8,128)(2,1)S(1)}, bf16[384,384]{1,0:T(8,128)(2,1)}, u32[]{:S(2)}) copy-start(bf16[384,384]{1,0:T(8,128)(2,1)} %k.3) | copy-start | bytes 884740
  1.2 4.0 %copy-start.4 = (bf16[384,384]{1,0:T(8,128)(2,1)S(1)}, bf16[384,384]{1,0:T(8,128)(2,1)}, u32[]{:S(2)}) copy-start(bf16[384,384]{1,0:T(8,128)(2,1)} %v.3) | copy-start | bytes 884740
  1.2 4.0 %copy-start.5 = (s32[1,384]{1,0:T(1,128)S(1)}, s32[1,384]{1,0:T(1,128)}, u32[]{:S(2)}) copy-start(s32[1,384]{1,0:T(1,128)} %seg) | copy-start | bytes 4612
  1.2 4.0 %copy-start.6 = (s32[1,384]{1,0:T(1,128)S(1)}, s32[1,384]{1,0:T(1,128)}, u32[]{:S(2)}) copy-start(s32[1,384]{1,0:T(1,128)} %flags.1) | copy-start | bytes 4612
  2.5 16.6 %collective-permute-start.1 = (bf16[384,640]{1,0:T(8,128)(2,1)S(1)}, bf16[384,640]{1,0:T(8,128)(2,1)S(1)}, u32[]{:S(2)}, u32[]{:S(2)}) collective-permute-start(bf16[384,640]{1,0:T(8,128)(2,1)S(1)} %get-tuple-element.31), channel_id=1, source_target_pairs={{0,2},{1,3},{2,0},{3,1},{4,6},{5,7},{6,4},{7,5},{8,10},{9,11},{10,... | collective-permute-start | bytes 1474568 | tf_op jit(solution)/shard_map/ppermute | solution.py:332
  5.2 19.5 %copy-start = (bf16[384,6144]{1,0:T(8,128)(2,1)S(1)}, bf16[384,6144]{1,0:T(8,128)(2,1)}, u32[]{:S(2)}) copy-start(bf16[384,6144]{1,0:T(8,128)(2,1)} %weight.7) | copy-start | bytes 14155780
  7.7 11.4 %collective-permute-start.2 = (bf16[64,1536]{1,0:T(8,128)(2,1)S(1)}, bf16[64,1536]{1,0:T(8,128)(2,1)S(1)}, u32[]{:S(2)}, u32[]{:S(2)}) collective-permute-start(bf16[64,1536]{1,0:T(8,128)(2,1)S(1)} %get-tuple-element.34), channel_id=1, source_target_pairs={{0,28},{4,0},{8,4},{12,8},{16,12},{20,16},{24,20},{28,24},{1,29},{... | collective-permute-start | bytes 589832 | tf_op jit(solution)/shard_map/ppermute | solution.py:337
  12.3 6.8 %collective-permute-start.3 = (bf16[64,384]{1,0:T(8,128)(2,1)S(1)}, bf16[64,384]{1,0:T(8,128)(2,1)S(1)}, u32[]{:S(2)}, u32[]{:S(2)}) collective-permute-start(bf16[64,384]{1,0:T(8,128)(2,1)S(1)} %get-tuple-element.35), channel_id=1, source_target_pairs={{0,4},{4,8},{8,12},{12,16},{16,20},{20,24},{24,28},{28,0},{1,5},{5... | collective-permute-start | bytes 147464 | tf_op jit(solution)/shard_map/ppermute | solution.py:337
  19.1 12.3 %collective-permute-start.5 = (bf16[384,640]{1,0:T(8,128)(2,1)S(1)}, bf16[384,640]{1,0:T(8,128)(2,1)S(1)}, u32[]{:S(2)}, u32[]{:S(2)}) collective-permute-start(bf16[384,640]{1,0:T(8,128)(2,1)S(1)} %collective-permute-done.1.refs_0_), channel_id=1, source_target_pairs={{0,4},{4,0},{8,12},{12,8},{16,20},{20,16},{24,28},{28,24},{1,5},{5... | collective-permute-start | bytes 1474568 | tf_op jit(solution)/shard_map/ppermute | solution.py:332
  19.1 13.3 %collective-permute-start.7 = (bf16[384,640]{1,0:T(8,128)(2,1)S(1)}, bf16[384,640]{1,0:T(8,128)(2,1)S(1)}, u32[]{:S(2)}, u32[]{:S(2)}) collective-permute-start(bf16[384,640]{1,0:T(8,128)(2,1)S(1)} %collective-permute-done.1.refs_0_), channel_id=1, source_target_pairs={{0,8},{4,12},{8,0},{12,4},{16,24},{20,28},{24,16},{28,20},{1,9},{5... | collective-permute-start | bytes 1474568 | tf_op jit(solution)/shard_map/ppermute | solution.py:332
  20.4 11.1 %collective-permute-start.6 = (bf16[448,384]{1,0:T(8,128)(2,1)S(1)}, bf16[448,384]{1,0:T(8,128)(2,1)S(1)}, u32[]{:S(2)}, u32[]{:S(2)}) collective-permute-start(bf16[448,384]{1,0:T(8,128)(2,1)S(1)} %constant_dynamic-update-slice_fusion.att), channel_id=1, source_target_pairs={{0,2},{1,3},{2,0},{3,1},{4,6},{5,7},{6,4},{7,5},{8,10},{9,11},{10,... | collective-permute-start | bytes 1032200 | tf_op jit(solution)/shard_map/ppermute | solution.py:332
  21.9 1.4 %collective-permute-start.4 = (bf16[64,1536]{1,0:T(8,128)(2,1)S(1)}, bf16[64,1536]{1,0:T(8,128)(2,1)S(1)}, u32[]{:S(2)}, u32[]{:S(2)}) collective-permute-start(bf16[64,1536]{1,0:T(8,128)(2,1)S(1)} %collective-permute-done.2.refs_2_), channel_id=1, source_target_pairs={{0,1},{1,0},{2,3},{3,2},{4,5},{5,4},{6,7},{7,6},{8,9},{9,8},{10,11... | collective-permute-start | bytes 589832 | tf_op jit(solution)/shard_map/ppermute | solution.py:332
  23.4 14.6 %collective-permute-start.10 = (bf16[384,512]{1,0:T(8,128)(2,1)S(1)}, bf16[384,512]{1,0:T(8,128)(2,1)S(1)}, u32[]{:S(2)}, u32[]{:S(2)}) collective-permute-start(bf16[384,512]{1,0:T(8,128)(2,1)S(1)} %get-tuple-element.46), channel_id=1, source_target_pairs={{0,2},{1,3},{2,0},{3,1},{4,6},{5,7},{6,4},{7,5},{8,10},{9,11},{10,... | collective-permute-start | bytes 1179656 | tf_op jit(solution)/shard_map/ppermute | solution.py:332
  31.5 6.8 %collective-permute-start.8 = (bf16[224,640]{1,0:T(8,128)(2,1)S(1)}, bf16[224,640]{1,0:T(8,128)(2,1)S(1)}, u32[]{:S(2)}, u32[]{:S(2)}) collective-permute-start(bf16[224,640]{1,0:T(8,128)(2,1)S(1)} %slice.6), channel_id=1, source_target_pairs={{0,8},{4,12},{8,0},{12,4},{16,24},{20,28},{24,16},{28,20},{1,9},{5... | collective-permute-start | bytes 860168 | tf_op jit(solution)/shard_map/ppermute | solution.py:332
  32.4 5.8 %collective-permute-start.9 = (bf16[160,640]{1,0:T(8,128)(2,1)S(1)}, bf16[160,640]{1,0:T(8,128)(2,1)S(1)}, u32[]{:S(2)}, u32[]{:S(2)}) collective-permute-start(bf16[160,640]{1,0:T(8,128)(2,1)S(1)} %slice.7), channel_id=1, source_target_pairs={{0,4},{4,0},{8,12},{12,8},{16,20},{20,16},{24,28},{28,24},{1,5},{5... | collective-permute-start | bytes 614408 | tf_op jit(solution)/shard_map/ppermute | solution.py:332
  38.9 6.9 %collective-permute-start.13 = (bf16[384,384]{1,0:T(8,128)(2,1)S(1)}, bf16[384,384]{1,0:T(8,128)(2,1)S(1)}, u32[]{:S(2)}, u32[]{:S(2)}) collective-permute-start(bf16[384,384]{1,0:T(8,128)(2,1)S(1)} %shard_map.107), channel_id=1, source_target_pairs={{0,2},{1,3},{2,0},{3,1},{4,6},{5,7},{6,4},{7,5},{8,10},{9,11},{10,... | collective-permute-start | bytes 884744 | tf_op jit(solution)/shard_map/ppermute | solution.py:332
  44.0 4.2 %collective-permute-start.12 = (bf16[448,896]{1,0:T(8,128)(2,1)S(1)}, bf16[448,896]{1,0:T(8,128)(2,1)S(1)}, u32[]{:S(2)}, u32[]{:S(2)}) collective-permute-start(bf16[448,896]{1,0:T(8,128)(2,1)S(1)} %get-tuple-element.53), channel_id=1, source_target_pairs={{0,1},{1,0},{2,3},{3,2},{4,5},{5,4},{6,7},{7,6},{8,9},{9,8},{10,11... | collective-permute-start | bytes 2408456 | tf_op jit(solution)/shard_map/ppermute | solution.py:332
  44.1 4.2 %collective-permute-start.11 = (bf16[448,1280]{1,0:T(8,128)(2,1)S(1)}, bf16[448,1280]{1,0:T(8,128)(2,1)S(1)}, u32[]{:S(2)}, u32[]{:S(2)}) collective-permute-start(bf16[448,1280]{1,0:T(8,128)(2,1)S(1)} %get-tuple-element.50), channel_id=1, source_target_pairs={{0,1},{1,0},{2,3},{3,2},{4,5},{5,4},{6,7},{7,6},{8,9},{9,8},{10,11... | collective-permute-start | bytes 3440648 | tf_op jit(solution)/shard_map/ppermute | solution.py:332

commit v6 on v5

--- a/solution.py
+++ b/solution.py
@@ -392,7 +392,7 @@
 
     by_y, near, far_att = lax.optimization_barrier((by_y, near, far_att))
     by_z = tie(by_z, near)
-    rows_a = width * 7 // 12 // 32 * 32
+    rows_a = width * 240 // 384 // 16 * 16
     diag_a = flip(by_y[:rows_a], "dp", 2)
     diag_b = flip(by_z[rows_a:], "dp", 1)
 
@@ -404,6 +404,15 @@
         flops=6 * home * width * cols,
         moved=(home + width) * cols * 6,
     )(t, place, cot_own, cot_sib, *early)[0]
+    own, sib, left = call(
+        functools.partial(early_kernel, cap, part),
+        [((dest, 2 * cols), BF16), ((dest, 2 * cols), BF16), ((dest, 2 * width), BF16)],
+        [SMEM] * 3 + [VMEM] * 6,
+        flops=12 * dest * width * cols,
+        moved=12 * width * cols + dest * part * 4,
+    )(gone, t, place, att, far_att, out_weight, *early)
+    other = flip(sib, "tensor", 1)
+    half, own = lax.optimization_barrier((half, own))
     send = call(
         last_kernel,
         [((home, width), BF16)],
@@ -412,14 +421,6 @@
         moved=(home + width) * (cols + 2 * rest) * 2,
     )(t, place, cot_own, cot_sib, half, diag_a, diag_b, direct)[0]
     far = flip(send, "tensor", 2)
-    own, sib, left = call(
-        functools.partial(early_kernel, cap, part),
-        [((dest, 2 * cols), BF16), ((dest, 2 * cols), BF16), ((dest, 2 * width), BF16)],
-        [SMEM] * 3 + [VMEM] * 6,
-        flops=12 * dest * width * cols,
-        moved=12 * width * cols + dest * part * 4,
-    )(gone, t, tie(place, send), att, far_att, out_weight, *early)
-    other = flip(sib, "tensor", 1)
     own_late, sib_late = call(
         late_kernel,
         [((dest, cols + rest), BF16)] * 2,

time: 49.6 us -> 49.6 us (level)
  transfers between devices with their start and end apart: 14 -> 14, of which waited for: 6 -> 5; matrix products, arithmetic and copies ran while one was open for 0% -> 0% of each run, Pallas kernels for 27% -> 27%
where the time goes in v6:
time: 49.6 us; the launch traced here: 49.5 us
  waiting for transfers between devices  17.5 us (35%)
  starting transfers between devices  16.1 us (32%)
  Pallas kernels  15 us (30%)
  between operations  0.81 us (2%)
    ppermute x12, starting transfers between devices, flip(): return lax.ppermute(values, axis, [(i, i ^ by) for i in range(size)])  11.5 us
    ppermute x12, waiting for transfers between devices, flip(): return lax.ppermute(values, axis, [(i, i ^ by) for i in range(size)])  10.7 us
    ppermute x2, waiting for transfers between devices, shifted(): lax.ppermute(values, axis, [(i, (i + by) % size) for i in range(size)])  6.79 us
    ppermute x2, starting transfers between devices, shifted(): lax.ppermute(values, axis, [(i, (i + by) % size) for i in range(size)])  4.61 us
    pallas_call x1, Pallas kernels, attend(): call(functools.partial(forward_kernel, cap), [((1,), jnp.int32), ((cap, p...  2.53 us
    pallas_call x1, Pallas kernels, shards(): call(functools.partial(early_kernel, cap, part), [((dest, 2 * cols), BF16...  2.5 us
    pallas_call x1, Pallas kernels, gradients(): call(backward_kernel, [((home, width), BF16)] * 3, [VMEM] * 6, [pltpu.VME...  2.4 us
    pallas_call x1, Pallas kernels, shards(): call(own_kernel, [((home, width), F32)], [SMEM, VMEM, VMEM, VMEM], flops=...  1.41 us
  transfers between devices with their start and end apart: 14, of which 5 were waited for; matrix products, arithmetic and copies ran while one was open for 0% of the time, Pallas kernels for 27%

profile of v6, /device:TPU:0, one launch (start us, length us, event | category | flops | bytes accessed | tf_op | source)
XLA Modules:
  0.0 49.5 jit_solution(2659561448970851166)
XLA Ops:
  0.6 0.5 %collective-permute-start = (bf16[448,1536]{1,0:T(8,128)(2,1)}, bf16[448,1536]{1,0:T(8,128)(2,1)S(1)}, u32[]{:S(2)}, u32[]{:S(2)}) collective-permute-start(bf16[448,1536]{1,0:T(8,128)(2,1)} %refs_0_.1), channel_id=1, source_target_pairs={{0,1},{1,0},{2,3},{3,2},{4,5},{5,4},{6,7},{7,6},{8,9},{9,8},{10,11... | collective-permute-start | bytes 4128776 | tf_op jit(solution)/shard_map/ppermute | solution.py:332
  1.2 0.0 copy-start.1
  1.2 0.0 copy-start.2
  1.2 0.0 copy-start.3
  1.2 0.0 copy-start.4
  1.2 0.0 copy-start.5
  1.2 0.0 copy-start.6
  1.2 1.4 %shard_map.102 = (bf16[384,640]{1,0:T(8,128)(2,1)S(1)}, bf16[384,512]{1,0:T(8,128)(2,1)S(1)}) custom-call(s32[1]{0:T(128)} %bitcast.t.t_ref, s32[1]{0:T(128)} %bitcast.1.place.place_ref, bf16[384,6144]{1,0:T(8,128)(2,1)} %weight.7), custom_call_target="tpu_custom_call" | custom-call | tf_op jit(solution)/shard_map/pallas_call | solution.py:355
  2.5 2.6 %collective-permute-start.1 = (bf16[384,640]{1,0:T(8,128)(2,1)S(1)}, bf16[384,640]{1,0:T(8,128)(2,1)S(1)}, u32[]{:S(2)}, u32[]{:S(2)}) collective-permute-start(bf16[384,640]{1,0:T(8,128)(2,1)S(1)} %get-tuple-element.33), channel_id=1, source_target_pairs={{0,2},{1,3},{2,0},{3,1},{4,6},{5,7},{6,4},{7,5},{8,10},{9,11},{10,... | collective-permute-start | bytes 1474568 | tf_op jit(solution)/shard_map/ppermute | solution.py:332
  5.1 0.0 copy-done.1
  5.1 0.0 copy-done.2
  5.1 0.0 copy-done.3
  5.2 0.0 copy-done.4
  5.2 0.0 copy-done.5
  5.2 0.0 copy-done.6
  5.2 0.0 copy-start
  5.2 2.5 %shard_map.103 = (s32[1]{0:T(128)}, bf16[64,1536]{1,0:T(8,128)(2,1)S(1)}, bf16[448,384]{1,0:T(8,128)(2,1)S(1)}, bf16[64,384]{1,0:T(8,128)(2,1)S(1)}, bf16[3,384,384]{2,1,0:T(8,128)(2,1)S(1)}) custom-call(s32[1,384]{1,0:T(1,128)S(1)} %copy-done.5, s32[1,384]{1,0:T(1,128)S(1)} %copy-done.6, bf16[384,384]{1,0:T(8,128)(2,1)S(1)} %copy-done.2, ...), custom_call_target="tpu_custom_call" | custom-call | tf_op jit(solution)/shard_map/pallas_call | solution.py:55
  7.7 4.6 %collective-permute-start.2 = (bf16[64,1536]{1,0:T(8,128)(2,1)S(1)}, bf16[64,1536]{1,0:T(8,128)(2,1)S(1)}, u32[]{:S(2)}, u32[]{:S(2)}) collective-permute-start(bf16[64,1536]{1,0:T(8,128)(2,1)S(1)} %get-tuple-element.36), channel_id=1, source_target_pairs={{0,28},{4,0},{8,4},{12,8},{16,12},{20,16},{24,20},{28,24},{1,29},{... | collective-permute-start | bytes 589832 | tf_op jit(solution)/shard_map/ppermute | solution.py:337
  12.3 0.0 collective-permute-start.3
  12.3 6.8 %collective-permute-done.3 = bf16[64,384]{1,0:T(8,128)(2,1)S(1)} collective-permute-done((bf16[64,384]{1,0:T(8,128)(2,1)S(1)}, bf16[64,384]{1,0:T(8,128)(2,1)S(1)}, u32[]{:S(2)}, u32[]{:S(2)}) %collective-permute-start.3) | collective-permute-done | bytes 49184 | tf_op jit(solution)/shard_map/ppermute | solution.py:337
  19.1 0.0 collective-permute-done.2.refs_2_
  19.1 0.0 collective-permute-done.1.refs_0_
  19.1 0.0 collective-permute-start.5
  19.1 1.2 %collective-permute-start.7 = (bf16[384,640]{1,0:T(8,128)(2,1)S(1)}, bf16[384,640]{1,0:T(8,128)(2,1)S(1)}, u32[]{:S(2)}, u32[]{:S(2)}) collective-permute-start(bf16[384,640]{1,0:T(8,128)(2,1)S(1)} %collective-permute-done.1.refs_0_), channel_id=1, source_target_pairs={{0,8},{4,12},{8,0},{12,4},{16,24},{20,28},{24,16},{28,20},{1,9},{5... | collective-permute-start | bytes 1474568 | tf_op jit(solution)/shard_map/ppermute | solution.py:332
  20.4 1.6 %collective-permute-start.6 = (bf16[448,384]{1,0:T(8,128)(2,1)S(1)}, bf16[448,384]{1,0:T(8,128)(2,1)S(1)}, u32[]{:S(2)}, u32[]{:S(2)}) collective-permute-start(bf16[448,384]{1,0:T(8,128)(2,1)S(1)} %constant_dynamic-update-slice_fusion.att), channel_id=1, source_target_pairs={{0,2},{1,3},{2,0},{3,1},{4,6},{5,7},{6,4},{7,5},{8,10},{9,11},{10,... | collective-permute-start | bytes 1032200 | tf_op jit(solution)/shard_map/ppermute | solution.py:332
  21.9 0.0 collective-permute-start.4
  21.9 1.4 %collective-permute-done.4.refs_3_ = bf16[64,1536]{1,0:T(8,128)(2,1)S(1)} collective-permute-done((bf16[64,1536]{1,0:T(8,128)(2,1)S(1)}, bf16[64,1536]{1,0:T(8,128)(2,1)S(1)}, u32[]{:S(2)}, u32[]{:S(2)}) %collective-permute-start.4) | collective-permute-done | bytes 196640 | tf_op jit(solution)/shard_map/ppermute | solution.py:332
  23.4 0.5 %collective-permute-start.11 = (bf16[384,512]{1,0:T(8,128)(2,1)S(1)}, bf16[384,512]{1,0:T(8,128)(2,1)S(1)}, u32[]{:S(2)}, u32[]{:S(2)}) collective-permute-start(bf16[384,512]{1,0:T(8,128)(2,1)S(1)} %get-tuple-element.53), channel_id=1, source_target_pairs={{0,2},{1,3},{2,0},{3,1},{4,6},{5,7},{6,4},{7,5},{8,10},{9,11},{10,... | collective-permute-start | bytes 1179656 | tf_op jit(solution)/shard_map/ppermute | solution.py:332
  23.9 0.0 collective-permute-done.refs_1_
  23.9 0.8 %shard_map.104 = (bf16[384,1536]{1,0:T(8,128)(2,1)S(1)}, bf16[384,1536]{1,0:T(8,128)(2,1)S(1)}) custom-call(s32[1]{0:T(128)} %get-tuple-element.35.gone_ref.gone, bf16[448,1536]{1,0:T(8,128)(2,1)S(1)} %copy-done.1, bf16[448,1536]{1,0:T(8,128)(2,1)S(1)} %collective-permute-done.refs_1_, bf16[64,1536]{1,0:T(8,128)(2,1)S(1)} %collective-permute-done.2.refs_2_, ...), custom_call_target="tpu_custom_call" | custom-call | tf_op jit(solution)/shard_map/pallas_call | solution.py:379
  24.7 0.0 copy-done
  24.7 1.4 %shard_map.105.near = f32[384,384]{1,0:T(8,128)S(1)} custom-call(s32[1]{0:T(128)} %bitcast.t.t_ref, bf16[384,1536]{1,0:T(8,128)(2,1)S(1)} %get-tuple-element.39.cot_own, bf16[384,1536]{1,0:T(8,128)(2,1)S(1)} %get-tuple-element.40.cot_sib, bf16[384,6144]{1,0:T(8,128)(2,1)S(1)} %copy-done), custom_call_target="tpu_custom_call" | custom-call | flops 905969664 | bytes 4718592 | tf_op jit(solution)/shard_map/pallas_call | solution.py:385
  26.2 5.3 %collective-permute-done.6.far_att = bf16[448,384]{1,0:T(8,128)(2,1)S(1)} collective-permute-done((bf16[448,384]{1,0:T(8,128)(2,1)S(1)}, bf16[448,384]{1,0:T(8,128)(2,1)S(1)}, u32[]{:S(2)}, u32[]{:S(2)}) %collective-permute-start.6) | collective-permute-done | bytes 344096 | tf_op jit(solution)/shard_map/ppermute | solution.py:332
  31.4 0.0 collective-permute-done.5.refs_1_
  31.5 1.0 %collective-permute-start.9 = (bf16[240,640]{1,0:T(8,128)(2,1)S(1)}, bf16[240,640]{1,0:T(8,128)(2,1)S(1)}, u32[]{:S(2)}, u32[]{:S(2)}) collective-permute-start(bf16[240,640]{1,0:T(8,128)(2,1)S(1)} %slice.6), channel_id=1, source_target_pairs={{0,8},{4,12},{8,0},{12,4},{16,24},{20,28},{24,16},{28,20},{1,9},{5... | collective-permute-start | bytes 921608 | tf_op jit(solution)/shard_map/ppermute | solution.py:332
  32.4 0.0 collective-permute-done.7.refs_2_
  32.4 2.0 %collective-permute-start.10 = (bf16[144,640]{1,0:T(8,128)(2,1)S(1)}, bf16[144,640]{1,0:T(8,128)(2,1)S(1)}, u32[]{:S(2)}, u32[]{:S(2)}) collective-permute-start(bf16[144,640]{1,0:T(8,128)(2,1)S(1)} %slice.7), channel_id=1, source_target_pairs={{0,4},{4,0},{8,12},{12,8},{16,20},{20,16},{24,28},{28,24},{1,5},{5... | collective-permute-start | bytes 552968 | tf_op jit(solution)/shard_map/ppermute | solution.py:332
  34.5 1.0 %shard_map.106.part_sum = f32[384,384]{1,0:T(8,128)S(1)} custom-call(s32[1]{0:T(128)} %bitcast.t.t_ref, s32[1]{0:T(128)} %bitcast.1.place.place_ref, bf16[384,1536]{1,0:T(8,128)(2,1)S(1)} %get-tuple-element.39.cot_own, bf16[384,1536]{1,0:T(8,128)(2,1)S(1)} %get-tuple-element.40.cot_sib, bf16[384,640]{1,0:T(8,128)(2,1)S(1)} %collective-permute-done.1.refs_0_, ...), custom_call_target="tpu_custom_call" | custom-call | flops 566231040 | bytes 2949120 | tf_op jit(solution)/shard_map/pallas_call | solution.py:400
  35.5 2.5 %shard_map.107 = (bf16[448,1280]{1,0:T(8,128)(2,1)S(1)}, bf16[448,1280]{1,0:T(8,128)(2,1)S(1)}, bf16[448,768]{1,0:T(8,128)(2,1)S(1)}) custom-call(s32[1]{0:T(128)} %get-tuple-element.35.gone_ref.gone, s32[1]{0:T(128)} %bitcast.t.t_ref, s32[1]{0:T(128)} %bitcast.1.place.place_ref, bf16[448,384]{1,0:T(8,128)(2,1)S(1)} %constant_dynamic-update-slice_fusion.att, ...), custom_call_target="tpu_custom_call" | custom-call | flops 1321205760 | bytes 5701632 | tf_op jit(solution)/shard_map/pallas_call | solution.py:407
  38.0 0.0 collective-permute-done.11.direct
  38.0 0.0 collective-permute-done.10.diag_b
  38.0 0.3 collective-permute-done.9.diag_a
  38.4 0.7 %shard_map.108 = bf16[384,384]{1,0:T(8,128)(2,1)S(1)} custom-call(s32[1]{0:T(128)} %bitcast.t.t_ref, s32[1]{0:T(128)} %bitcast.1.place.place_ref, bf16[384,1536]{1,0:T(8,128)(2,1)S(1)} %get-tuple-element.39.cot_own, bf16[384,1536]{1,0:T(8,128)(2,1)S(1)} %get-tuple-element.40.cot_sib, f32[384,384]{1,0:T(8,128)S(1)} %shard_map.106.part_sum, ...), custom_call_target="tpu_custom_call" | custom-call | flops 339738624 | bytes 1769472 | tf_op jit(solution)/shard_map/pallas_call | solution.py:416
  39.1 1.6 %collective-permute-start.13 = (bf16[384,384]{1,0:T(8,128)(2,1)S(1)}, bf16[384,384]{1,0:T(8,128)(2,1)S(1)}, u32[]{:S(2)}, u32[]{:S(2)}) collective-permute-start(bf16[384,384]{1,0:T(8,128)(2,1)S(1)} %shard_map.108), channel_id=1, source_target_pairs={{0,2},{1,3},{2,0},{3,1},{4,6},{5,7},{6,4},{7,5},{8,10},{9,11},{10,... | collective-permute-start | bytes 884744 | tf_op jit(solution)/shard_map/ppermute | solution.py:332
  40.6 0.0 collective-permute-start.8
  40.6 1.1 %shard_map.109 = (bf16[448,896]{1,0:T(8,128)(2,1)S(1)}, bf16[448,896]{1,0:T(8,128)(2,1)S(1)}) custom-call(s32[1]{0:T(128)} %bitcast.t.t_ref, s32[1]{0:T(128)} %bitcast.1.place.place_ref, bf16[448,768]{1,0:T(8,128)(2,1)S(1)} %get-tuple-element.55.left, bf16[384,6144]{1,0:T(8,128)(2,1)S(1)} %copy-done, bf16[240,640]{1,0:T(8,128)(2,1)S(1)} %collective-permute-done.9.diag_a, ...), custom_call_target="tpu_custom_call" | custom-call | flops 792723456 | bytes 3145728 | tf_op jit(solution)/shard_map/pallas_call | solution.py:424
  41.7 0.6 %collective-permute-start.12 = (bf16[448,896]{1,0:T(8,128)(2,1)S(1)}, bf16[448,896]{1,0:T(8,128)(2,1)S(1)}, u32[]{:S(2)}, u32[]{:S(2)}) collective-permute-start(bf16[448,896]{1,0:T(8,128)(2,1)S(1)} %get-tuple-element.57), channel_id=1, source_target_pairs={{0,1},{1,0},{2,3},{3,2},{4,5},{5,4},{6,7},{7,6},{8,9},{9,8},{10,11... | collective-permute-start | bytes 2408456 | tf_op jit(solution)/shard_map/ppermute | solution.py:332
  42.3 3.6 %collective-permute-done.13.far = bf16[384,384]{1,0:T(8,128)(2,1)S(1)} collective-permute-done((bf16[384,384]{1,0:T(8,128)(2,1)S(1)}, bf16[384,384]{1,0:T(8,128)(2,1)S(1)}, u32[]{:S(2)}, u32[]{:S(2)}) %collective-permute-start.13) | collective-permute-done | bytes 294944 | tf_op jit(solution)/shard_map/ppermute | solution.py:332
  45.9 2.4 %shard_map.111 = (bf16[384,384]{1,0:T(8,128)(2,1)}, bf16[384,384]{1,0:T(8,128)(2,1)}, bf16[384,384]{1,0:T(8,128)(2,1)}) custom-call(bf16[384,384]{1,0:T(8,128)(2,1)S(1)} %copy-done.2, bf16[384,384]{1,0:T(8,128)(2,1)S(1)} %copy-done.3, bf16[384,384]{1,0:T(8,128)(2,1)S(1)} %copy-done.4, bf16[3,384,384]{2,1,0:T(8,128)(2,1)S(1)} %get-tuple-element.58.pt, ...), custom_call_target="tpu_custom_call" | custom-call | flops 45298483200 | bytes 2654208 | tf_op jit(solution)/shard_map/pallas_call | solution.py:318
  48.3 0.0 collective-permute-done.12.other_late
  48.3 0.0 collective-permute-done.8.other
  48.3 1.2 %shard_map.110 = bf16[448,1536]{1,0:T(8,128)(2,1)} custom-call(s32[1]{0:T(128)} %bitcast.t.t_ref, s32[1]{0:T(128)} %bitcast.1.place.place_ref, bf16[448,1280]{1,0:T(8,128)(2,1)S(1)} %get-tuple-element.49.own, bf16[448,1280]{1,0:T(8,128)(2,1)S(1)} %collective-permute-done.8.other, bf16[448,896]{1,0:T(8,128)(2,1)S(1)} %get-tuple-element.56.own_late, ...), custom_call_target="tpu_custom_call" | custom-call | bytes 4128768 | tf_op jit(solution)/shard_map/pallas_call | solution.py:432
  (3 shorter events, 0.1 us)
Async XLA Ops:
  0.6 23.3 %collective-permute-start = (bf16[448,1536]{1,0:T(8,128)(2,1)}, bf16[448,1536]{1,0:T(8,128)(2,1)S(1)}, u32[]{:S(2)}, u32[]{:S(2)}) collective-permute-start(bf16[448,1536]{1,0:T(8,128)(2,1)} %refs_0_.1), channel_id=1, source_target_pairs={{0,1},{1,0},{2,3},{3,2},{4,5},{5,4},{6,7},{7,6},{8,9},{9,8},{10,11... | collective-permute-start | bytes 4128776 | tf_op jit(solution)/shard_map/ppermute | solution.py:332
  1.2 4.0 %copy-start.1 = (bf16[448,1536]{1,0:T(8,128)(2,1)S(1)}, bf16[448,1536]{1,0:T(8,128)(2,1)}, u32[]{:S(2)}) copy-start(bf16[448,1536]{1,0:T(8,128)(2,1)} %refs_0_.1) | copy-start | bytes 4128772
  1.2 4.0 %copy-start.2 = (bf16[384,384]{1,0:T(8,128)(2,1)S(1)}, bf16[384,384]{1,0:T(8,128)(2,1)}, u32[]{:S(2)}) copy-start(bf16[384,384]{1,0:T(8,128)(2,1)} %q.3) | copy-start | bytes 884740
  1.2 4.0 %copy-start.3 = (bf16[384,384]{1,0:T(8,128)(2,1)S(1)}, bf16[384,384]{1,0:T(8,128)(2,1)}, u32[]{:S(2)}) copy-start(bf16[384,384]{1,0:T(8,128)(2,1)} %k.3) | copy-start | bytes 884740
  1.2 4.0 %copy-start.4 = (bf16[384,384]{1,0:T(8,128)(2,1)S(1)}, bf16[384,384]{1,0:T(8,128)(2,1)}, u32[]{:S(2)}) copy-start(bf16[384,384]{1,0:T(8,128)(2,1)} %v.3) | copy-start | bytes 884740
  1.2 4.0 %copy-start.5 = (s32[1,384]{1,0:T(1,128)S(1)}, s32[1,384]{1,0:T(1,128)}, u32[]{:S(2)}) copy-start(s32[1,384]{1,0:T(1,128)} %seg) | copy-start | bytes 4612
  1.2 4.0 %copy-start.6 = (s32[1,384]{1,0:T(1,128)S(1)}, s32[1,384]{1,0:T(1,128)}, u32[]{:S(2)}) copy-start(s32[1,384]{1,0:T(1,128)} %flags.1) | copy-start | bytes 4612
  2.5 16.6 %collective-permute-start.1 = (bf16[384,640]{1,0:T(8,128)(2,1)S(1)}, bf16[384,640]{1,0:T(8,128)(2,1)S(1)}, u32[]{:S(2)}, u32[]{:S(2)}) collective-permute-start(bf16[384,640]{1,0:T(8,128)(2,1)S(1)} %get-tuple-element.33), channel_id=1, source_target_pairs={{0,2},{1,3},{2,0},{3,1},{4,6},{5,7},{6,4},{7,5},{8,10},{9,11},{10,... | collective-permute-start | bytes 1474568 | tf_op jit(solution)/shard_map/ppermute | solution.py:332
  5.2 19.6 %copy-start = (bf16[384,6144]{1,0:T(8,128)(2,1)S(1)}, bf16[384,6144]{1,0:T(8,128)(2,1)}, u32[]{:S(2)}) copy-start(bf16[384,6144]{1,0:T(8,128)(2,1)} %weight.7) | copy-start | bytes 14155780
  7.7 11.4 %collective-permute-start.2 = (bf16[64,1536]{1,0:T(8,128)(2,1)S(1)}, bf16[64,1536]{1,0:T(8,128)(2,1)S(1)}, u32[]{:S(2)}, u32[]{:S(2)}) collective-permute-start(bf16[64,1536]{1,0:T(8,128)(2,1)S(1)} %get-tuple-element.36), channel_id=1, source_target_pairs={{0,28},{4,0},{8,4},{12,8},{16,12},{20,16},{24,20},{28,24},{1,29},{... | collective-permute-start | bytes 589832 | tf_op jit(solution)/shard_map/ppermute | solution.py:337
  12.3 6.8 %collective-permute-start.3 = (bf16[64,384]{1,0:T(8,128)(2,1)S(1)}, bf16[64,384]{1,0:T(8,128)(2,1)S(1)}, u32[]{:S(2)}, u32[]{:S(2)}) collective-permute-start(bf16[64,384]{1,0:T(8,128)(2,1)S(1)} %get-tuple-element.37), channel_id=1, source_target_pairs={{0,4},{4,8},{8,12},{12,16},{16,20},{20,24},{24,28},{28,0},{1,5},{5... | collective-permute-start | bytes 147464 | tf_op jit(solution)/shard_map/ppermute | solution.py:337
  19.1 12.3 %collective-permute-start.5 = (bf16[384,640]{1,0:T(8,128)(2,1)S(1)}, bf16[384,640]{1,0:T(8,128)(2,1)S(1)}, u32[]{:S(2)}, u32[]{:S(2)}) collective-permute-start(bf16[384,640]{1,0:T(8,128)(2,1)S(1)} %collective-permute-done.1.refs_0_), channel_id=1, source_target_pairs={{0,4},{4,0},{8,12},{12,8},{16,20},{20,16},{24,28},{28,24},{1,5},{5... | collective-permute-start | bytes 1474568 | tf_op jit(solution)/shard_map/ppermute | solution.py:332
  19.1 13.3 %collective-permute-start.7 = (bf16[384,640]{1,0:T(8,128)(2,1)S(1)}, bf16[384,640]{1,0:T(8,128)(2,1)S(1)}, u32[]{:S(2)}, u32[]{:S(2)}) collective-permute-start(bf16[384,640]{1,0:T(8,128)(2,1)S(1)} %collective-permute-done.1.refs_0_), channel_id=1, source_target_pairs={{0,8},{4,12},{8,0},{12,4},{16,24},{20,28},{24,16},{28,20},{1,9},{5... | collective-permute-start | bytes 1474568 | tf_op jit(solution)/shard_map/ppermute | solution.py:332
  20.4 11.1 %collective-permute-start.6 = (bf16[448,384]{1,0:T(8,128)(2,1)S(1)}, bf16[448,384]{1,0:T(8,128)(2,1)S(1)}, u32[]{:S(2)}, u32[]{:S(2)}) collective-permute-start(bf16[448,384]{1,0:T(8,128)(2,1)S(1)} %constant_dynamic-update-slice_fusion.att), channel_id=1, source_target_pairs={{0,2},{1,3},{2,0},{3,1},{4,6},{5,7},{6,4},{7,5},{8,10},{9,11},{10,... | collective-permute-start | bytes 1032200 | tf_op jit(solution)/shard_map/ppermute | solution.py:332
  21.9 1.4 %collective-permute-start.4 = (bf16[64,1536]{1,0:T(8,128)(2,1)S(1)}, bf16[64,1536]{1,0:T(8,128)(2,1)S(1)}, u32[]{:S(2)}, u32[]{:S(2)}) collective-permute-start(bf16[64,1536]{1,0:T(8,128)(2,1)S(1)} %collective-permute-done.2.refs_2_), channel_id=1, source_target_pairs={{0,1},{1,0},{2,3},{3,2},{4,5},{5,4},{6,7},{7,6},{8,9},{9,8},{10,11... | collective-permute-start | bytes 589832 | tf_op jit(solution)/shard_map/ppermute | solution.py:332
  23.4 14.6 %collective-permute-start.11 = (bf16[384,512]{1,0:T(8,128)(2,1)S(1)}, bf16[384,512]{1,0:T(8,128)(2,1)S(1)}, u32[]{:S(2)}, u32[]{:S(2)}) collective-permute-start(bf16[384,512]{1,0:T(8,128)(2,1)S(1)} %get-tuple-element.53), channel_id=1, source_target_pairs={{0,2},{1,3},{2,0},{3,1},{4,6},{5,7},{6,4},{7,5},{8,10},{9,11},{10,... | collective-permute-start | bytes 1179656 | tf_op jit(solution)/shard_map/ppermute | solution.py:332
  31.5 6.9 %collective-permute-start.9 = (bf16[240,640]{1,0:T(8,128)(2,1)S(1)}, bf16[240,640]{1,0:T(8,128)(2,1)S(1)}, u32[]{:S(2)}, u32[]{:S(2)}) collective-permute-start(bf16[240,640]{1,0:T(8,128)(2,1)S(1)} %slice.6), channel_id=1, source_target_pairs={{0,8},{4,12},{8,0},{12,4},{16,24},{20,28},{24,16},{28,20},{1,9},{5... | collective-permute-start | bytes 921608 | tf_op jit(solution)/shard_map/ppermute | solution.py:332
  32.4 5.6 %collective-permute-start.10 = (bf16[144,640]{1,0:T(8,128)(2,1)S(1)}, bf16[144,640]{1,0:T(8,128)(2,1)S(1)}, u32[]{:S(2)}, u32[]{:S(2)}) collective-permute-start(bf16[144,640]{1,0:T(8,128)(2,1)S(1)} %slice.7), channel_id=1, source_target_pairs={{0,4},{4,0},{8,12},{12,8},{16,20},{20,16},{24,28},{28,24},{1,5},{5... | collective-permute-start | bytes 552968 | tf_op jit(solution)/shard_map/ppermute | solution.py:332
  39.1 6.8 %collective-permute-start.13 = (bf16[384,384]{1,0:T(8,128)(2,1)S(1)}, bf16[384,384]{1,0:T(8,128)(2,1)S(1)}, u32[]{:S(2)}, u32[]{:S(2)}) collective-permute-start(bf16[384,384]{1,0:T(8,128)(2,1)S(1)} %shard_map.108), channel_id=1, source_target_pairs={{0,2},{1,3},{2,0},{3,1},{4,6},{5,7},{6,4},{7,5},{8,10},{9,11},{10,... | collective-permute-start | bytes 884744 | tf_op jit(solution)/shard_map/ppermute | solution.py:332
  40.6 7.7 %collective-permute-start.8 = (bf16[448,1280]{1,0:T(8,128)(2,1)S(1)}, bf16[448,1280]{1,0:T(8,128)(2,1)S(1)}, u32[]{:S(2)}, u32[]{:S(2)}) collective-permute-start(bf16[448,1280]{1,0:T(8,128)(2,1)S(1)} %get-tuple-element.50), channel_id=1, source_target_pairs={{0,1},{1,0},{2,3},{3,2},{4,5},{5,4},{6,7},{7,6},{8,9},{9,8},{10,11... | collective-permute-start | bytes 3440648 | tf_op jit(solution)/shard_map/ppermute | solution.py:332
  41.7 6.6 %collective-permute-start.12 = (bf16[448,896]{1,0:T(8,128)(2,1)S(1)}, bf16[448,896]{1,0:T(8,128)(2,1)S(1)}, u32[]{:S(2)}, u32[]{:S(2)}) collective-permute-start(bf16[448,896]{1,0:T(8,128)(2,1)S(1)} %get-tuple-element.57), channel_id=1, source_target_pairs={{0,1},{1,0},{2,3},{3,2},{4,5},{5,4},{6,7},{7,6},{8,9},{9,8},{10,11... | collective-permute-start | bytes 2408456 | tf_op jit(solution)/shard_map/ppermute | solution.py:332

commit v7 on v5

--- a/solution.py
+++ b/solution.py
@@ -299,12 +299,12 @@
 
         cot = (near[:, cols] + far[:, cols].astype(F32)).astype(BF16)
         weights = pt[h]
-        bv[:, cols] = nn(weights, cot).astype(BF16)
-        send(bv, gv, 0)
         rise = nt(v[:, cols], cot)
         wide = weights.astype(F32)
         mean = jnp.sum(wide * rise, axis=0, keepdims=True)
         slope = (wide * (rise - mean) * HEAD ** (-0.5)).astype(BF16)
+        bv[:, cols] = nn(weights, cot).astype(BF16)
+        send(bv, gv, 0)
         bk[:, cols] = nn(slope, q[:, cols]).astype(BF16)
         send(bk, gk, 1)
         bq[:, cols] = tn(slope, k[:, cols]).astype(BF16)

time: 49.6 us -> 49.4 us (level)
  transfers between devices with their start and end apart: 14 -> 14, of which waited for: 6 -> 6; matrix products, arithmetic and copies ran while one was open for 0% -> 0% of each run, Pallas kernels for 27% -> 26%
where the time goes in v7:
time: 49.4 us; the launch traced here: 49.3 us
  waiting for transfers between devices  17.5 us (35%)
  starting transfers between devices  16 us (32%)
  Pallas kernels  14.8 us (30%)
  between operations  0.81 us (2%)
    ppermute x12, starting transfers between devices, flip(): return lax.ppermute(values, axis, [(i, i ^ by) for i in range(size)])  11.4 us
    ppermute x12, waiting for transfers between devices, flip(): return lax.ppermute(values, axis, [(i, i ^ by) for i in range(size)])  10.7 us
    ppermute x2, waiting for transfers between devices, shifted(): lax.ppermute(values, axis, [(i, (i + by) % size) for i in range(size)])  6.79 us
    ppermute x2, starting transfers between devices, shifted(): lax.ppermute(values, axis, [(i, (i + by) % size) for i in range(size)])  4.61 us
    pallas_call x1, Pallas kernels, attend(): call(functools.partial(forward_kernel, cap), [((1,), jnp.int32), ((cap, p...  2.53 us
    pallas_call x1, Pallas kernels, shards(): call(functools.partial(early_kernel, cap, part), [((dest, 2 * cols), BF16...  2.5 us
    pallas_call x1, Pallas kernels, gradients(): call(backward_kernel, [((home, width), BF16)] * 3, [VMEM] * 6, [pltpu.VME...  2.25 us
    pallas_call x1, Pallas kernels, shards(): call(own_kernel, [((home, width), F32)], [SMEM, VMEM, VMEM, VMEM], flops=...  1.4 us
  transfers between devices with their start and end apart: 14, of which 6 were waited for; matrix products, arithmetic and copies ran while one was open for 0% of the time, Pallas kernels for 26%

profile of v7, /device:TPU:0, one launch (start us, length us, event | category | flops | bytes accessed | tf_op | source)
XLA Modules:
  0.0 49.3 jit_solution(8054583796007426316)
XLA Ops:
  0.6 0.5 %collective-permute-start = (bf16[448,1536]{1,0:T(8,128)(2,1)}, bf16[448,1536]{1,0:T(8,128)(2,1)S(1)}, u32[]{:S(2)}, u32[]{:S(2)}) collective-permute-start(bf16[448,1536]{1,0:T(8,128)(2,1)} %refs_0_.1), channel_id=1, source_target_pairs={{0,1},{1,0},{2,3},{3,2},{4,5},{5,4},{6,7},{7,6},{8,9},{9,8},{10,11... | collective-permute-start | bytes 4128776 | tf_op jit(solution)/shard_map/ppermute | solution.py:332
  1.2 0.0 copy-start.1
  1.2 0.0 copy-start.2
  1.2 0.0 copy-start.3
  1.2 0.0 copy-start.4
  1.2 0.0 copy-start.5
  1.2 0.0 copy-start.6
  1.2 1.4 %shard_map.102 = (bf16[384,640]{1,0:T(8,128)(2,1)S(1)}, bf16[384,512]{1,0:T(8,128)(2,1)S(1)}) custom-call(s32[1]{0:T(128)} %bitcast.t.t_ref, s32[1]{0:T(128)} %bitcast.1.place.place_ref, bf16[384,6144]{1,0:T(8,128)(2,1)} %weight.7), custom_call_target="tpu_custom_call" | custom-call | tf_op jit(solution)/shard_map/pallas_call | solution.py:355
  2.5 2.6 %collective-permute-start.1 = (bf16[384,640]{1,0:T(8,128)(2,1)S(1)}, bf16[384,640]{1,0:T(8,128)(2,1)S(1)}, u32[]{:S(2)}, u32[]{:S(2)}) collective-permute-start(bf16[384,640]{1,0:T(8,128)(2,1)S(1)} %get-tuple-element.31), channel_id=1, source_target_pairs={{0,2},{1,3},{2,0},{3,1},{4,6},{5,7},{6,4},{7,5},{8,10},{9,11},{10,... | collective-permute-start | bytes 1474568 | tf_op jit(solution)/shard_map/ppermute | solution.py:332
  5.1 0.0 copy-done.1
  5.1 0.0 copy-done.2
  5.1 0.0 copy-done.3
  5.2 0.0 copy-done.4
  5.2 0.0 copy-done.5
  5.2 0.0 copy-done.6
  5.2 0.0 copy-start
  5.2 2.5 %shard_map.103 = (s32[1]{0:T(128)}, bf16[64,1536]{1,0:T(8,128)(2,1)S(1)}, bf16[448,384]{1,0:T(8,128)(2,1)S(1)}, bf16[64,384]{1,0:T(8,128)(2,1)S(1)}, bf16[3,384,384]{2,1,0:T(8,128)(2,1)S(1)}) custom-call(s32[1,384]{1,0:T(1,128)S(1)} %copy-done.5, s32[1,384]{1,0:T(1,128)S(1)} %copy-done.6, bf16[384,384]{1,0:T(8,128)(2,1)S(1)} %copy-done.2, ...), custom_call_target="tpu_custom_call" | custom-call | tf_op jit(solution)/shard_map/pallas_call | solution.py:55
  7.7 4.6 %collective-permute-start.2 = (bf16[64,1536]{1,0:T(8,128)(2,1)S(1)}, bf16[64,1536]{1,0:T(8,128)(2,1)S(1)}, u32[]{:S(2)}, u32[]{:S(2)}) collective-permute-start(bf16[64,1536]{1,0:T(8,128)(2,1)S(1)} %get-tuple-element.34), channel_id=1, source_target_pairs={{0,28},{4,0},{8,4},{12,8},{16,12},{20,16},{24,20},{28,24},{1,29},{... | collective-permute-start | bytes 589832 | tf_op jit(solution)/shard_map/ppermute | solution.py:337
  12.3 0.0 collective-permute-start.3
  12.3 6.8 %collective-permute-done.3 = bf16[64,384]{1,0:T(8,128)(2,1)S(1)} collective-permute-done((bf16[64,384]{1,0:T(8,128)(2,1)S(1)}, bf16[64,384]{1,0:T(8,128)(2,1)S(1)}, u32[]{:S(2)}, u32[]{:S(2)}) %collective-permute-start.3) | collective-permute-done | bytes 49184 | tf_op jit(solution)/shard_map/ppermute | solution.py:337
  19.1 0.0 collective-permute-done.2.refs_2_
  19.1 0.0 collective-permute-done.1.refs_0_
  19.1 0.0 collective-permute-start.5
  19.1 1.2 %collective-permute-start.7 = (bf16[384,640]{1,0:T(8,128)(2,1)S(1)}, bf16[384,640]{1,0:T(8,128)(2,1)S(1)}, u32[]{:S(2)}, u32[]{:S(2)}) collective-permute-start(bf16[384,640]{1,0:T(8,128)(2,1)S(1)} %collective-permute-done.1.refs_0_), channel_id=1, source_target_pairs={{0,8},{4,12},{8,0},{12,4},{16,24},{20,28},{24,16},{28,20},{1,9},{5... | collective-permute-start | bytes 1474568 | tf_op jit(solution)/shard_map/ppermute | solution.py:332
  20.4 1.6 %collective-permute-start.6 = (bf16[448,384]{1,0:T(8,128)(2,1)S(1)}, bf16[448,384]{1,0:T(8,128)(2,1)S(1)}, u32[]{:S(2)}, u32[]{:S(2)}) collective-permute-start(bf16[448,384]{1,0:T(8,128)(2,1)S(1)} %constant_dynamic-update-slice_fusion.att), channel_id=1, source_target_pairs={{0,2},{1,3},{2,0},{3,1},{4,6},{5,7},{6,4},{7,5},{8,10},{9,11},{10,... | collective-permute-start | bytes 1032200 | tf_op jit(solution)/shard_map/ppermute | solution.py:332
  21.9 0.0 collective-permute-start.4
  21.9 1.4 %collective-permute-done.4.refs_3_ = bf16[64,1536]{1,0:T(8,128)(2,1)S(1)} collective-permute-done((bf16[64,1536]{1,0:T(8,128)(2,1)S(1)}, bf16[64,1536]{1,0:T(8,128)(2,1)S(1)}, u32[]{:S(2)}, u32[]{:S(2)}) %collective-permute-start.4) | collective-permute-done | bytes 196640 | tf_op jit(solution)/shard_map/ppermute | solution.py:332
  23.4 0.5 %collective-permute-start.10 = (bf16[384,512]{1,0:T(8,128)(2,1)S(1)}, bf16[384,512]{1,0:T(8,128)(2,1)S(1)}, u32[]{:S(2)}, u32[]{:S(2)}) collective-permute-start(bf16[384,512]{1,0:T(8,128)(2,1)S(1)} %get-tuple-element.46), channel_id=1, source_target_pairs={{0,2},{1,3},{2,0},{3,1},{4,6},{5,7},{6,4},{7,5},{8,10},{9,11},{10,... | collective-permute-start | bytes 1179656 | tf_op jit(solution)/shard_map/ppermute | solution.py:332
  23.9 0.0 collective-permute-done.refs_1_
  23.9 0.8 %shard_map.104 = (bf16[384,1536]{1,0:T(8,128)(2,1)S(1)}, bf16[384,1536]{1,0:T(8,128)(2,1)S(1)}) custom-call(s32[1]{0:T(128)} %get-tuple-element.33.gone_ref.gone, bf16[448,1536]{1,0:T(8,128)(2,1)S(1)} %copy-done.1, bf16[448,1536]{1,0:T(8,128)(2,1)S(1)} %collective-permute-done.refs_1_, bf16[64,1536]{1,0:T(8,128)(2,1)S(1)} %collective-permute-done.2.refs_2_, ...), custom_call_target="tpu_custom_call" | custom-call | tf_op jit(solution)/shard_map/pallas_call | solution.py:379
  24.7 0.0 copy-done
  24.7 1.4 %shard_map.105.near = f32[384,384]{1,0:T(8,128)S(1)} custom-call(s32[1]{0:T(128)} %bitcast.t.t_ref, bf16[384,1536]{1,0:T(8,128)(2,1)S(1)} %get-tuple-element.37.cot_own, bf16[384,1536]{1,0:T(8,128)(2,1)S(1)} %get-tuple-element.38.cot_sib, bf16[384,6144]{1,0:T(8,128)(2,1)S(1)} %copy-done), custom_call_target="tpu_custom_call" | custom-call | flops 905969664 | bytes 4718592 | tf_op jit(solution)/shard_map/pallas_call | solution.py:385
  26.1 5.3 %collective-permute-done.6.far_att = bf16[448,384]{1,0:T(8,128)(2,1)S(1)} collective-permute-done((bf16[448,384]{1,0:T(8,128)(2,1)S(1)}, bf16[448,384]{1,0:T(8,128)(2,1)S(1)}, u32[]{:S(2)}, u32[]{:S(2)}) %collective-permute-start.6) | collective-permute-done | bytes 344096 | tf_op jit(solution)/shard_map/ppermute | solution.py:332
  31.4 0.0 collective-permute-done.5.refs_1_
  31.5 1.0 %collective-permute-start.8 = (bf16[224,640]{1,0:T(8,128)(2,1)S(1)}, bf16[224,640]{1,0:T(8,128)(2,1)S(1)}, u32[]{:S(2)}, u32[]{:S(2)}) collective-permute-start(bf16[224,640]{1,0:T(8,128)(2,1)S(1)} %slice.6), channel_id=1, source_target_pairs={{0,8},{4,12},{8,0},{12,4},{16,24},{20,28},{24,16},{28,20},{1,9},{5... | collective-permute-start | bytes 860168 | tf_op jit(solution)/shard_map/ppermute | solution.py:332
  32.4 0.0 collective-permute-done.7.refs_2_
  32.4 2.0 %collective-permute-start.9 = (bf16[160,640]{1,0:T(8,128)(2,1)S(1)}, bf16[160,640]{1,0:T(8,128)(2,1)S(1)}, u32[]{:S(2)}, u32[]{:S(2)}) collective-permute-start(bf16[160,640]{1,0:T(8,128)(2,1)S(1)} %slice.7), channel_id=1, source_target_pairs={{0,4},{4,0},{8,12},{12,8},{16,20},{20,16},{24,28},{28,24},{1,5},{5... | collective-permute-start | bytes 614408 | tf_op jit(solution)/shard_map/ppermute | solution.py:332
  34.5 1.0 %shard_map.106.part_sum = f32[384,384]{1,0:T(8,128)S(1)} custom-call(s32[1]{0:T(128)} %bitcast.t.t_ref, s32[1]{0:T(128)} %bitcast.1.place.place_ref, bf16[384,1536]{1,0:T(8,128)(2,1)S(1)} %get-tuple-element.37.cot_own, bf16[384,1536]{1,0:T(8,128)(2,1)S(1)} %get-tuple-element.38.cot_sib, bf16[384,640]{1,0:T(8,128)(2,1)S(1)} %collective-permute-done.1.refs_0_, ...), custom_call_target="tpu_custom_call" | custom-call | flops 566231040 | bytes 2949120 | tf_op jit(solution)/shard_map/pallas_call | solution.py:400
  35.5 2.5 %collective-permute-done.10.direct = bf16[384,512]{1,0:T(8,128)(2,1)S(1)} collective-permute-done((bf16[384,512]{1,0:T(8,128)(2,1)S(1)}, bf16[384,512]{1,0:T(8,128)(2,1)S(1)}, u32[]{:S(2)}, u32[]{:S(2)}) %collective-permute-start.10) | collective-permute-done | bytes 393248 | tf_op jit(solution)/shard_map/ppermute | solution.py:332
  37.9 0.3 collective-permute-done.9.diag_b
  38.3 0.0 collective-permute-done.8.diag_a
  38.3 0.7 %shard_map.107 = bf16[384,384]{1,0:T(8,128)(2,1)S(1)} custom-call(s32[1]{0:T(128)} %bitcast.t.t_ref, s32[1]{0:T(128)} %bitcast.1.place.place_ref, bf16[384,1536]{1,0:T(8,128)(2,1)S(1)} %get-tuple-element.37.cot_own, bf16[384,1536]{1,0:T(8,128)(2,1)S(1)} %get-tuple-element.38.cot_sib, f32[384,384]{1,0:T(8,128)S(1)} %shard_map.106.part_sum, ...), custom_call_target="tpu_custom_call" | custom-call | flops 339738624 | bytes 1769472 | tf_op jit(solution)/shard_map/pallas_call | solution.py:407
  38.9 1.4 %collective-permute-start.13 = (bf16[384,384]{1,0:T(8,128)(2,1)S(1)}, bf16[384,384]{1,0:T(8,128)(2,1)S(1)}, u32[]{:S(2)}, u32[]{:S(2)}) collective-permute-start(bf16[384,384]{1,0:T(8,128)(2,1)S(1)} %shard_map.107), channel_id=1, source_target_pairs={{0,2},{1,3},{2,0},{3,1},{4,6},{5,7},{6,4},{7,5},{8,10},{9,11},{10,... | collective-permute-start | bytes 884744 | tf_op jit(solution)/shard_map/ppermute | solution.py:332
  40.4 2.5 %shard_map.108 = (bf16[448,1280]{1,0:T(8,128)(2,1)S(1)}, bf16[448,1280]{1,0:T(8,128)(2,1)S(1)}, bf16[448,768]{1,0:T(8,128)(2,1)S(1)}) custom-call(s32[1]{0:T(128)} %get-tuple-element.33.gone_ref.gone, s32[1]{0:T(128)} %bitcast.t.t_ref, s32[1]{0:T(128)} %bitcast.1.place.place_ref, bf16[448,384]{1,0:T(8,128)(2,1)S(1)} %constant_dynamic-update-slice_fusion.att, ...), custom_call_target="tpu_custom_call" | custom-call | flops 1321205760 | bytes 5701632 | tf_op jit(solution)/shard_map/pallas_call | solution.py:415
  42.9 1.1 %shard_map.109 = (bf16[448,896]{1,0:T(8,128)(2,1)S(1)}, bf16[448,896]{1,0:T(8,128)(2,1)S(1)}) custom-call(s32[1]{0:T(128)} %bitcast.t.t_ref, s32[1]{0:T(128)} %bitcast.1.place.place_ref, bf16[448,768]{1,0:T(8,128)(2,1)S(1)} %get-tuple-element.51.left, bf16[384,6144]{1,0:T(8,128)(2,1)S(1)} %copy-done, bf16[224,640]{1,0:T(8,128)(2,1)S(1)} %collective-permute-done.8.diag_a, ...), custom_call_target="tpu_custom_call" | custom-call | flops 792723456 | bytes 3145728 | tf_op jit(solution)/shard_map/pallas_call | solution.py:423
  44.0 0.1 collective-permute-start.12
  44.1 0.5 %collective-permute-start.11 = (bf16[448,1280]{1,0:T(8,128)(2,1)S(1)}, bf16[448,1280]{1,0:T(8,128)(2,1)S(1)}, u32[]{:S(2)}, u32[]{:S(2)}) collective-permute-start(bf16[448,1280]{1,0:T(8,128)(2,1)S(1)} %get-tuple-element.50), channel_id=1, source_target_pairs={{0,1},{1,0},{2,3},{3,2},{4,5},{5,4},{6,7},{7,6},{8,9},{9,8},{10,11... | collective-permute-start | bytes 3440648 | tf_op jit(solution)/shard_map/ppermute | solution.py:332
  44.6 1.2 %collective-permute-done.13.far = bf16[384,384]{1,0:T(8,128)(2,1)S(1)} collective-permute-done((bf16[384,384]{1,0:T(8,128)(2,1)S(1)}, bf16[384,384]{1,0:T(8,128)(2,1)S(1)}, u32[]{:S(2)}, u32[]{:S(2)}) %collective-permute-start.13) | collective-permute-done | bytes 294944 | tf_op jit(solution)/shard_map/ppermute | solution.py:332
  45.8 2.2 %shard_map.111 = (bf16[384,384]{1,0:T(8,128)(2,1)}, bf16[384,384]{1,0:T(8,128)(2,1)}, bf16[384,384]{1,0:T(8,128)(2,1)}) custom-call(bf16[384,384]{1,0:T(8,128)(2,1)S(1)} %copy-done.2, bf16[384,384]{1,0:T(8,128)(2,1)S(1)} %copy-done.3, bf16[384,384]{1,0:T(8,128)(2,1)S(1)} %copy-done.4, bf16[3,384,384]{2,1,0:T(8,128)(2,1)S(1)} %get-tuple-element.54.pt, ...), custom_call_target="tpu_custom_call" | custom-call | flops 45298483200 | bytes 2654208 | tf_op jit(solution)/shard_map/pallas_call | solution.py:318
  48.1 0.0 collective-permute-done.12.other_late
  48.1 0.0 collective-permute-done.11.other
  48.1 1.2 %shard_map.110 = bf16[448,1536]{1,0:T(8,128)(2,1)} custom-call(s32[1]{0:T(128)} %bitcast.t.t_ref, s32[1]{0:T(128)} %bitcast.1.place.place_ref, bf16[448,1280]{1,0:T(8,128)(2,1)S(1)} %get-tuple-element.49.own, bf16[448,1280]{1,0:T(8,128)(2,1)S(1)} %collective-permute-done.11.other, bf16[448,896]{1,0:T(8,128)(2,1)S(1)} %get-tuple-element.52.own_late, ...), custom_call_target="tpu_custom_call" | custom-call | bytes 4128768 | tf_op jit(solution)/shard_map/pallas_call | solution.py:431
  (3 shorter events, 0.1 us)
Async XLA Ops:
  0.6 23.3 %collective-permute-start = (bf16[448,1536]{1,0:T(8,128)(2,1)}, bf16[448,1536]{1,0:T(8,128)(2,1)S(1)}, u32[]{:S(2)}, u32[]{:S(2)}) collective-permute-start(bf16[448,1536]{1,0:T(8,128)(2,1)} %refs_0_.1), channel_id=1, source_target_pairs={{0,1},{1,0},{2,3},{3,2},{4,5},{5,4},{6,7},{7,6},{8,9},{9,8},{10,11... | collective-permute-start | bytes 4128776 | tf_op jit(solution)/shard_map/ppermute | solution.py:332
  1.2 4.0 %copy-start.1 = (bf16[448,1536]{1,0:T(8,128)(2,1)S(1)}, bf16[448,1536]{1,0:T(8,128)(2,1)}, u32[]{:S(2)}) copy-start(bf16[448,1536]{1,0:T(8,128)(2,1)} %refs_0_.1) | copy-start | bytes 4128772
  1.2 4.0 %copy-start.2 = (bf16[384,384]{1,0:T(8,128)(2,1)S(1)}, bf16[384,384]{1,0:T(8,128)(2,1)}, u32[]{:S(2)}) copy-start(bf16[384,384]{1,0:T(8,128)(2,1)} %q.3) | copy-start | bytes 884740
  1.2 4.0 %copy-start.3 = (bf16[384,384]{1,0:T(8,128)(2,1)S(1)}, bf16[384,384]{1,0:T(8,128)(2,1)}, u32[]{:S(2)}) copy-start(bf16[384,384]{1,0:T(8,128)(2,1)} %k.3) | copy-start | bytes 884740
  1.2 4.0 %copy-start.4 = (bf16[384,384]{1,0:T(8,128)(2,1)S(1)}, bf16[384,384]{1,0:T(8,128)(2,1)}, u32[]{:S(2)}) copy-start(bf16[384,384]{1,0:T(8,128)(2,1)} %v.3) | copy-start | bytes 884740
  1.2 4.0 %copy-start.5 = (s32[1,384]{1,0:T(1,128)S(1)}, s32[1,384]{1,0:T(1,128)}, u32[]{:S(2)}) copy-start(s32[1,384]{1,0:T(1,128)} %seg) | copy-start | bytes 4612
  1.2 4.0 %copy-start.6 = (s32[1,384]{1,0:T(1,128)S(1)}, s32[1,384]{1,0:T(1,128)}, u32[]{:S(2)}) copy-start(s32[1,384]{1,0:T(1,128)} %flags.1) | copy-start | bytes 4612
  2.5 16.6 %collective-permute-start.1 = (bf16[384,640]{1,0:T(8,128)(2,1)S(1)}, bf16[384,640]{1,0:T(8,128)(2,1)S(1)}, u32[]{:S(2)}, u32[]{:S(2)}) collective-permute-start(bf16[384,640]{1,0:T(8,128)(2,1)S(1)} %get-tuple-element.31), channel_id=1, source_target_pairs={{0,2},{1,3},{2,0},{3,1},{4,6},{5,7},{6,4},{7,5},{8,10},{9,11},{10,... | collective-permute-start | bytes 1474568 | tf_op jit(solution)/shard_map/ppermute | solution.py:332
  5.2 19.6 %copy-start = (bf16[384,6144]{1,0:T(8,128)(2,1)S(1)}, bf16[384,6144]{1,0:T(8,128)(2,1)}, u32[]{:S(2)}) copy-start(bf16[384,6144]{1,0:T(8,128)(2,1)} %weight.7) | copy-start | bytes 14155780
  7.7 11.4 %collective-permute-start.2 = (bf16[64,1536]{1,0:T(8,128)(2,1)S(1)}, bf16[64,1536]{1,0:T(8,128)(2,1)S(1)}, u32[]{:S(2)}, u32[]{:S(2)}) collective-permute-start(bf16[64,1536]{1,0:T(8,128)(2,1)S(1)} %get-tuple-element.34), channel_id=1, source_target_pairs={{0,28},{4,0},{8,4},{12,8},{16,12},{20,16},{24,20},{28,24},{1,29},{... | collective-permute-start | bytes 589832 | tf_op jit(solution)/shard_map/ppermute | solution.py:337
  12.3 6.8 %collective-permute-start.3 = (bf16[64,384]{1,0:T(8,128)(2,1)S(1)}, bf16[64,384]{1,0:T(8,128)(2,1)S(1)}, u32[]{:S(2)}, u32[]{:S(2)}) collective-permute-start(bf16[64,384]{1,0:T(8,128)(2,1)S(1)} %get-tuple-element.35), channel_id=1, source_target_pairs={{0,4},{4,8},{8,12},{12,16},{16,20},{20,24},{24,28},{28,0},{1,5},{5... | collective-permute-start | bytes 147464 | tf_op jit(solution)/shard_map/ppermute | solution.py:337
  19.1 12.3 %collective-permute-start.5 = (bf16[384,640]{1,0:T(8,128)(2,1)S(1)}, bf16[384,640]{1,0:T(8,128)(2,1)S(1)}, u32[]{:S(2)}, u32[]{:S(2)}) collective-permute-start(bf16[384,640]{1,0:T(8,128)(2,1)S(1)} %collective-permute-done.1.refs_0_), channel_id=1, source_target_pairs={{0,4},{4,0},{8,12},{12,8},{16,20},{20,16},{24,28},{28,24},{1,5},{5... | collective-permute-start | bytes 1474568 | tf_op jit(solution)/shard_map/ppermute | solution.py:332
  19.1 13.3 %collective-permute-start.7 = (bf16[384,640]{1,0:T(8,128)(2,1)S(1)}, bf16[384,640]{1,0:T(8,128)(2,1)S(1)}, u32[]{:S(2)}, u32[]{:S(2)}) collective-permute-start(bf16[384,640]{1,0:T(8,128)(2,1)S(1)} %collective-permute-done.1.refs_0_), channel_id=1, source_target_pairs={{0,8},{4,12},{8,0},{12,4},{16,24},{20,28},{24,16},{28,20},{1,9},{5... | collective-permute-start | bytes 1474568 | tf_op jit(solution)/shard_map/ppermute | solution.py:332
  20.4 11.1 %collective-permute-start.6 = (bf16[448,384]{1,0:T(8,128)(2,1)S(1)}, bf16[448,384]{1,0:T(8,128)(2,1)S(1)}, u32[]{:S(2)}, u32[]{:S(2)}) collective-permute-start(bf16[448,384]{1,0:T(8,128)(2,1)S(1)} %constant_dynamic-update-slice_fusion.att), channel_id=1, source_target_pairs={{0,2},{1,3},{2,0},{3,1},{4,6},{5,7},{6,4},{7,5},{8,10},{9,11},{10,... | collective-permute-start | bytes 1032200 | tf_op jit(solution)/shard_map/ppermute | solution.py:332
  21.9 1.4 %collective-permute-start.4 = (bf16[64,1536]{1,0:T(8,128)(2,1)S(1)}, bf16[64,1536]{1,0:T(8,128)(2,1)S(1)}, u32[]{:S(2)}, u32[]{:S(2)}) collective-permute-start(bf16[64,1536]{1,0:T(8,128)(2,1)S(1)} %collective-permute-done.2.refs_2_), channel_id=1, source_target_pairs={{0,1},{1,0},{2,3},{3,2},{4,5},{5,4},{6,7},{7,6},{8,9},{9,8},{10,11... | collective-permute-start | bytes 589832 | tf_op jit(solution)/shard_map/ppermute | solution.py:332
  23.4 14.6 %collective-permute-start.10 = (bf16[384,512]{1,0:T(8,128)(2,1)S(1)}, bf16[384,512]{1,0:T(8,128)(2,1)S(1)}, u32[]{:S(2)}, u32[]{:S(2)}) collective-permute-start(bf16[384,512]{1,0:T(8,128)(2,1)S(1)} %get-tuple-element.46), channel_id=1, source_target_pairs={{0,2},{1,3},{2,0},{3,1},{4,6},{5,7},{6,4},{7,5},{8,10},{9,11},{10,... | collective-permute-start | bytes 1179656 | tf_op jit(solution)/shard_map/ppermute | solution.py:332
  31.5 6.8 %collective-permute-start.8 = (bf16[224,640]{1,0:T(8,128)(2,1)S(1)}, bf16[224,640]{1,0:T(8,128)(2,1)S(1)}, u32[]{:S(2)}, u32[]{:S(2)}) collective-permute-start(bf16[224,640]{1,0:T(8,128)(2,1)S(1)} %slice.6), channel_id=1, source_target_pairs={{0,8},{4,12},{8,0},{12,4},{16,24},{20,28},{24,16},{28,20},{1,9},{5... | collective-permute-start | bytes 860168 | tf_op jit(solution)/shard_map/ppermute | solution.py:332
  32.4 5.8 %collective-permute-start.9 = (bf16[160,640]{1,0:T(8,128)(2,1)S(1)}, bf16[160,640]{1,0:T(8,128)(2,1)S(1)}, u32[]{:S(2)}, u32[]{:S(2)}) collective-permute-start(bf16[160,640]{1,0:T(8,128)(2,1)S(1)} %slice.7), channel_id=1, source_target_pairs={{0,4},{4,0},{8,12},{12,8},{16,20},{20,16},{24,28},{28,24},{1,5},{5... | collective-permute-start | bytes 614408 | tf_op jit(solution)/shard_map/ppermute | solution.py:332
  38.9 6.9 %collective-permute-start.13 = (bf16[384,384]{1,0:T(8,128)(2,1)S(1)}, bf16[384,384]{1,0:T(8,128)(2,1)S(1)}, u32[]{:S(2)}, u32[]{:S(2)}) collective-permute-start(bf16[384,384]{1,0:T(8,128)(2,1)S(1)} %shard_map.107), channel_id=1, source_target_pairs={{0,2},{1,3},{2,0},{3,1},{4,6},{5,7},{6,4},{7,5},{8,10},{9,11},{10,... | collective-permute-start | bytes 884744 | tf_op jit(solution)/shard_map/ppermute | solution.py:332
  44.0 4.1 %collective-permute-start.12 = (bf16[448,896]{1,0:T(8,128)(2,1)S(1)}, bf16[448,896]{1,0:T(8,128)(2,1)S(1)}, u32[]{:S(2)}, u32[]{:S(2)}) collective-permute-start(bf16[448,896]{1,0:T(8,128)(2,1)S(1)} %get-tuple-element.53), channel_id=1, source_target_pairs={{0,1},{1,0},{2,3},{3,2},{4,5},{5,4},{6,7},{7,6},{8,9},{9,8},{10,11... | collective-permute-start | bytes 2408456 | tf_op jit(solution)/shard_map/ppermute | solution.py:332
  44.1 4.0 %collective-permute-start.11 = (bf16[448,1280]{1,0:T(8,128)(2,1)S(1)}, bf16[448,1280]{1,0:T(8,128)(2,1)S(1)}, u32[]{:S(2)}, u32[]{:S(2)}) collective-permute-start(bf16[448,1280]{1,0:T(8,128)(2,1)S(1)} %get-tuple-element.50), channel_id=1, source_target_pairs={{0,1},{1,0},{2,3},{3,2},{4,5},{5,4},{6,7},{7,6},{8,9},{9,8},{10,11... | collective-permute-start | bytes 3440648 | tf_op jit(solution)/shard_map/ppermute | solution.py:332
